TPU v7x, 32 devices: a whole 2x2x4 slice. The times are simulated.
32 devices in a mesh: wide: 8 (over z, x), narrow: 4 (over y, core).
Axes of the slice: x: 2, y: 2, z: 4, core: 2. Of those that a mesh axis runs over, the one named last changes fastest.
Arguments:
- tokens: bfloat16 [2, 32, 384, 768], P(None, ('wide', 'narrow')), may hold values from -6 to 6
- lengths: int32 [2, 32], P(None, ('wide', 'narrow')), may hold values from 96 to 384, as said below
- w_inward: bfloat16 [2, 1769472], P(None, ('wide', 'narrow')), may hold values from -0.21875 to 0.21875
- query_bias: bfloat16 [2, 768], P(None, ('wide', 'narrow')), may hold values from -1 to 1
- value_bias: bfloat16 [2, 768], P(None, ('wide', 'narrow')), may hold values from -1 to 1
- w_outward: bfloat16 [2, 589824], P(None, ('wide', 'narrow')), may hold values from -0.625 to 0.625
- outward_bias: bfloat16 [2, 768], P(None, ('wide', 'narrow')), may hold values from -1 to 1
- attn_gain: bfloat16 [2, 768], P(None, ('wide', 'narrow')), may hold values from 0.25 to 1.75
- attn_shift: bfloat16 [2, 768], P(None, ('wide', 'narrow')), may hold values from -1 to 1
- w_expand: bfloat16 [2, 2359296], P(None, ('wide', 'narrow')), may hold values from -0.21875 to 0.21875
- expand_bias: bfloat16 [2, 3072], P(None, ('wide', 'narrow')), may hold values from -1 to 1
- w_contract: bfloat16 [2, 2359296], P(None, ('wide', 'narrow')), may hold values from -0.15625 to 0.15625
- contract_bias: bfloat16 [2, 768], P(None, ('wide', 'narrow')), may hold values from -1 to 1
- ffn_gain: bfloat16 [2, 768], P(None, ('wide', 'narrow')), may hold values from 0.25 to 1.75
- ffn_shift: bfloat16 [2, 768], P(None, ('wide', 'narrow')), may hold values from -1 to 1
- cotangent: bfloat16 [2, 32, 384, 768], P(None, ('wide', 'narrow')), may hold values from -6 to 6
Outputs:
- layer_output: float32 [2, 32, 384, 768], P(None, ('wide', 'narrow'))
- grad_tokens: float32 [2, 32, 384, 768], P(None, ('wide', 'narrow'))
- grad_w_inward: float32 [2, 1769472], P(None, ('wide', 'narrow'))
- grad_query_bias: float32 [2, 768], P(None, ('wide', 'narrow'))
- grad_value_bias: float32 [2, 768], P(None, ('wide', 'narrow'))
- grad_w_outward: float32 [2, 589824], P(None, ('wide', 'narrow'))
- grad_outward_bias: float32 [2, 768], P(None, ('wide', 'narrow'))
- grad_attn_gain: float32 [2, 768], P(None, ('wide', 'narrow'))
- grad_attn_shift: float32 [2, 768], P(None, ('wide', 'narrow'))
- grad_w_expand: float32 [2, 2359296], P(None, ('wide', 'narrow'))
- grad_expand_bias: float32 [2, 3072], P(None, ('wide', 'narrow'))
- grad_w_contract: float32 [2, 2359296], P(None, ('wide', 'narrow'))
- grad_contract_bias: float32 [2, 768], P(None, ('wide', 'narrow'))
- grad_ffn_gain: float32 [2, 768], P(None, ('wide', 'narrow'))
- grad_ffn_shift: float32 [2, 768], P(None, ('wide', 'narrow'))
Inputs may be any that keep to these rules, and one draw needn't show every extreme that they name: `lengths`: each micro-batch holds one sequence of exactly 384 real tokens and one of exactly 96; the rest of a row is padding.
All inputs are finite; a program needn't handle non-finite values.
Results may differ from a plain program's by a relative error of at most 0.019.
Values may be sent and summed in bfloat16 or wider, within the bound.
No kernel may reach another device: no remote copies, remote signals or barrier semaphores. Data moves between devices by JAX's collectives and lax.ppermute only.
A program may use at most 256 MiB of HBM per device.

v0:
```python
from functools import partial

import jax
import jax.numpy as jnp
from jax import lax
from jax.sharding import PartitionSpec as P

HEAD_DIM = 64


epsilon = 1e-06


def norm_forward(inputs, gain_vector, shift_vector):
    centred = inputs - jnp.mean(inputs, axis=-1, keepdims=True)
    inv_std = lax.rsqrt(jnp.mean(centred * centred, axis=-1, keepdims=True) + epsilon)
    normed = centred * inv_std
    return (
        normed * gain_vector.astype(jnp.float32) + shift_vector.astype(jnp.float32),
        normed,
        inv_std,
    )


def norm_backward(upstream, normed, inv_std, gain_vector):
    scaled = upstream * gain_vector.astype(jnp.float32)
    grad_gain = jnp.sum(upstream * normed, axis=(0, 1))
    grad_shift = jnp.sum(upstream, axis=(0, 1))
    inner = (
        scaled
        - jnp.mean(scaled, axis=-1, keepdims=True)
        - normed * jnp.mean(scaled * normed, axis=-1, keepdims=True)
    )
    return (inner * inv_std, grad_gain, grad_shift)


def split_heads(matrix):
    return matrix.reshape(matrix.shape[0], matrix.shape[1], -1, HEAD_DIM)


def shape_weights(gathered):
    (
        w_inward,
        query_bias,
        value_bias,
        w_outward,
        outward_bias,
        attn_gain,
        attn_shift,
        w_expand,
        expand_bias,
        w_contract,
        contract_bias,
        ffn_gain,
        ffn_shift,
    ) = gathered
    model_width = query_bias.shape[0]
    hidden_width = expand_bias.shape[0]
    return (
        w_inward.reshape(model_width, 3 * model_width),
        query_bias,
        value_bias,
        w_outward.reshape(model_width, model_width),
        outward_bias,
        attn_gain,
        attn_shift,
        w_expand.reshape(model_width, hidden_width),
        expand_bias,
        w_contract.reshape(hidden_width, model_width),
        contract_bias,
        ffn_gain,
        ffn_shift,
    )


def attention_scores(queries, keys_all, valid_keys):
    scores = jnp.einsum(
        "nqhe,nkhe->nhqk", queries, keys_all, preferred_element_type=jnp.float32
    ) * HEAD_DIM ** (-0.5)
    return jnp.where(valid_keys[:, None, None, :], scores, -1e30)


def forward_layer(stream, gathered, valid_keys):
    (
        w_inward,
        query_bias,
        value_bias,
        w_outward,
        outward_bias,
        attn_gain,
        attn_shift,
        w_expand,
        expand_bias,
        w_contract,
        contract_bias,
        ffn_gain,
        ffn_shift,
    ) = gathered
    model_width = stream.shape[2]
    entry = stream.astype(jnp.bfloat16)
    joined = jnp.einsum("nsd,de->nse", entry, w_inward, preferred_element_type=jnp.float32)
    queries = split_heads(
        (joined[..., :model_width] + query_bias.astype(jnp.float32)).astype(jnp.bfloat16)
    )
    keys_all = split_heads(joined[..., model_width : 2 * model_width].astype(jnp.bfloat16))
    values_all = split_heads(
        (joined[..., 2 * model_width :] + value_bias.astype(jnp.float32)).astype(jnp.bfloat16)
    )
    scores = attention_scores(queries, keys_all, valid_keys)
    highest_score = jnp.max(scores, axis=-1, keepdims=True)
    raised = jnp.exp(scores - highest_score)
    row_total = jnp.sum(raised, axis=-1, keepdims=True)
    soft_low = (raised / row_total).astype(jnp.bfloat16)
    log_total = highest_score + jnp.log(row_total)
    attended = jnp.einsum(
        "nhqk,nkhe->nqhe", soft_low, values_all, preferred_element_type=jnp.float32
    )
    attended = attended.reshape(stream.shape).astype(jnp.bfloat16)
    branch = jnp.einsum(
        "nsd,de->nse", attended, w_outward, preferred_element_type=jnp.float32
    ) + outward_bias.astype(jnp.float32)
    first_out, normed_one, inv_one = norm_forward(stream + branch, attn_gain, attn_shift)
    first_low = first_out.astype(jnp.bfloat16)
    hidden_pre = jnp.einsum(
        "nsd,df->nsf", first_low, w_expand, preferred_element_type=jnp.float32
    ) + expand_bias.astype(jnp.float32)
    hidden = jax.nn.gelu(hidden_pre, approximate=False).astype(jnp.bfloat16)
    branch_two = jnp.einsum(
        "nsf,fd->nsd", hidden, w_contract, preferred_element_type=jnp.float32
    ) + contract_bias.astype(jnp.float32)
    output, normed_two, inv_two = norm_forward(first_out + branch_two, ffn_gain, ffn_shift)
    kept_values = (
        entry,
        queries,
        keys_all,
        values_all,
        log_total,
        attended,
        normed_one,
        inv_one,
        first_low,
        hidden_pre,
        hidden,
        normed_two,
        inv_two,
    )
    return (output, kept_values)


def backward_layer(upstream, gathered, kept_values, valid_keys):
    (
        w_inward,
        query_bias,
        value_bias,
        w_outward,
        outward_bias,
        attn_gain,
        attn_shift,
        w_expand,
        expand_bias,
        w_contract,
        contract_bias,
        ffn_gain,
        ffn_shift,
    ) = gathered
    (
        entry,
        queries,
        keys_all,
        values_all,
        log_total,
        attended,
        normed_one,
        inv_one,
        first_low,
        hidden_pre,
        hidden,
        normed_two,
        inv_two,
    ) = kept_values
    grad_second, grad_ffn_gain, grad_ffn_shift = norm_backward(
        upstream, normed_two, inv_two, ffn_gain
    )
    grad_branch_two = grad_second.astype(jnp.bfloat16)
    grad_contract_bias = jnp.sum(grad_branch_two.astype(jnp.float32), axis=(0, 1))
    grad_w_contract = jnp.einsum(
        "nsf,nsd->fd", hidden, grad_branch_two, preferred_element_type=jnp.float32
    )
    grad_hidden = jnp.einsum(
        "nsd,fd->nsf", grad_branch_two, w_contract, preferred_element_type=jnp.float32
    )
    gelu_pull = jax.vjp(partial(jax.nn.gelu, approximate=False), hidden_pre)[1]
    grad_pre = gelu_pull(grad_hidden)[0].astype(jnp.bfloat16)
    grad_expand_bias = jnp.sum(grad_pre.astype(jnp.float32), axis=(0, 1))
    grad_w_expand = jnp.einsum(
        "nsd,nsf->df", first_low, grad_pre, preferred_element_type=jnp.float32
    )
    grad_first = grad_second + jnp.einsum(
        "nsf,df->nsd", grad_pre, w_expand, preferred_element_type=jnp.float32
    )
    grad_first_in, grad_attn_gain, grad_attn_shift = norm_backward(
        grad_first, normed_one, inv_one, attn_gain
    )
    grad_branch = grad_first_in.astype(jnp.bfloat16)
    grad_outward_bias = jnp.sum(grad_branch.astype(jnp.float32), axis=(0, 1))
    grad_w_outward = jnp.einsum(
        "nsd,nse->de", attended, grad_branch, preferred_element_type=jnp.float32
    )
    grad_attended = split_heads(
        jnp.einsum(
            "nse,de->nsd", grad_branch, w_outward, preferred_element_type=jnp.float32
        ).astype(jnp.bfloat16)
    )
    scores = attention_scores(queries, keys_all, valid_keys)
    soft_weights = jnp.exp(scores - log_total)
    grad_soft = jnp.einsum(
        "nqhe,nkhe->nhqk", grad_attended, values_all, preferred_element_type=jnp.float32
    )
    grad_values = jnp.einsum(
        "nhqk,nqhe->nkhe",
        soft_weights.astype(jnp.bfloat16),
        grad_attended,
        preferred_element_type=jnp.float32,
    )
    inner_sum = jnp.sum(soft_weights * grad_soft, axis=-1, keepdims=True)
    grad_scores = (soft_weights * (grad_soft - inner_sum)).astype(jnp.bfloat16)
    factor = HEAD_DIM ** (-0.5)
    grad_queries = (
        jnp.einsum("nhqk,nkhe->nqhe", grad_scores, keys_all, preferred_element_type=jnp.float32)
        * factor
    )
    grad_keys = (
        jnp.einsum("nhqk,nqhe->nkhe", grad_scores, queries, preferred_element_type=jnp.float32)
        * factor
    )
    query_low = grad_queries.reshape(entry.shape).astype(jnp.bfloat16)
    key_low = grad_keys.reshape(entry.shape).astype(jnp.bfloat16)
    value_low = grad_values.reshape(entry.shape).astype(jnp.bfloat16)
    grad_query_bias = jnp.sum(query_low.astype(jnp.float32), axis=(0, 1))
    grad_value_bias = jnp.sum(value_low.astype(jnp.float32), axis=(0, 1))
    grad_joined = jnp.concatenate([query_low, key_low, value_low], axis=-1)
    grad_w_inward = jnp.einsum(
        "nsd,nse->de", entry, grad_joined, preferred_element_type=jnp.float32
    )
    grad_stream = grad_first_in + jnp.einsum(
        "nse,de->nsd", grad_joined, w_inward, preferred_element_type=jnp.float32
    )
    return (
        grad_stream,
        (
            grad_w_inward.reshape(-1),
            grad_query_bias,
            grad_value_bias,
            grad_w_outward.reshape(-1),
            grad_outward_bias,
            grad_attn_gain,
            grad_attn_shift,
            grad_w_expand.reshape(-1),
            grad_expand_bias,
            grad_w_contract.reshape(-1),
            grad_contract_bias,
            grad_ffn_gain,
            grad_ffn_shift,
        ),
    )


def local(
    tokens,
    lengths,
    w_inward,
    query_bias,
    value_bias,
    w_outward,
    outward_bias,
    attn_gain,
    attn_shift,
    w_expand,
    expand_bias,
    w_contract,
    contract_bias,
    ffn_gain,
    ffn_shift,
    cotangent,
):
    stacked = (
        w_inward,
        query_bias,
        value_bias,
        w_outward,
        outward_bias,
        attn_gain,
        attn_shift,
        w_expand,
        expand_bias,
        w_contract,
        contract_bias,
        ffn_gain,
        ffn_shift,
    )
    layer_total = w_inward.shape[0]
    micro_total = tokens.shape[0]
    places = lax.broadcasted_iota(jnp.int32, (tokens.shape[1], tokens.shape[2]), 1)

    def layer_shards(layer_index):
        return tuple((member[layer_index] for member in stacked))

    totals = [None] * layer_total
    outputs = []
    input_grads = []
    for batch_index in range(micro_total):
        valid_keys = places < lengths[batch_index][:, None]
        stream = tokens[batch_index].astype(jnp.float32)
        saved_layers = []
        for layer_index in range(layer_total):
            shard_set = layer_shards(layer_index)
            gathered = shape_weights(
                (
                    lax.all_gather(shard_set[0], ("wide", "narrow"), axis=0, tiled=True),
                    lax.all_gather(shard_set[1], ("wide", "narrow"), axis=0, tiled=True),
                    lax.all_gather(shard_set[2], ("wide", "narrow"), axis=0, tiled=True),
                    lax.all_gather(shard_set[3], ("wide", "narrow"), axis=0, tiled=True),
                    lax.all_gather(shard_set[4], ("wide", "narrow"), axis=0, tiled=True),
                    lax.all_gather(shard_set[5], ("wide", "narrow"), axis=0, tiled=True),
                    lax.all_gather(shard_set[6], ("wide", "narrow"), axis=0, tiled=True),
                    lax.all_gather(shard_set[7], ("wide", "narrow"), axis=0, tiled=True),
                    lax.all_gather(shard_set[8], ("wide", "narrow"), axis=0, tiled=True),
                    lax.all_gather(shard_set[9], ("wide", "narrow"), axis=0, tiled=True),
                    lax.all_gather(shard_set[10], ("wide", "narrow"), axis=0, tiled=True),
                    lax.all_gather(shard_set[11], ("wide", "narrow"), axis=0, tiled=True),
                    lax.all_gather(shard_set[12], ("wide", "narrow"), axis=0, tiled=True),
                )
            )
            stream, kept_values = forward_layer(stream, gathered, valid_keys)
            saved_layers.append(kept_values)
        outputs.append(stream)
        upstream = cotangent[batch_index].astype(jnp.float32)
        for layer_index in reversed(range(layer_total)):
            shard_set = layer_shards(layer_index)
            gathered = shape_weights(
                (
                    lax.all_gather(shard_set[0], ("wide", "narrow"), axis=0, tiled=True),
                    lax.all_gather(shard_set[1], ("wide", "narrow"), axis=0, tiled=True),
                    lax.all_gather(shard_set[2], ("wide", "narrow"), axis=0, tiled=True),
                    lax.all_gather(shard_set[3], ("wide", "narrow"), axis=0, tiled=True),
                    lax.all_gather(shard_set[4], ("wide", "narrow"), axis=0, tiled=True),
                    lax.all_gather(shard_set[5], ("wide", "narrow"), axis=0, tiled=True),
                    lax.all_gather(shard_set[6], ("wide", "narrow"), axis=0, tiled=True),
                    lax.all_gather(shard_set[7], ("wide", "narrow"), axis=0, tiled=True),
                    lax.all_gather(shard_set[8], ("wide", "narrow"), axis=0, tiled=True),
                    lax.all_gather(shard_set[9], ("wide", "narrow"), axis=0, tiled=True),
                    lax.all_gather(shard_set[10], ("wide", "narrow"), axis=0, tiled=True),
                    lax.all_gather(shard_set[11], ("wide", "narrow"), axis=0, tiled=True),
                    lax.all_gather(shard_set[12], ("wide", "narrow"), axis=0, tiled=True),
                )
            )
            upstream, grad_terms = backward_layer(
                upstream, gathered, saved_layers[layer_index], valid_keys
            )
            shares = (
                lax.psum_scatter(
                    grad_terms[0], ("wide", "narrow"), scatter_dimension=0, tiled=True
                ),
                lax.psum_scatter(
                    grad_terms[1], ("wide", "narrow"), scatter_dimension=0, tiled=True
                ),
                lax.psum_scatter(
                    grad_terms[2], ("wide", "narrow"), scatter_dimension=0, tiled=True
                ),
                lax.psum_scatter(
                    grad_terms[3], ("wide", "narrow"), scatter_dimension=0, tiled=True
                ),
                lax.psum_scatter(
                    grad_terms[4], ("wide", "narrow"), scatter_dimension=0, tiled=True
                ),
                lax.psum_scatter(
                    grad_terms[5], ("wide", "narrow"), scatter_dimension=0, tiled=True
                ),
                lax.psum_scatter(
                    grad_terms[6], ("wide", "narrow"), scatter_dimension=0, tiled=True
                ),
                lax.psum_scatter(
                    grad_terms[7], ("wide", "narrow"), scatter_dimension=0, tiled=True
                ),
                lax.psum_scatter(
                    grad_terms[8], ("wide", "narrow"), scatter_dimension=0, tiled=True
                ),
                lax.psum_scatter(
                    grad_terms[9], ("wide", "narrow"), scatter_dimension=0, tiled=True
                ),
                lax.psum_scatter(
                    grad_terms[10], ("wide", "narrow"), scatter_dimension=0, tiled=True
                ),
                lax.psum_scatter(
                    grad_terms[11], ("wide", "narrow"), scatter_dimension=0, tiled=True
                ),
                lax.psum_scatter(
                    grad_terms[12], ("wide", "narrow"), scatter_dimension=0, tiled=True
                ),
            )
            if totals[layer_index] is None:
                totals[layer_index] = tuple(shares)
            else:
                totals[layer_index] = tuple(
                    (previous + current for previous, current in zip(totals[layer_index], shares))
                )
        input_grads.append(upstream)
    stacked_grads = tuple(
        (
            jnp.stack([totals[layer_index][position] for layer_index in range(layer_total)])
            for position in range(len(stacked))
        )
    )
    return (jnp.stack(outputs), jnp.stack(input_grads)) + stacked_grads


def solution(mesh):
    return jax.shard_map(
        local,
        mesh=mesh,
        in_specs=(
            P(None, ("wide", "narrow"), None, None),
            P(None, ("wide", "narrow")),
            P(None, ("wide", "narrow")),
            P(None, ("wide", "narrow")),
            P(None, ("wide", "narrow")),
            P(None, ("wide", "narrow")),
            P(None, ("wide", "narrow")),
            P(None, ("wide", "narrow")),
            P(None, ("wide", "narrow")),
            P(None, ("wide", "narrow")),
            P(None, ("wide", "narrow")),
            P(None, ("wide", "narrow")),
            P(None, ("wide", "narrow")),
            P(None, ("wide", "narrow")),
            P(None, ("wide", "narrow")),
            P(None, ("wide", "narrow"), None, None),
        ),
        out_specs=(
            P(None, ("wide", "narrow"), None, None),
            P(None, ("wide", "narrow"), None, None),
            P(None, ("wide", "narrow")),
            P(None, ("wide", "narrow")),
            P(None, ("wide", "narrow")),
            P(None, ("wide", "narrow")),
            P(None, ("wide", "narrow")),
            P(None, ("wide", "narrow")),
            P(None, ("wide", "narrow")),
            P(None, ("wide", "narrow")),
            P(None, ("wide", "narrow")),
            P(None, ("wide", "narrow")),
            P(None, ("wide", "narrow")),
            P(None, ("wide", "narrow")),
            P(None, ("wide", "narrow")),
        ),
        check_vma=False,
    )
```

profile of v0, /device:TPU:0, one launch (start us, length us, event | category | flops | bytes accessed | tf_op | source)
XLA Modules:
  0.0 2189.1 jit_solution(13862281661348175670)
XLA Ops:
  22.1 43.1 %all-reduce.46 = (bf16[3072]{0:T(1024)(128)(2,1)S(1)}, bf16[3072]{0:T(1024)(128)(2,1)S(1)}, bf16[768]{0:T(1024)(128)(2,1)S(1)}, bf16[768]{0:T(1024)(128)(2,1)S(1...) all-reduce(bf16[3072]{0:T(1024)(128)(2,1)S(1)} %dynamic-update-slic, ...), channel_id=23, replica_groups=mesh['wide'=8,'narrow'=4] {'wide','narrow'}, use_global_device_ids=true, to_apply=%add.14 | all-reduce | flops 18432 | bytes 73728
  77.5 25.5 %reduce.169 = bf16[589824]{0:T(1024)(128)(2,1)S(1)} reduce(bf16[1,589824]{1,0:T(2,128)(2,1)} %all-gather.45.cloned.1.call-done, bf16[]{:T(256)} %constant.267), dimensions={0}, to_apply=%all-gather.16.reduce_sub_computation | reduce | bytes 2359298 | tf_op jit(solution)/shard_map/all_gather | solution.py:322
  104.9 26.2 %all-gather.37.cloned.1.call-done = bf16[1,589824]{1,0:T(2,128)(2,1)} async-done(((bf16[1,18432]{1,0:T(2,128)(2,1)}), bf16[1,589824]{1,0:T(2,128)(2,1)}) %all-gather.37.cloned.1.call-update) | async-done | bytes 1179664 | tf_op jit(solution)/shard_map/all_gather | solution.py:322
  131.1 25.5 %reduce.165 = bf16[589824]{0:T(1024)(128)(2,1)S(1)} reduce(bf16[1,589824]{1,0:T(2,128)(2,1)} %all-gather.37.cloned.1.call-done, bf16[]{:T(256)} %constant.267), dimensions={0}, to_apply=%all-gather.3.reduce_sub_computation | reduce | bytes 2359298 | tf_op jit(solution)/shard_map/all_gather | solution.py:322
  159.0 47.2 %all-gather.35.cloned.1.call-done = bf16[1,1769472]{1,0:T(2,128)(2,1)} async-done(((bf16[1,55296]{1,0:T(2,128)(2,1)}), bf16[1,1769472]{1,0:T(2,128)(2,1)}) %all-gather.35.cloned.1.call-update) | async-done | bytes 3538960 | tf_op jit(solution)/shard_map/all_gather | solution.py:319
  206.2 74.6 %reduce.164 = bf16[1769472]{0:T(1024)(128)(2,1)S(1)} reduce(bf16[1,1769472]{1,0:T(2,128)(2,1)} %all-gather.35.cloned.1.call-done, bf16[]{:T(256)} %constant.267), dimensions={0}, to_apply=%all-gather.reduce_sub_computation | reduce | bytes 7077890 | tf_op jit(solution)/shard_map/all_gather | solution.py:319
  286.0 74.6 %reduce.168 = bf16[1769472]{0:T(1024)(128)(2,1)S(1)} reduce(bf16[1,1769472]{1,0:T(2,128)(2,1)} %all-gather.43.cloned.1.call-done, bf16[]{:T(256)} %constant.267), dimensions={0}, to_apply=%all-gather.13.reduce_sub_computation | reduce | bytes 7077890 | tf_op jit(solution)/shard_map/all_gather | solution.py:319
  401.4 101.1 %reduce.166 = bf16[2359296]{0:T(1024)(128)(2,1)} reduce(bf16[1,2359296]{1,0:T(2,128)(2,1)} %all-gather.39.cloned.1.call-done, bf16[]{:T(256)} %constant.267), dimensions={0}, to_apply=%all-gather.7.reduce_sub_computation | reduce | bytes 9437186 | tf_op jit(solution)/shard_map/all_gather | solution.py:326
  510.6 101.5 %reduce.170 = bf16[2359296]{0:T(1024)(128)(2,1)} reduce(bf16[1,2359296]{1,0:T(2,128)(2,1)} %all-gather.47.cloned.1.call-done, bf16[]{:T(256)} %constant.267), dimensions={0}, to_apply=%all-gather.20.reduce_sub_computation | reduce | bytes 9437186 | tf_op jit(solution)/shard_map/all_gather | solution.py:326
  620.5 101.0 %reduce.171 = bf16[2359296]{0:T(1024)(128)(2,1)} reduce(bf16[1,2359296]{1,0:T(2,128)(2,1)} %all-gather.49.cloned.1.call-done, bf16[]{:T(256)} %constant.267), dimensions={0}, to_apply=%all-gather.22.reduce_sub_computation | reduce | bytes 9437186 | tf_op jit(solution)/shard_map/all_gather | solution.py:328
  721.5 9.4 reshape.1873
  730.9 101.1 %reduce.167 = bf16[2359296]{0:T(1024)(128)(2,1)} reduce(bf16[1,2359296]{1,0:T(2,128)(2,1)} %all-gather.41.cloned.1.call-done, bf16[]{:T(256)} %constant.267), dimensions={0}, to_apply=%all-gather.9.reduce_sub_computation | reduce | bytes 9437186 | tf_op jit(solution)/shard_map/all_gather | solution.py:328
  832.0 9.3 reshape.1866
  841.3 15.6 multiply_convert_fusion.5
  864.8 15.7 multiply_convert_fusion.7
  918.9 14.7 multiply_convert_fusion.4
  936.1 15.0 multiply_convert_fusion.6
  1139.5 9.2 add_bitcast_fusion
  1204.3 9.6 copy.162
  1213.9 10.9 reshape.1969
  1234.5 9.6 copy.161
  1244.0 10.7 reshape.1968
  1280.9 67.3 %all-reduce.50.cloned.1.call-done = (f32[768]{0:T(1024)}, f32[768]{0:T(1024)}, f32[768]{0:T(1024)}, f32[768]{0:T(1024)}, f32[768]{0:T(1024)}, /*index=5*/f32[768...) async-done(((f32[768]{0:T(1024)}, f32[768]{0:T(1024)}, ...) | async-done | bytes 73744
  1366.8 803.0 %all-reduce.52.cloned.1.call-done = (f32[1769472]{0:T(1024)}, f32[1769472]{0:T(1024)}, f32[589824]{0:T(1024)}, f32[589824]{0:T(1024)}, f32[2359296]{0:T(1024)}, ...) async-done(((f32[1769472]{0:T(1024)}, f32[1769472]{0:T(1024)}, f32[589824]{0:T(1024)}, f32[589824]{0:T(1024)}, f32[2359296]{0:T(1024)}, ...) | async-done | bytes 56623120
  (807 shorter events, 450.2 us)
Async XLA Ops:
  7.3 65.6 %copy-start.4 = (bf16[2,1,384,768]{3,2,1,0:T(8,128)(2,1)S(1)}, bf16[2,1,384,768]{3,2,1,0:T(8,128)(2,1)}, u32[]{:S(2)}) copy-start(bf16[2,1,384,768]{3,2,1,0:T(8,128)(2,1)} %param.31) | copy-start | bytes 3538948
  7.3 66.4 %copy-start.220 = (s32[2,1]{0,1:T(1,128)S(1)}, s32[2,1]{0,1:T(1,128)}, u32[]{:S(2)}) copy-start(s32[2,1]{0,1:T(1,128)} %param.17) | copy-start | bytes 28
  7.3 70.2 %all-gather.45.cloned.1.call-start = ((), (), s32[]{:S(2)}) async-start(), calls=%async_computation.5 | async-start | bytes 2433024 | tf_op jit(solution)/shard_map/all_gather | solution.py:322
  9.2 121.9 %all-gather.37.cloned.1.call-start = ((), (), s32[]{:S(2)}) async-start(), calls=%async_computation.1 | async-start | bytes 2433024 | tf_op jit(solution)/shard_map/all_gather | solution.py:322
  10.0 196.2 %all-gather.35.cloned.1.call-start = ((), (), s32[]{:S(2)}) async-start(), calls=%async_computation | async-start | bytes 7299072 | tf_op jit(solution)/shard_map/all_gather | solution.py:319
  12.2 273.7 %all-gather.43.cloned.1.call-start = ((), (), s32[]{:S(2)}) async-start(), calls=%async_computation.4 | async-start | bytes 7299072 | tf_op jit(solution)/shard_map/all_gather | solution.py:319
  12.8 388.5 %all-gather.39.cloned.1.call-start = ((), (), s32[]{:S(2)}) async-start(), calls=%async_computation.2 | async-start | bytes 9732096 | tf_op jit(solution)/shard_map/all_gather | solution.py:326
  15.3 495.4 %all-gather.47.cloned.1.call-start = ((), (), s32[]{:S(2)}) async-start(), calls=%async_computation.6 | async-start | bytes 9732096 | tf_op jit(solution)/shard_map/all_gather | solution.py:326
  15.9 604.6 %all-gather.49.cloned.1.call-start = ((), (), s32[]{:S(2)}) async-start(), calls=%async_computation.7 | async-start | bytes 9732096 | tf_op jit(solution)/shard_map/all_gather | solution.py:328
  17.2 713.8 %all-gather.41.cloned.1.call-start = ((), (), s32[]{:S(2)}) async-start(), calls=%async_computation.3 | async-start | bytes 9732096 | tf_op jit(solution)/shard_map/all_gather | solution.py:328
  17.9 1330.2 %all-reduce.50.cloned.1.call-start = ((), (), s32[]{:S(2)}) async-start(), calls=%async_computation.8 | async-start | bytes 180224
  65.2 815.4 %copy-start.112 = (f32[768]{0:T(1024)}, f32[768]{0:T(1024)S(1)}, u32[]{:S(2)}) copy-start(f32[768]{0:T(1024)S(1)} %convert_element_type.949) | copy-start | bytes 9220
  66.4 814.2 %copy-start.115 = (f32[768]{0:T(1024)}, f32[768]{0:T(1024)S(1)}, u32[]{:S(2)}) copy-start(f32[768]{0:T(1024)S(1)} %convert_element_type.950) | copy-start | bytes 9220
  391.8 488.8 %copy-start.53 = (f32[384,768]{1,0:T(8,128)}, f32[384,768]{1,0:T(8,128)S(1)}, u32[]{:S(2)}) copy-start(f32[384,768]{1,0:T(8,128)S(1)} %get-tuple-element.184) | copy-start | bytes 3538948
  391.8 488.8 %copy-start.129 = (f32[384]{0:T(512)}, f32[384]{0:T(512)S(1)}, u32[]{:S(2)}) copy-start(f32[384]{0:T(512)S(1)} %broadcast_multiply_fusion.23) | copy-start | bytes 4612
  399.1 457.8 %copy-start.6 = (f32[384,768]{1,0:T(8,128)}, f32[384,768]{1,0:T(8,128)S(1)}, u32[]{:S(2)}) copy-start(f32[384,768]{1,0:T(8,128)S(1)} %get-tuple-element.177) | copy-start | bytes 3538948
  399.1 457.8 %copy-start.124 = (f32[384]{0:T(512)}, f32[384]{0:T(512)S(1)}, u32[]{:S(2)}) copy-start(f32[384]{0:T(512)S(1)} %broadcast_multiply_fusion.19) | copy-start | bytes 4612
  400.1 441.2 %copy-start.137 = (f32[384]{0:T(512)}, f32[384]{0:T(512)S(1)}, u32[]{:S(2)}) copy-start(f32[384]{0:T(512)S(1)} %add_rsqrt_fusion.3) | copy-start | bytes 4612
  860.0 56.8 %copy-start.13 = (f32[384,768]{1,0:T(8,128)}, f32[384,768]{1,0:T(8,128)S(1)}, u32[]{:S(2)}) copy-start(f32[384,768]{1,0:T(8,128)S(1)} %get-tuple-element.180) | copy-start | bytes 3538948
  918.5 55.8 %copy-start.10 = (f32[384,768]{1,0:T(8,128)}, f32[384,768]{1,0:T(8,128)S(1)}, u32[]{:S(2)}) copy-start(f32[384,768]{1,0:T(8,128)S(1)} %get-tuple-element.198) | copy-start | bytes 3538948
  918.5 105.8 %copy-start.127 = (f32[384]{0:T(512)}, f32[384]{0:T(512)S(1)}, u32[]{:S(2)}) copy-start(f32[384]{0:T(512)S(1)} %broadcast_multiply_fusion.17) | copy-start | bytes 4612
  1131.7 61.7 %copy-start.82 = (bf16[12,64,384]{2,1,0:T(8,128)(2,1)}, bf16[12,64,384]{2,1,0:T(8,128)(2,1)S(1)}, u32[]{:S(2)}) copy-start(bf16[12,64,384]{2,1,0:T(8,128)(2,1)S(1)} %fusion.73) | copy-start | bytes 1769476
  1133.3 60.0 %copy-start.84 = (bf16[12,64,384]{2,1,0:T(8,128)(2,1)}, bf16[12,64,384]{2,1,0:T(8,128)(2,1)S(1)}, u32[]{:S(2)}) copy-start(bf16[12,64,384]{2,1,0:T(8,128)(2,1)S(1)} %get-tuple-element.223) | copy-start | bytes 1769476
  1198.5 971.3 %all-reduce.52.cloned.1.call-start = ((), (), s32[]{:S(2)}) async-start(), calls=%async_computation.9 | async-start | bytes 113246208
  (227 other events, 1703.8 us)
Sparse Core Ops, SparseCore 0:
  11.6 60.2 all-gather.44
  74.8 56.2 all-gather.36
  134.6 71.5 all-gather.34
  208.9 71.2 all-gather.42
  283.5 80.6 all-gather.38
  367.5 80.6 all-gather.46
  451.7 80.6 all-gather.48
  535.8 80.6 all-gather.40
  1198.6 149.4 all-reduce.49
  1354.4 815.3 all-reduce.51
where the time goes:
time: 2200 us; the launch traced here: 2190 us
  waiting for transfers between devices  946 us (43%)
  other arithmetic  682 us (31%)
  matrix products  310 us (14%)
  local copies, waits for them, and re-layouts  190 us (9%)
  blocking collectives  43.1 us (2%)
    unnamed x12, waiting for transfers between devices  873 us
    all_gather x2, other arithmetic, local(): lax.all_gather(shard_set[7], ('wide', 'narrow'), axis=0, tiled=True)  203 us
    all_gather x2, other arithmetic, local(): lax.all_gather(shard_set[9], ('wide', 'narrow'), axis=0, tiled=True)  202 us
    all_gather x2, other arithmetic, local(): lax.all_gather(shard_set[0], ('wide', 'narrow'), axis=0, tiled=True)  149 us
    dot_general x4, matrix products, forward_layer(): jnp.einsum('nsd,df->nsf', first_low, w_expand, preferred_element_type=jnp...  61 us
    unnamed x537, local copies, waits for them, and re-layouts  52.4 us
    add x11, local copies, waits for them, and re-layouts, local(): previous + current  52.2 us
    all_gather x2, other arithmetic, local(): lax.all_gather(shard_set[3], ('wide', 'narrow'), axis=0, tiled=True)  51.1 us
  transfers between devices with their start and end apart: 10, of which 4 were waited for; matrix products, arithmetic and copies ran while one was open for 32% of the time, Pallas kernels for 0%

commit v1 on v0

v1 whole, which is shorter than its diff:
```python
import math
from functools import partial

import jax
import jax.numpy as jnp
from jax import lax
from jax.experimental import pallas as pl
from jax.experimental.pallas import tpu as pltpu
from jax.sharding import PartitionSpec as P

HEAD_DIM = 64
EPSILON = 1e-06
AXES = ("wide", "narrow")
F32 = jnp.float32
BF16 = jnp.bfloat16
ANY = pl.BlockSpec(memory_space=pl.ANY)
VMEM = pl.BlockSpec(memory_space=pltpu.VMEM)
SMEM = pl.BlockSpec(memory_space=pltpu.SMEM)
LIMIT = 60 * 2**20
SHARE = 48


def mm(left, right, over=(1, 0)):
    return lax.dot_general(
        left, right, (((over[0],), (over[1],)), ((), ())), preferred_element_type=F32
    )


def nt(left, right):
    return mm(left, right, (1, 1))


def tn(left, right):
    return mm(left, right, (0, 0))


def norm_rows(h):
    centred = h - jnp.mean(h, axis=-1, keepdims=True)
    inv = lax.rsqrt(jnp.mean(centred * centred, axis=-1, keepdims=True) + EPSILON)
    return centred * inv, inv


def norm_rows_back(g, n, inv, gain):
    t = g * gain
    return inv * (
        t
        - jnp.mean(t, axis=-1, keepdims=True)
        - n * jnp.mean(t * n, axis=-1, keepdims=True)
    )


def gelu_pair(f):
    u = jnp.abs(f)
    t = 1.0 / (1.0 + (0.3275911 / math.sqrt(2.0)) * u)
    e = jnp.exp(-0.5 * f * f)
    c = [0.5 * v for v in (0.254829592, -0.284496736, 1.421413741, -1.453152027, 1.061405429)]
    tail = e * (t * (c[0] + t * (c[1] + t * (c[2] + t * (c[3] + t * c[4])))))
    phi = jnp.where(f >= 0, 1.0 - tail, tail)
    return f * phi, phi + f * (e * (1.0 / math.sqrt(2.0 * math.pi)))


def even_lanes():
    return lax.broadcasted_iota(jnp.int32, (1, 2 * HEAD_DIM), 1) < HEAD_DIM


def place_of(idx, block, far, first_is_x):
    k, other = block % 4, block // 4
    z = idx[0] ^ (3 * (k % 2)) ^ (k // 2)
    if first_is_x:
        x, y = idx[1] ^ other, idx[2] ^ far
    else:
        x, y = idx[1] ^ far, idx[2] ^ other
    return z * 4 + x * 2 + y


def relative_of(idx, chip, first_is_x):
    r = (chip // 4) ^ idx[0]
    k = (r // 2) + 2 * ((r ^ (r // 2)) % 2)
    i = (chip // 2 % 2) ^ idx[1]
    j = (chip % 2) ^ idx[2]
    return (i * 8 + j * 4 + k) if first_is_x else (j * 8 + i * 4 + k)


def copy(src, dst, sem):
    return pltpu.make_async_copy(src, dst, sem)


def attn_forward_kernel(count, idx, x_ref, vec, *refs):
    given, refs = refs[:count], refs[count:]
    y1_ref, n1_ref, r1_ref, qkv_ref, p_ref, att_ref, w_ref, w, qkv, p, att, sem_in, sem_out = refs
    c = idx[3]

    def fetch(block, carry):
        for s, pieces in enumerate((given[:4], given[4:8])):
            for far in range(2):
                chip = place_of(idx, block, far, s == 0)
                rows = pl.ds(pl.multiple_of(chip * SHARE, SHARE), SHARE)
                for side in range(2):
                    copy(
                        pieces[2 * side + far].at[block, 0],
                        w.at[2 * s + (c ^ side), rows],
                        sem_in.at[2 * s + side],
                    ).start()
        return carry

    def fetch_whole(chip, carry):
        rows = pl.ds(pl.multiple_of(chip * SHARE, SHARE), SHARE)
        for s in range(2):
            for core in range(2):
                copy(given[0].at[2 * chip + core, 0, s], w.at[2 * s + core, rows], sem_in.at[2 * s + core]).start()
        return carry

    if count == 1:
        lax.fori_loop(0, 16, fetch_whole, 0)
    else:
        lax.fori_loop(0, 8, fetch, 0)
    for i in range(4):
        copy(w.at[0], w.at[0], sem_in.at[i]).wait()
    save_w = copy(w, w_ref, sem_out.at[0])
    save_w.start()
    length = x_ref.shape[0] // 2
    for n in range(2):
        rows = slice(n * length, (n + 1) * length)
        xr = x_ref[rows].astype(BF16)
        qkv[0, rows] = (mm(xr, w[0]) + vec[0:1]).astype(BF16)
        qkv[1, rows] = mm(xr, w[1]).astype(BF16)
        qkv[2, rows] = (mm(xr, w[2]) + vec[1:2]).astype(BF16)
    save_qkv = copy(qkv, qkv_ref, sem_out.at[1])
    save_qkv.start()
    pairs = x_ref.shape[1] // (2 * HEAD_DIM)
    places = lax.broadcasted_iota(jnp.int32, (1, length), 1)

    def pair(step, carry):
        n, j = step // pairs, step % pairs
        rows = pl.ds(pl.multiple_of(n * length, length), length)
        lanes = pl.ds(pl.multiple_of(j * 2 * HEAD_DIM, 2 * HEAD_DIM), 2 * HEAD_DIM)
        even = even_lanes()
        hidden = jnp.where(places < idx[4 + n], 0.0, -1e30)
        q2 = qkv[0, rows, lanes] * jnp.asarray(HEAD_DIM**-0.5, BF16)
        k2 = qkv[1, rows, lanes]
        v2 = qkv[2, rows, lanes]
        parts = []
        for h in range(2):
            mine = even if h == 0 else jnp.logical_not(even)
            s = nt(jnp.where(mine, q2, jnp.zeros_like(q2)), k2) + hidden
            e = jnp.exp(s - jnp.max(s, axis=-1, keepdims=True))
            soft = (e * (1.0 / jnp.sum(e, axis=-1, keepdims=True))).astype(BF16)
            p[2 * step + h] = soft
            parts.append(mm(soft, v2))
        att[rows, lanes] = jnp.where(even, parts[0], parts[1]).astype(BF16)
        copy(p.at[pl.ds(2 * step, 2)], p_ref.at[pl.ds(2 * step, 2)], sem_out.at[2]).start()
        return carry

    lax.fori_loop(0, 2 * pairs, pair, 0)
    save_att = copy(att, att_ref, sem_out.at[3])
    save_att.start()
    for n in range(2):
        rows = slice(n * length, (n + 1) * length)
        h = x_ref[rows].astype(F32) + (mm(att[rows], w[3]) + vec[2:3])
        normed, inv = norm_rows(h)
        n1_ref[rows] = normed
        r1_ref[rows] = inv
        y1_ref[rows] = normed * vec[3:4] + vec[4:5]
    save_w.wait()
    save_qkv.wait()
    copy(p, p_ref, sem_out.at[2]).wait()
    save_att.wait()


def attn_forward(idx, x, vec, pieces):
    t, d = x.shape
    heads = d // HEAD_DIM
    length = t // 2
    return pl.pallas_call(
        partial(attn_forward_kernel, len(pieces)),
        in_specs=[SMEM, VMEM, VMEM] + [ANY] * len(pieces),
        out_specs=[VMEM, VMEM, VMEM, ANY, ANY, ANY, ANY],
        out_shape=[
            jax.ShapeDtypeStruct((t, d), F32),
            jax.ShapeDtypeStruct((t, d), F32),
            jax.ShapeDtypeStruct((t, 1), F32),
            jax.ShapeDtypeStruct((3, t, d), BF16),
            jax.ShapeDtypeStruct((2 * heads, length, length), BF16),
            jax.ShapeDtypeStruct((t, d), BF16),
            jax.ShapeDtypeStruct((4, d, d), BF16),
        ],
        scratch_shapes=[
            pltpu.VMEM((4, d, d), BF16),
            pltpu.VMEM((3, t, d), BF16),
            pltpu.VMEM((2 * heads, length, length), BF16),
            pltpu.VMEM((t, d), BF16),
            pltpu.SemaphoreType.DMA((4,)),
            pltpu.SemaphoreType.DMA((4,)),
        ],
        compiler_params=pltpu.CompilerParams(vmem_limit_bytes=LIMIT),
        cost_estimate=pl.CostEstimate(flops=8 * t * d * d + 4 * t * length * d, bytes_accessed=40 * 2**20, transcendentals=2 * heads * length * length),
        name="attn_forward",
    )(idx, x, vec, *pieces)


def ffn_forward_kernel(count, idx, y1_ref, vec, *refs):
    given, refs = refs[:count], refs[count:]
    x_ref, n2_ref, r2_ref, ur_ref, gp_ref, we_ref, wc_ref, we, wc, ur, gp, acc, sem_in, sem_out = refs
    c = idx[3]

    def fetch(block, carry):
        for s, pieces in enumerate((given[:4], given[4:8])):
            for far in range(2):
                chip = place_of(idx, block, far, s == 0)
                rows = pl.ds(pl.multiple_of(chip * SHARE, SHARE), SHARE)
                for side in range(2):
                    core = c ^ side
                    piece = pieces[2 * side + far]
                    copy(piece.at[block, 0], we.at[2 * core + s, rows], sem_in.at[2 * s + side]).start()
                    down = pl.ds(pl.multiple_of(chip * 4 * SHARE + core * 2 * SHARE + s * SHARE, SHARE), SHARE)
                    copy(piece.at[block, 1], wc.at[down], sem_in.at[4 + 2 * s + side]).start()
        return carry

    def fetch_whole(chip, carry):
        rows = pl.ds(pl.multiple_of(chip * SHARE, SHARE), SHARE)
        for s in range(2):
            for core in range(2):
                share = given[0].at[2 * chip + core]
                copy(share.at[1, s], we.at[2 * core + s, rows], sem_in.at[2 * s + core]).start()
                down = pl.ds(pl.multiple_of(chip * 4 * SHARE + core * 2 * SHARE + s * SHARE, SHARE), SHARE)
                copy(share.at[2, s], wc.at[down], sem_in.at[4 + 2 * s + core]).start()
        return carry

    if count == 1:
        lax.fori_loop(0, 16, fetch_whole, 0)
    else:
        lax.fori_loop(0, 8, fetch, 0)
    for i in range(4):
        copy(we.at[0], we.at[0], sem_in.at[i]).wait()
    save_we = copy(we, we_ref, sem_out.at[0])
    save_we.start()
    d = y1_ref.shape[1]
    length = y1_ref.shape[0] // 2
    save_wc = copy(wc, wc_ref, sem_out.at[1])
    for j in range(4):
        cols = slice(j * d, (j + 1) * d)
        for n in range(2):
            rows = slice(n * length, (n + 1) * length)
            f = mm(y1_ref[rows].astype(BF16), we[j]) + vec[5 + j : 6 + j]
            u, slope = gelu_pair(f)
            u = u.astype(BF16)
            ur[j, rows] = u
            gp[j, rows] = slope.astype(BF16)
            if j == 0 and n == 0:
                for i in range(4):
                    copy(we.at[0], we.at[0], sem_in.at[4 + i]).wait()
                save_wc.start()
            part = mm(u, wc[cols])
            if j == 0:
                acc[rows] = part
            else:
                acc[rows] += part
        copy(ur.at[j], ur_ref.at[j], sem_out.at[2]).start()
        copy(gp.at[j], gp_ref.at[j], sem_out.at[3]).start()
    for n in range(2):
        rows = slice(n * length, (n + 1) * length)
        normed, inv = norm_rows(y1_ref[rows] + (acc[rows] + vec[9:10]))
        n2_ref[rows] = normed
        r2_ref[rows] = inv
        x_ref[rows] = normed * vec[10:11] + vec[11:12]
    save_we.wait()
    save_wc.wait()
    copy(ur, ur_ref, sem_out.at[2]).wait()
    copy(gp, gp_ref, sem_out.at[3]).wait()


def ffn_forward(idx, y1, vec, pieces):
    t, d = y1.shape
    hidden = 4 * d
    return pl.pallas_call(
        partial(ffn_forward_kernel, len(pieces)),
        in_specs=[SMEM, VMEM, VMEM] + [ANY] * len(pieces),
        out_specs=[VMEM, VMEM, VMEM, ANY, ANY, ANY, ANY],
        out_shape=[
            jax.ShapeDtypeStruct((t, d), F32),
            jax.ShapeDtypeStruct((t, d), F32),
            jax.ShapeDtypeStruct((t, 1), F32),
            jax.ShapeDtypeStruct((4, t, d), BF16),
            jax.ShapeDtypeStruct((4, t, d), BF16),
            jax.ShapeDtypeStruct((4, d, d), BF16),
            jax.ShapeDtypeStruct((hidden, d), BF16),
        ],
        scratch_shapes=[
            pltpu.VMEM((4, d, d), BF16),
            pltpu.VMEM((hidden, d), BF16),
            pltpu.VMEM((4, t, d), BF16),
            pltpu.VMEM((4, t, d), BF16),
            pltpu.VMEM((t, d), F32),
            pltpu.SemaphoreType.DMA((8,)),
            pltpu.SemaphoreType.DMA((4,)),
        ],
        compiler_params=pltpu.CompilerParams(vmem_limit_bytes=LIMIT),
        cost_estimate=pl.CostEstimate(flops=4 * t * d * hidden, bytes_accessed=40 * 2**20, transcendentals=2 * t * hidden),
        name="ffn_forward",
    )(idx, y1, vec, *pieces)


def send_rows(idx, block, chip, core, s, m, sums, sem):
    if len(sums) == 1:
        copy(block, sums[0].at[2 * chip + core, s, m], sem).start()
        return
    keep, give = sums
    to = jnp.where(s == 1, relative_of(idx, chip, True), relative_of(idx, chip, False))

    @pl.when(core == idx[3])
    def _():
        copy(block, keep.at[s, to, m], sem).start()

    @pl.when(core != idx[3])
    def _():
        copy(block, give.at[s, to, m], sem).start()


def send_square(idx, stage, core, s, m, sums, sem):
    def go(chip, carry):
        rows = pl.ds(pl.multiple_of(chip * SHARE, SHARE), SHARE)
        send_rows(idx, stage.at[rows], chip, core, s, m, sums, sem)
        return carry

    lax.fori_loop(0, 16, go, 0)


def sums_shapes(d, whole, m=1):
    if whole:
        return [jax.ShapeDtypeStruct((32, 2, m, SHARE, d), BF16)]
    return [jax.ShapeDtypeStruct((2, 16, 1, SHARE, d), BF16)] * 2


def halves_of(ref):
    length = ref.shape[0] // 2
    return [slice(n * length, (n + 1) * length) for n in range(2)]


def add_small(ref, row, value):
    ref[row : row + 1] += jnp.sum(value.astype(F32), axis=0, keepdims=True)


def contract_backward_kernel(count, idx, g_ref, n2_ref, r2_ref, vec, ur_ref, gp_ref, wc_ref, *refs):
    dh2_ref, small_ref, ef_ref = refs[:3]
    sums, refs = refs[3 : 3 + count], refs[3 + count :]
    wc, ur, gp, stage, e2, sem_in, sem_out = refs
    d = g_ref.shape[1]
    loads = []
    for j in range(4):
        cols = pl.ds(j * d, d)
        loads.append([
            copy(ur_ref.at[j], ur.at[j], sem_in.at[3 * j]),
            copy(wc_ref.at[cols], wc.at[cols], sem_in.at[3 * j + 1]),
            copy(gp_ref.at[j], gp.at[j], sem_in.at[3 * j + 2]),
        ])
        for load in loads[j]:
            load.start()
    small_ref[...] = jnp.zeros_like(small_ref)
    for rows in halves_of(g_ref):
        g, normed = g_ref[rows].astype(F32), n2_ref[rows]
        add_small(small_ref, 5, g * normed)
        add_small(small_ref, 6, g)
        dh2 = norm_rows_back(g, normed, r2_ref[rows], vec[10:11])
        low = dh2.astype(BF16)
        add_small(small_ref, 4, low)
        dh2_ref[rows] = dh2
        e2[rows] = low
    for j in range(4):
        cols = slice(j * d, (j + 1) * d)
        for load in loads[j]:
            load.wait()
        stage[j] = tn(ur[j], e2[...]).astype(BF16)

        def go(b, carry):
            rows = pl.ds(pl.multiple_of(b * SHARE, SHARE), SHARE)
            send_rows(idx, stage.at[j, rows], 4 * j + b // 4, b // 2 % 2, b % 2, len(sums) % 2, sums, sem_out.at[0])
            return carry

        lax.fori_loop(0, 16, go, 0)
        for rows in halves_of(g_ref):
            ef = (nt(e2[rows], wc[cols]) * gp[j, rows].astype(F32)).astype(BF16)
            gp[j, rows] = ef
            add_small(small_ref, j, ef)
        copy(gp.at[j], ef_ref.at[j], sem_out.at[1]).start()
    copy(stage, stage, sem_out.at[0]).wait()
    copy(gp, ef_ref, sem_out.at[1]).wait()


def contract_backward(whole, idx, g, n2, r2, vec, ur, gp, wc):
    t, d = n2.shape
    sums = sums_shapes(d, whole, 2)
    return pl.pallas_call(
        partial(contract_backward_kernel, len(sums)),
        in_specs=[SMEM] + [VMEM] * 4 + [ANY] * 3,
        out_specs=[VMEM, VMEM, ANY] + [ANY] * len(sums),
        out_shape=[
            jax.ShapeDtypeStruct((t, d), F32),
            jax.ShapeDtypeStruct((8, d), F32),
            jax.ShapeDtypeStruct((4, t, d), BF16),
            *sums,
        ],
        scratch_shapes=[
            pltpu.VMEM((4 * d, d), BF16),
            pltpu.VMEM((4, t, d), BF16),
            pltpu.VMEM((4, t, d), BF16),
            pltpu.VMEM((4, d, d), BF16),
            pltpu.VMEM((t, d), BF16),
            pltpu.SemaphoreType.DMA((12,)),
            pltpu.SemaphoreType.DMA((2,)),
        ],
        compiler_params=pltpu.CompilerParams(vmem_limit_bytes=LIMIT),
        cost_estimate=pl.CostEstimate(flops=16 * t * d * d, bytes_accessed=40 * 2**20, transcendentals=0),
        name="contract_backward",
    )(idx, g, n2, r2, vec, ur, gp, wc)


def expand_backward_kernel(count, idx, dh2_ref, n1_ref, r1_ref, vec, ef_ref, we_ref, w_ref, *refs):
    if count == 1:
        refs = refs[1:]
    dh1_ref, small_ref, da_ref = refs[:3]
    sums, refs = refs[3 : 3 + count], refs[3 + count :]
    we, ef, wo, stage, y1r, dy1, sem_in, sem_out = refs
    loads = []
    for j in range(4):
        loads.append([copy(ef_ref.at[j], ef.at[j], sem_in.at[2 * j]), copy(we_ref.at[j], we.at[j], sem_in.at[2 * j + 1])])
        for load in loads[j]:
            load.start()
    last = copy(w_ref.at[3], wo, sem_in.at[8])
    last.start()
    small_ref[...] = jnp.zeros_like(small_ref)
    for rows in halves_of(dh2_ref):
        y1r[rows] = (n1_ref[rows] * vec[3:4] + vec[4:5]).astype(BF16)
    for j in range(4):
        for load in loads[j]:
            load.wait()
        stage[j] = tn(y1r[...], ef[j]).astype(BF16)
        send_square(idx, stage.at[j], j // 2, j % 2, 0, sums, sem_out.at[0])
        for rows in halves_of(dh2_ref):
            part = nt(ef[j, rows], we[j])
            dy1[rows] = (dh2_ref[rows] if j == 0 else dy1[rows]) + part
    last.wait()
    for rows in halves_of(dh2_ref):
        g, normed = dy1[rows], n1_ref[rows]
        add_small(small_ref, 1, g * normed)
        add_small(small_ref, 2, g)
        dh1 = norm_rows_back(g, normed, r1_ref[rows], vec[3:4])
        dh1_ref[rows] = dh1
        e1 = dh1.astype(BF16)
        add_small(small_ref, 0, e1)
        da_ref[rows] = nt(e1, wo[...]).astype(BF16)
    copy(stage, stage, sem_out.at[0]).wait()


def expand_backward(whole, idx, dh2, n1, r1, vec, ef, we, w, *passed):
    t, d = dh2.shape
    sums = sums_shapes(d, whole, 2)
    return pl.pallas_call(
        partial(expand_backward_kernel, len(sums)),
        in_specs=[SMEM] + [VMEM] * 4 + [ANY] * (3 + len(passed)),
        out_specs=[VMEM, VMEM, VMEM] + [ANY] * len(sums),
        input_output_aliases={8: 3} if passed else {},
        out_shape=[
            jax.ShapeDtypeStruct((t, d), F32),
            jax.ShapeDtypeStruct((8, d), F32),
            jax.ShapeDtypeStruct((t, d), BF16),
            *sums,
        ],
        scratch_shapes=[
            pltpu.VMEM((4, d, d), BF16),
            pltpu.VMEM((4, t, d), BF16),
            pltpu.VMEM((d, d), BF16),
            pltpu.VMEM((4, d, d), BF16),
            pltpu.VMEM((t, d), BF16),
            pltpu.VMEM((t, d), F32),
            pltpu.SemaphoreType.DMA((9,)),
            pltpu.SemaphoreType.DMA((1,)),
        ],
        compiler_params=pltpu.CompilerParams(vmem_limit_bytes=LIMIT),
        cost_estimate=pl.CostEstimate(flops=18 * t * d * d, bytes_accessed=40 * 2**20, transcendentals=0),
        name="expand_backward",
    )(idx, dh2, n1, r1, vec, ef, we, w, *passed)


def heads_backward_kernel(da_ref, qkv_ref, p_ref, back_ref, small_ref, p, sem_in):
    t, d = da_ref.shape
    length = t // 2
    pairs = d // (2 * HEAD_DIM)
    factor = HEAD_DIM**-0.5
    steps = 2 * pairs

    def load(step, slot):
        return copy(p_ref.at[pl.ds(2 * step, 2)], p.at[slot], sem_in.at[slot])

    load(0, 0).start()

    def pair(step, carry):
        slot = step % 2

        @pl.when(step + 1 < steps)
        def _():
            load(step + 1, 1 - slot).start()

        load(step, slot).wait()
        n, j = step // pairs, step % pairs
        rows = pl.ds(pl.multiple_of(n * length, length), length)
        lanes = pl.ds(pl.multiple_of(j * 2 * HEAD_DIM, 2 * HEAD_DIM), 2 * HEAD_DIM)
        even = even_lanes()
        q2, k2, v2 = (qkv_ref[i, rows, lanes] for i in range(3))
        da2 = da_ref[rows, lanes]
        dqs, dks, dvs = [], [], []
        for h in range(2):
            mine = even if h == 0 else jnp.logical_not(even)
            soft = p[slot, h]
            dp = nt(jnp.where(mine, da2, jnp.zeros_like(da2)), v2)
            dvs.append(tn(soft, da2))
            soft = soft.astype(F32)
            inner = jnp.sum(soft * dp, axis=-1, keepdims=True)
            ds = (soft * (dp - inner)).astype(BF16)
            dqs.append(mm(ds, k2))
            dks.append(tn(ds, q2))
        dq, dk, dv = (jnp.where(even, m[0], m[1]) for m in (dqs, dks, dvs))
        back_ref[0, rows, lanes] = (dq * factor).astype(BF16)
        back_ref[1, rows, lanes] = (dk * factor).astype(BF16)
        back_ref[2, rows, lanes] = dv.astype(BF16)
        return carry

    lax.fori_loop(0, steps, pair, 0)
    small_ref[0:1] = jnp.sum(back_ref[0].astype(F32), axis=0, keepdims=True)
    small_ref[1:2] = jnp.sum(back_ref[2].astype(F32), axis=0, keepdims=True)


def heads_backward(da, qkv, p):
    t, d = da.shape
    length = t // 2
    return pl.pallas_call(
        heads_backward_kernel,
        in_specs=[VMEM, VMEM, ANY],
        out_specs=[VMEM, VMEM],
        out_shape=[jax.ShapeDtypeStruct((3, t, d), BF16), jax.ShapeDtypeStruct((8, d), F32)],
        scratch_shapes=[pltpu.VMEM((2, 2, length, length), BF16), pltpu.SemaphoreType.DMA((2,))],
        compiler_params=pltpu.CompilerParams(vmem_limit_bytes=LIMIT),
        cost_estimate=pl.CostEstimate(flops=30 * t * length * d, bytes_accessed=20 * 2**20, transcendentals=0),
        name="heads_backward",
    )(da, qkv, p)


def inward_backward_kernel(count, idx, dh1_ref, x_ref, att_ref, back, w_ref, *refs):
    dx_ref = refs[0]
    sums, refs = refs[1 : 1 + count], refs[1 + count :]
    w, stage, sem_in, sem_out = refs
    load = copy(w_ref, w, sem_in.at[0])
    load.start()
    xr = x_ref[...].astype(BF16)
    for i, (core, s) in enumerate(((0, 0), (1, 0), (0, 1))):
        stage[i] = tn(xr, back[i]).astype(BF16)
        send_square(idx, stage.at[i], core, s, 0, sums, sem_out.at[0])
    stage[3] = tn(att_ref[...], dh1_ref[...].astype(BF16)).astype(BF16)
    send_square(idx, stage.at[3], 1, 1, 0, sums, sem_out.at[0])
    load.wait()
    for rows in halves_of(dh1_ref):
        dx_ref[rows] = dh1_ref[rows] + (nt(back[0, rows], w[0]) + nt(back[1, rows], w[1]) + nt(back[2, rows], w[2]))
    copy(stage, stage, sem_out.at[0]).wait()


def inward_backward(whole, idx, dh1, x, att, back, w):
    t, d = dh1.shape
    sums = sums_shapes(d, whole)
    return pl.pallas_call(
        partial(inward_backward_kernel, len(sums)),
        in_specs=[SMEM] + [VMEM] * 4 + [ANY],
        out_specs=[VMEM] + [ANY] * len(sums),
        out_shape=[jax.ShapeDtypeStruct((t, d), F32), *sums],
        scratch_shapes=[
            pltpu.VMEM((4, d, d), BF16),
            pltpu.VMEM((4, d, d), BF16),
            pltpu.SemaphoreType.DMA((1,)),
            pltpu.SemaphoreType.DMA((1,)),
        ],
        compiler_params=pltpu.CompilerParams(vmem_limit_bytes=LIMIT),
        cost_estimate=pl.CostEstimate(flops=14 * t * d * d, bytes_accessed=30 * 2**20, transcendentals=0),
        name="inward_backward",
    )(idx, dh1, x, att, back, w)


BITS = {"c": 1, "y": 2, "x": 4, "z1": 8, "z2": 16, "z3": 24}


def swap(array, by):
    return lax.ppermute(array, AXES, [(i, i ^ BITS[by]) for i in range(32)])


def tie(values, *others):
    return lax.optimization_barrier((values, others))[0]


def pair_up(share):
    return jnp.stack([share, swap(share, "z3")])


def column_up(pair):
    return jnp.concatenate([pair, swap(pair, "z1")])


def near_up(cols):
    return tuple(jnp.concatenate([col, swap(col, by)]) for col, by in zip(cols, "xy"))


def far_up(near):
    return tuple(swap(piece, by) for piece, by in zip(near, "yx"))


def other_core(pieces):
    return tuple(swap(piece, "c") for piece in pieces)


def in_order(near, far, near_c, far_c):
    return sum(((near[s], far[s], near_c[s], far_c[s]) for s in range(2)), ())


def place_small(qb, vb, ob, ag, ash, eb, cb, fg, fs, width, device):
    layers, rows = qb.shape
    lanes = lax.broadcasted_iota(jnp.int32, (1, 1, width), 2)
    thin = jnp.stack([qb, vb, ob, ag, ash, cb, fg, fs], axis=1).astype(F32)
    thin = jnp.where(lanes // rows == device, jnp.tile(thin, (1, 1, width // rows)), 0.0)
    lines = lax.broadcasted_iota(jnp.int32, (1, 4, width), 1)
    wide = jnp.tile(eb.astype(F32)[:, None], (1, 4, width // eb.shape[1]))
    wide = jnp.where(lines * (width // eb.shape[1]) + lanes // eb.shape[1] == device, wide, 0.0)
    return jnp.concatenate([thin[:, 0:5], wide, thin[:, 5:8], jnp.zeros((layers, 4, width), F32)], axis=1)


def own_small(total, rows, device):
    layers, _, width = total.shape
    thin = lax.dynamic_slice_in_dim(total, device * rows, rows, 2)
    count = width // (4 * rows)
    wide = lax.dynamic_slice(total, (0, 5 + device // count, device % count * 4 * rows), (layers, 1, 4 * rows))
    return [thin[:, i] for i in range(5)] + [wide[:, 0]] + [thin[:, i] for i in range(9, 12)]


def add_swap(array, by):
    return array + swap(array, by)


class Sums:
    def __init__(self, keep, give):
        self.both = [keep]
        self.parts = [[], []]
        self.give = give

    def total(self, s, lo, hi):
        whole = None
        for a in [b[s] for b in self.both] + self.parts[s]:
            a = a[lo:hi].astype(F32)
            whole = a if whole is None else whole + a
        return whole

    def latest(self):
        return self.parts if self.parts[0] else self.both

    def hold(self, *others):
        if self.parts[0]:
            self.parts = tie(self.parts, *others)
        else:
            self.both = tie(self.both, *others)

    def core(self):
        self.both = self.both + [swap(self.give, "c")]

    def plane(self, lo, bys):
        arrived = [swap(self.total(s, lo, 2 * lo).astype(BF16), bys[s]) for s in range(2)]
        for s in range(2):
            self.parts[s] = self.parts[s] + [arrived[s]]

    def first(self):
        self.plane(8, "yx")

    def second(self):
        self.plane(4, "xy")

    def line(self, lo, by):
        arrived = swap(jnp.stack([self.total(s, lo, 2 * lo) for s in range(2)]).astype(BF16), by)
        for s in range(2):
            self.parts[s] = self.parts[s] + [arrived[s]]

    def third(self):
        self.line(2, "z1")

    def fourth(self):
        self.line(1, "z3")

    def result(self):
        return jnp.stack([self.total(s, 0, 1)[0] for s in range(2)])


def front(first, last, rows, width, c, attention):
    layers = first.shape[0]
    first = first.reshape(layers, rows, -1)
    cut = lambda i: first[:, :, i * width : (i + 1) * width]
    if attention:
        zero, one = (cut(0), cut(2)), (cut(1), last.reshape(layers, rows, width))
    else:
        zero, one = (cut(0), cut(1)), (cut(2), cut(3))
    zero, one = jnp.stack(zero, 1), jnp.stack(one, 1)
    return jnp.where(c == 0, zero, one), jnp.where(c == 0, one, zero)


def both_cores(mine, got, c):
    return jnp.where(c == 0, jnp.concatenate([mine, got], 2), jnp.concatenate([got, mine], 2))


def gather_any(w_inward, w_outward, w_expand, w_contract, width):
    whole = lambda m, n: lax.all_gather(m, AXES, axis=0, tiled=True).reshape(-1, n)
    inward, outward = whole(w_inward, 3 * width), whole(w_outward, width)
    expand, contract = whole(w_expand, 4 * width), whole(w_contract, width)
    cut = lambda m, i: m[:, i * width : (i + 1) * width].reshape(16, SHARE, width)
    squares = [cut(inward, i) for i in range(3)] + [cut(outward, 0)] + [cut(expand, i) for i in range(4)]
    down = contract.reshape(16, 2, 2, SHARE, width)
    sides = []
    for core in range(2):
        pick = (core, 2 + core, 4 + 2 * core, 5 + 2 * core)
        pairs = [squares[i] for i in pick] + [down[:, core, s] for s in range(2)]
        sides.append(jnp.stack(pairs, 1).reshape(16, 3, 2, SHARE, width))
    return jnp.stack(sides, 1).reshape(32, 3, 2, SHARE, width)


def collect_any(attn, ffn, width):
    attn = attn.reshape(16, 2, 2, SHARE, width)
    ffn = ffn.reshape(16, 2, 2, 2, SHARE, width)
    expand, contract = ffn[:, :, :, 0], ffn[:, :, :, 1]
    inward = jnp.concatenate([attn[:, 0, 0], attn[:, 1, 0], attn[:, 0, 1]], axis=-1)
    expand = jnp.concatenate([expand[:, core, s] for core in range(2) for s in range(2)], axis=-1)
    return tuple(
        lax.psum_scatter(m.reshape(-1).astype(F32), AXES, scatter_dimension=0, tiled=True)
        for m in (inward, attn[:, 1, 1], expand, contract)
    )


def local(blocked, tokens, lengths, w_inward, qb, vb, w_outward, ob, ag, ash, w_expand, eb, w_contract, cb, fg, fs, cotangent):
    layers = w_inward.shape[0]
    width = tokens.shape[-1]
    rows = qb.shape[1]
    device = lax.axis_index("wide") * lax.axis_size("narrow") + lax.axis_index("narrow")
    me = device if blocked else jnp.int32(0)
    c = me & 1
    place = jnp.stack([me >> 3, (me >> 2) & 1, (me >> 1) & 1, c]).astype(jnp.int32)
    idx = jnp.concatenate([place, lengths.reshape(-1), jnp.zeros((2,), jnp.int32)])
    small = place_small(qb, vb, ob, ag, ash, eb, cb, fg, fs, width, device)
    x = tokens.reshape(-1, width)
    kept = []

    def keep_layer(x, attn, ffn):
        y1, n1, r1, qkv, p, att, w = attn
        out, n2, r2, ur, gp, we, wc = ffn
        kept.append((x, n1, r1, qkv, p, att, w, n2, r2, ur, gp, we, wc))
        return out

    if blocked:
        mine, got = front(w_inward, w_outward, rows, width, c, True)
        halves = lambda col: (col[:, 0, None], col[:, 1, None])
        halves2 = lambda col: (col[:, :, 0], col[:, :, 1])
        share_a = both_cores(mine, swap(got, "c"), c)
        small = add_swap(small, "c")
        mine, got = front(w_expand, None, rows, width, c, False)
        share_e = both_cores(mine, swap(got, "c"), c)
        contract = w_contract.reshape(layers, 2, SHARE, width)
        share_f = [jnp.stack([share_e[l], contract[l]]) for l in range(layers)]
        a_pair = pair_up(share_a[0])
        share, a_pair, small = tie((share_f[0], a_pair, small))
        f_pair = pair_up(share)
        a_col = column_up(a_pair)
        small = add_swap(small, "z1")
        f_pair, a_col, small = tie((f_pair, a_col, small))
        f_col = column_up(f_pair)
        a_near = near_up(halves(a_col))
        small = add_swap(small, "z2")
        a_near, small = tie((a_near, small))
        a_far = far_up(a_near)
        a_core = other_core(a_near)
        f_col, a_far, small = tie((f_col, a_far, small))
        f_near = near_up(halves2(f_col))
        small = add_swap(small, "x")
        a1_pair = pair_up(tie((share_a[1], a_far))[0])
        a_core += other_core(a_far)
        x, f_near, a1_pair, small = tie((x, f_near, a1_pair, small))
        f_far = far_up(f_near)
        small = add_swap(small, "y")
        a1_col = column_up(a1_pair)
        f_core = other_core(f_near)
        vecs = [small[l] for l in range(layers)]
        attn = attn_forward(idx, x, vecs[0], in_order(a_near, a_far, a_core[:2], a_core[2:]))
        f_far, a1_col, f_core, y1, share = tie((f_far, a1_col, f_core, attn[0], share_f[1]))
        f_core += other_core(f_far)
        a1_near = near_up(halves(a1_col))
        f1_pair = pair_up(share)
        y1, a1_near, f1_pair = tie((y1, a1_near, f1_pair))
        a1_far = far_up(a1_near)
        f1_col = column_up(f1_pair)
        ffn = ffn_forward(idx, y1, vecs[0], in_order(f_near, f_far, f_core[:2], f_core[2:]))
        x1 = keep_layer(x, (y1,) + tuple(attn[1:]), ffn)
        a1_far, f1_col, x1 = tie((a1_far, f1_col, x1))
        a1_core = other_core(a1_near + a1_far)
        f1_near = near_up(halves2(f1_col))
        x1, f1_near = tie((x1, f1_near))
        f1_far = far_up(f1_near)
        f1_core = other_core(f1_near)
        attn = attn_forward(idx, x1, vecs[1], in_order(a1_near, a1_far, a1_core[:2], a1_core[2:]))
        f1_far, f1_core, y1 = tie((f1_far, f1_core, attn[0]))
        f1_core += other_core(f1_far)
        ffn = ffn_forward(idx, y1, vecs[1], in_order(f1_near, f1_far, f1_core[:2], f1_core[2:]))
        output = keep_layer(x1, attn, ffn)
    else:
        small = lax.psum(small, AXES)
        vecs = [small[l] for l in range(layers)]
        for l in range(layers):
            pieces = (gather_any(w_inward[l], w_outward[l], w_expand[l], w_contract[l], width),)
            attn = attn_forward(idx, x, vecs[l], pieces)
            x = keep_layer(x, attn, ffn_forward(idx, attn[0], vecs[l], pieces))
        output = x
    g = cotangent.reshape(-1, width)
    w_sums, smalls = [None] * layers, [None] * layers

    def contract_back(l, g):
        x, n1, r1, qkv, p, att, w, n2, r2, ur, gp, we, wc = kept[l]
        return contract_backward(not blocked or l > 0, idx, g, n2, r2, vecs[l], ur, gp, wc)

    def expand_back(l, dh2, ef, *passed):
        x, n1, r1, qkv, p, att, w, n2, r2, ur, gp, we, wc = kept[l]
        return expand_backward(not blocked or l > 0, idx, dh2, n1, r1, vecs[l], ef, we, w, *passed)

    def heads_back(l, da):
        x, n1, r1, qkv, p, att, w, n2, r2, ur, gp, we, wc = kept[l]
        return heads_backward(da, qkv, p)

    def inward_back(l, dh1, back):
        x, n1, r1, qkv, p, att, w, n2, r2, ur, gp, we, wc = kept[l]
        return inward_backward(not blocked, idx, dh1, x, att, back, w)

    def small_rows(small_c, small_e, small_h):
        return jnp.concatenate([small_h[0:2], small_e[0:3], small_c[0:7]])

    if blocked:
        dh2, small_c, ef, whole = contract_back(1, g)
        dh1, small_e, da, whole = expand_back(1, dh2, ef, whole)
        f1 = lax.psum_scatter(whole, AXES, scatter_dimension=0, tiled=True)
        back, small_h = heads_back(1, da)
        smalls[1] = small_rows(small_c, small_e, small_h)
        g, *sums = inward_back(1, dh1, back)
        a1 = Sums(*sums)
        a1.core()
        dh2, small_c, ef, *sums = contract_back(0, g)
        c0 = Sums(*sums)
        ef, c0.give, a1.both = tie((ef, c0.give, a1.both))
        c0.core()
        a1.first()
        dh1, small_e, da, *sums = expand_back(0, dh2, ef)
        e0 = Sums(*sums)
        da, e0.give, a1.parts, c0.both = tie((da, e0.give, a1.parts, c0.both))
        e0.core()
        a1.second()
        c0.first()
        back, small_h = heads_back(0, da)
        smalls[0] = small_rows(small_c, small_e, small_h)
        back, a1.parts, c0.parts, e0.both = tie((back, a1.parts, c0.parts, e0.both))
        a1.third()
        c0.second()
        e0.first()
        g, *sums = inward_back(0, dh1, back)
        a0 = Sums(*sums)
        small, a0.give, a1.parts, c0.parts, e0.parts = tie((jnp.stack(smalls), a0.give, a1.parts, c0.parts, e0.parts))
        a0.core()
        e0.second()
        c0.third()
        a1.fourth()
        small = add_swap(small, "z2")
        small, a0.both, e0.parts, c0.parts = tie((small, a0.both, e0.parts, c0.parts))
        a0.first()
        e0.third()
        c0.fourth()
        small = add_swap(small, "z1")
        small, a0.parts, e0.parts, f1 = tie((small, a0.parts, e0.parts, f1))
        a0.second()
        e0.fourth()
        small = add_swap(small, "x")
        small, a0.parts, e0.parts = tie((small, a0.parts, e0.parts))
        a0.third()
        small = add_swap(small, "y")
        small, a0.parts = tie((small, a0.parts))
        a0.fourth()
        small = add_swap(small, "c")
        f1 = f1[0].astype(F32)
        a0, e0, c0, a1 = (m.result()[:, 0] for m in (a0, e0, c0, a1))
        w_sums = [(a0, e0, c0), (a1, f1[:, 0], f1[:, 1])]
    else:
        for l in reversed(range(layers)):
            dh2, small_c, ef, whole = contract_back(l, g)
            dh1, small_e, da, whole = expand_back(l, dh2, ef, whole)
            back, small_h = heads_back(l, da)
            g, sums_a = inward_back(l, dh1, back)
            smalls[l] = small_rows(small_c, small_e, small_h)
            w_sums[l] = collect_any(sums_a, whole, width)
        small = lax.psum(jnp.stack(smalls), AXES)
    names = ("qb", "vb", "ob", "ag", "as", "eb", "cb", "fg", "fs")
    outs = dict(zip(names, own_small(small, rows, device)))
    flat = {"in": [], "out": [], "ex": [], "co": []}
    for l in range(layers):
        if not blocked:
            for name, share in zip(("in", "out", "ex", "co"), w_sums[l]):
                flat[name].append(share)
            continue
        attn, expand, contract = w_sums[l]
        squares = jnp.stack([attn[0], attn[1], expand[0], expand[1]])
        low, high = squares[:, :rows], squares[:, rows:]
        mine = jnp.where(c == 0, low, high)
        got = swap(jnp.where(c == 0, high, low), "c")
        zero, one = jnp.where(c == 0, mine, got), jnp.where(c == 0, got, mine)
        flat["in"].append(jnp.concatenate([zero[0], one[0], zero[1]], axis=1).reshape(-1))
        flat["out"].append(one[1].reshape(-1))
        flat["ex"].append(jnp.concatenate([zero[2], zero[3], one[2], one[3]], axis=1).reshape(-1))
        flat["co"].append(contract.reshape(-1))
    flat = {k: jnp.stack(v) for k, v in flat.items()}
    shape = tokens.shape
    return (
        output.reshape(shape), g.reshape(shape), flat["in"], outs["qb"], outs["vb"], flat["out"], outs["ob"],
        outs["ag"], outs["as"], flat["ex"], outs["eb"], flat["co"], outs["cb"], outs["fg"], outs["fs"],
    )


def solution(mesh):
    flat = P(None, AXES)
    deep = P(None, AXES, None, None)
    blocked = mesh.shape["wide"] == 8 and mesh.shape["narrow"] == 4
    return jax.shard_map(
        partial(local, blocked),
        mesh=mesh,
        in_specs=(deep,) + (flat,) * 14 + (deep,),
        out_specs=(deep, deep) + (flat,) * 13,
        check_vma=False,
    )
```

time: 2200 us -> 554 us (0.25)
  waiting for transfers between devices: 946 us -> 129 us
  other arithmetic: 682 us -> 52.9 us
  matrix products: 310 us -> 0 us
  Pallas kernels: 0 us -> 246 us
  local copies, waits for them, and re-layouts: 190 us -> 22 us
  starting transfers between devices: 0.4 us -> 78.3 us
  blocking collectives: 43.1 us -> 0 us
    unnamed x12 -> x1, waiting for transfers between devices: 873 us -> 0.02 us
    all_gather x8 -> x0, other arithmetic: 605 us -> none  [the longest x2 203 us: local(): lax.all_gather(shard_set[7], ('wide', 'narrow'), axis=0, tiled=True)]
    dot_general x72 -> x0, matrix products: 310 us -> none  [the longest x4 61 us: forward_layer(): jnp.einsum('nsd,df->nsf', first_low, w_expand, preferred_element_type=jnp...]
    pallas_call x0 -> x12, Pallas kernels: none -> 246 us  [the longest x2 47.6 us: attn_forward(): pl.pallas_call(partial(attn_forward_kernel, len(pieces)), in_specs=[SMEM,...]
    ppermute x0 -> x82, waiting for transfers between devices: none -> 129 us  [swap(): return lax.ppermute(array, AXES, [(i, i ^ BITS[by]) for i in range(32)])]
    ppermute x0 -> x82, starting transfers between devices: none -> 78.2 us  [swap(): return lax.ppermute(array, AXES, [(i, i ^ BITS[by]) for i in range(32)])]
    all_gather x8 -> x0, waiting for transfers between devices: 73.4 us -> none  [the longest x2 47.2 us: local(): lax.all_gather(shard_set[0], ('wide', 'narrow'), axis=0, tiled=True)]
    add x11 -> x0, local copies, waits for them, and re-layouts: 52.2 us -> none  [local(): previous + current]
  transfers between devices with their start and end apart: 10 -> 83, of which waited for: 4 -> 27; matrix products, arithmetic and copies ran while one was open for 32% -> 11% of each run, Pallas kernels for 0% -> 27%
where the time goes in v1:
time: 554 us; the launch traced here: 544 us
  Pallas kernels  246 us (44%)
  waiting for transfers between devices  129 us (23%)
  starting transfers between devices  78.3 us (14%)
  other arithmetic  52.9 us (10%)
  local copies, waits for them, and re-layouts  22 us (4%)
  between operations  16.2 us (3%)
    ppermute x82, waiting for transfers between devices, swap(): return lax.ppermute(array, AXES, [(i, i ^ BITS[by]) for i in range(32)])  129 us
    ppermute x82, starting transfers between devices, swap(): return lax.ppermute(array, AXES, [(i, i ^ BITS[by]) for i in range(32)])  78.2 us
    pallas_call x2, Pallas kernels, attn_forward(): pl.pallas_call(partial(attn_forward_kernel, len(pieces)), in_specs=[SMEM,...  47.6 us
    pallas_call x2, Pallas kernels, ffn_forward(): pl.pallas_call(partial(ffn_forward_kernel, len(pieces)), in_specs=[SMEM,...  44.6 us
    pallas_call x2, Pallas kernels, expand_backward(): pl.pallas_call(partial(expand_backward_kernel, len(sums)), in_specs=[SMEM...  41.5 us
    pallas_call x2, Pallas kernels, contract_backward(): pl.pallas_call(partial(contract_backward_kernel, len(sums)), in_specs=[SM...  40.5 us
    pallas_call x2, Pallas kernels, heads_backward(): pl.pallas_call(heads_backward_kernel, in_specs=[VMEM, VMEM, ANY], out_spe...  37.2 us
    pallas_call x2, Pallas kernels, inward_backward(): pl.pallas_call(partial(inward_backward_kernel, len(sums)), in_specs=[SMEM...  34.3 us
  transfers between devices with their start and end apart: 83, of which 27 were waited for; matrix products, arithmetic and copies ran while one was open for 11% of the time, Pallas kernels for 27%

profile of v1, /device:TPU:0, one launch (start us, length us, event | category | flops | bytes accessed | tf_op | source)
XLA Modules:
  0.0 543.7 jit_solution(2305972817778417015)
XLA Ops:
  14.2 4.7 collective-permute-start.2
  19.0 4.5 collective-permute-done.2
  29.1 13.5 %collective-permute-done.6 = f32[2,16,768]{2,1,0:T(8,128)S(1)} collective-permute-done((f32[2,16,768]{2,1,0:T(8,128)S(1)}, f32[2,16,768]{2,1,0:T(8,128)S(1)}, u32[]{:S(2)}, u32[]{:S(2)}) %collective-permute-start.6) | collective-permute-done | bytes 98336 | tf_op jit(solution)/shard_map/ppermute | solution.py:589
  55.1 7.5 %collective-permute-done.7 = bf16[2,2,2,48,768]{4,3,1,2,0:T(8,128)(2,1)S(1)} collective-permute-done((bf16[2,2,2,48,768]{4,3,1,2,0:T(8,128)(2,1)S(1)}, bf16[2,2,2,48,768]{4,3,1,2,0:T(8,128)(2,1)S(1)}, u32[]{:S(2)}, u32[]{:S(2)}) %collective-permute-start.7) | collective-permute-done | bytes 589856 | tf_op jit(solution)/shard_map/ppermute | solution.py:589
  71.6 12.2 %collective-permute-done.16 = f32[2,16,768]{2,1,0:T(8,128)S(1)} collective-permute-done((f32[2,16,768]{2,1,0:T(8,128)S(1)}, f32[2,16,768]{2,1,0:T(8,128)S(1)}, u32[]{:S(2)}, u32[]{:S(2)}) %collective-permute-start.16) | collective-permute-done | bytes 98336 | tf_op jit(solution)/shard_map/ppermute | solution.py:589
  93.8 23.6 %attn_forward.2 = (f32[768,768]{1,0:T(8,128)}, f32[768,768]{1,0:T(8,128)}, f32[768,1]{1,0:T(8,128)}, bf16[3,768,768]{2,1,0:T(8,128)(2,1)}, bf16[24,384,384]{2,1,...) custom-call(s32[8]{0:T(128)} %concatenate.148.idx, bf16[768,768]{1,0:T(8,128)(2,1)} %bitcast.607, ...), custom_call_target="tpu_custom_call" | custom-call | flops 4529848320 | bytes 41943040 | tf_op jit(solution)/shard_map/attn_forward/pallas_call | solution.py:174
  120.6 8.4 %collective-permute-done.29 = bf16[2,2,48,768]{3,2,0,1:T(8,128)(2,1)S(1)} collective-permute-done((bf16[2,2,48,768]{3,2,0,1:T(8,128)(2,1)S(1)}, bf16[2,2,48,768]{3,2,0,1:T(8,128)(2,1)S(1)}, u32[]{:S(2)}, u32[]{:S(2)}) %collective-permute-start.29) | collective-permute-done | bytes 294944 | tf_op jit(solution)/shard_map/ppermute | solution.py:589
  129.1 6.2 %collective-permute-start.32 = (bf16[2,2,2,48,768]{4,3,1,0,2:T(8,128)(2,1)S(1)}, bf16[2,2,2,48,768]{4,3,1,0,2:T(8,128)(2,1)S(1)}, u32[]{:S(2)}, u32[]{:S(2)}) collective-permute-start(bf16[2,2,2,48,768]{4,3,1,0,2:T(8,128)(2,1)S(1)} %pad_maximum_fusion.13), channel_id=1, source_target_pairs={{0,8},{1,9},{2,10},{3,11},{4,12},{5,13},{6,14},{7,15},{8,0},{9,1},... | collective-permute-start | bytes 1769480 | tf_op jit(solution)/shard_map/ppermute | solution.py:589
  137.7 10.6 %collective-permute-done.32 = bf16[2,2,2,48,768]{4,3,1,0,2:T(8,128)(2,1)S(1)} collective-permute-done((bf16[2,2,2,48,768]{4,3,1,0,2:T(8,128)(2,1)S(1)}, bf16[2,2,2,48,768]{4,3,1,0,2:T(8,128)(2,1)S(1)}, u32[]{:S(2)}, u32[]{:S(2)}) %collective-permute-start.32) | collective-permute-done | bytes 589856 | tf_op jit(solution)/shard_map/ppermute | solution.py:589
  148.4 22.3 %ffn_forward.2 = (f32[768,768]{1,0:T(8,128)}, f32[768,768]{1,0:T(8,128)}, f32[768,1]{1,0:T(8,128)}, bf16[4,768,768]{2,1,0:T(8,128)(2,1)}, bf16[4,768,768]{2,1,0:...) custom-call(s32[8]{0:T(128)} %concatenate.148.idx, f32[768,768]{1,0:T(8,128)} %get-tuple-element.215.y1_ref, ...), custom_call_target="tpu_custom_call" | custom-call | flops 7247757312 | bytes 41943040 | tf_op jit(solution)/shard_map/ffn_forward/pallas_call | solution.py:275
  173.8 11.2 %collective-permute-done.36 = bf16[4,2,48,768]{3,2,1,0:T(8,128)(2,1)S(1)} collective-permute-done((bf16[4,2,48,768]{3,2,1,0:T(8,128)(2,1)S(1)}, bf16[4,2,48,768]{3,2,1,0:T(8,128)(2,1)S(1)}, u32[]{:S(2)}, u32[]{:S(2)}) %collective-permute-start.36) | collective-permute-done | bytes 589856 | tf_op jit(solution)/shard_map/ppermute | solution.py:589
  193.2 24.0 %attn_forward.3 = (f32[768,768]{1,0:T(8,128)}, f32[768,768]{1,0:T(8,128)}, f32[768,1]{1,0:T(8,128)}, bf16[3,768,768]{2,1,0:T(8,128)(2,1)}, bf16[24,384,384]{2,1,...) custom-call(s32[8]{0:T(128)} %concatenate.148.idx, f32[768,768]{1,0:T(8,128)} %get-tuple-element.225.x_ref, ...), custom_call_target="tpu_custom_call" | custom-call | flops 4529848320 | bytes 41943040 | tf_op jit(solution)/shard_map/attn_forward/pallas_call | solution.py:174
  222.9 22.3 %ffn_forward.3 = (f32[768,768]{1,0:T(8,128)}, f32[768,768]{1,0:T(8,128)}, f32[768,1]{1,0:T(8,128)}, bf16[4,768,768]{2,1,0:T(8,128)(2,1)}, bf16[4,768,768]{2,1,0:...) custom-call(s32[8]{0:T(128)} %concatenate.148.idx, f32[768,768]{1,0:T(8,128)} %get-tuple-element.229.y1_ref, ...), custom_call_target="tpu_custom_call" | custom-call | flops 7247757312 | bytes 41943040 | tf_op jit(solution)/shard_map/ffn_forward/pallas_call | solution.py:275
  245.2 19.0 %contract_backward.2 = (f32[768,768]{1,0:T(8,128)}, f32[8,768]{1,0:T(8,128)}, bf16[4,768,768]{2,1,0:T(8,128)(2,1)}, bf16[32,2,2,48,768]{4,3,2,1,0:T(8,128)(2,1)}) custom-call(s32[8]{0:T(128)} %concatenate.148.idx, bf16[768,768]{1,0:T(8,128)(2,1)} %bitcast.606, f32[768,768]{1,0:T(8,128)} %get-tuple-element.235.n2_ref, f32[768,1]{1,0:T(8,128)} %get-tuple-element.236.r2_ref, ...), custom_call_target="tpu_custom_call" | custom-call | flops 7247757312 | bytes 41943040 | tf_op jit(solution)/shard_map/contract_backward/pallas_call | solution.py:392
  264.3 19.8 %expand_backward.2 = (f32[768,768]{1,0:T(8,128)}, f32[8,768]{1,0:T(8,128)}, bf16[768,768]{1,0:T(8,128)(2,1)}, bf16[32,2,2,48,768]{4,3,2,1,0:T(8,128)(2,1)}) custom-call(s32[8]{0:T(128)} %concatenate.148.idx, f32[768,768]{1,0:T(8,128)} %get-tuple-element.240.dh2_ref, f32[768,768]{1,0:T(8,128)} %get-tuple-element.241.n1_ref, ...), custom_call_target="tpu_custom_call", output_to_operand_aliasing={{3}: (8, {})} | custom-call | flops 8153726976 | bytes 41943040 | tf_op jit(solution)/shard_map/expand_backward/pallas_call | solution.py:457
  284.1 18.5 %heads_backward.2 = (bf16[3,768,768]{2,1,0:T(8,128)(2,1)}, f32[8,768]{1,0:T(8,128)}) custom-call(bf16[768,768]{1,0:T(8,128)(2,1)} %get-tuple-element.249.da_ref, bf16[3,768,768]{2,1,0:T(8,128)(2,1)} %get-tuple-element.250.qkv_ref, bf16[24,384,384]{2,1,0:T(8,128)(2,1)} %get-tuple-element.251.p_ref), custom_call_target="tpu_custom_call" | custom-call | flops 6794772480 | bytes 20971520 | tf_op jit(solution)/shard_map/heads_backward/pallas_call | solution.py:535
  302.6 17.2 %inward_backward.2 = (f32[768,768]{1,0:T(8,128)}, bf16[2,16,1,48,768]{4,3,2,1,0:T(8,128)(2,1)}, bf16[2,16,1,48,768]{4,3,2,1,0:T(8,128)(2,1)}) custom-call(s32[8]{0:T(128)} %concatenate.148.idx, f32[768,768]{1,0:T(8,128)} %get-tuple-element.247.dh1_ref, f32[768,768]{1,0:T(8,128)} %get-tuple-element.225.x_ref, bf16[768,768]{1,0:T(8,128)(2,1)} %get-tuple-element.248.att_ref, ...), custom_call_target="tpu_custom_call" | custom-call | flops 6341787648 | bytes 31457280 | tf_op jit(solution)/shard_map/inward_backward/pallas_call | solution.py:568
  320.0 21.5 %contract_backward.3 = (f32[768,768]{1,0:T(8,128)}, f32[8,768]{1,0:T(8,128)}, bf16[4,768,768]{2,1,0:T(8,128)(2,1)}, bf16[2,16,1,48,768]{4,3,2,1,0:T(8,128)(2,1)}, bf16[2,16,1,48,768]{4,3,2,1,0:T(8,128)(2,1)}) custom-call(s32[8]{0:T(128)} %concatenate.148.idx, f32[768,768]{1,0:T(8,128)} %get-tuple-element.253.g_ref, f32[768,768]{1,0:T(8,128)} %get-tuple-element.254.n2_ref, ...), custom_call_target="tpu_custom_call" | custom-call | flops 7247757312 | bytes 41943040 | tf_op jit(solution)/shard_map/contract_backward/pallas_call | solution.py:392
  345.8 21.7 %expand_backward.3 = (f32[768,768]{1,0:T(8,128)}, f32[8,768]{1,0:T(8,128)}, bf16[768,768]{1,0:T(8,128)(2,1)}, bf16[2,16,1,48,768]{4,3,2,1,0:T(8,128)(2,1)}, bf16[2,16,1,48,768]{4,3,2,1,0:T(8,128)(2,1)}) custom-call(s32[8]{0:T(128)} %concatenate.148.idx, f32[768,768]{1,0:T(8,128)} %get-tuple-element.259.dh2_ref, f32[768,768]{1,0:T(8,128)} %get-tuple-element.260.n1_ref, ...), custom_call_target="tpu_custom_call" | custom-call | flops 8153726976 | bytes 41943040 | tf_op jit(solution)/shard_map/expand_backward/pallas_call | solution.py:457
  382.3 18.7 %heads_backward.3 = (bf16[3,768,768]{2,1,0:T(8,128)(2,1)}, f32[8,768]{1,0:T(8,128)}) custom-call(bf16[768,768]{1,0:T(8,128)(2,1)} %get-tuple-element.277.da_ref, bf16[3,768,768]{2,1,0:T(8,128)(2,1)} %get-tuple-element.278.qkv_ref, bf16[24,384,384]{2,1,0:T(8,128)(2,1)} %get-tuple-element.279.p_ref), custom_call_target="tpu_custom_call" | custom-call | flops 6794772480 | bytes 20971520 | tf_op jit(solution)/shard_map/heads_backward/pallas_call | solution.py:535
  420.8 17.2 %inward_backward.3 = (f32[768,768]{1,0:T(8,128)}, bf16[2,16,1,48,768]{4,3,2,1,0:T(8,128)(2,1)}, bf16[2,16,1,48,768]{4,3,2,1,0:T(8,128)(2,1)}) custom-call(s32[8]{0:T(128)} %concatenate.148.idx, f32[768,768]{1,0:T(8,128)} %get-tuple-element.269.dh1_ref, bf16[768,768]{1,0:T(8,128)(2,1)} %bitcast.608, bf16[768,768]{1,0:T(8,128)(2,1)} %get-tuple-element.270.att_ref, ...), custom_call_target="tpu_custom_call" | custom-call | flops 6341787648 | bytes 31457280 | tf_op jit(solution)/shard_map/inward_backward/pallas_call | solution.py:568
  457.7 6.8 %collective-permute-done.78 = bf16[2,1,1,48,768]{4,3,2,1,0:T(8,128)(2,1)S(1)} collective-permute-done((bf16[2,1,1,48,768]{4,3,2,1,0:T(8,128)(2,1)S(1)}, bf16[2,1,1,48,768]{4,3,2,1,0:T(8,128)(2,1)S(1)}, u32[]{:S(2)}, u32[]{:S(2)}) %collective-permute-start.78) | collective-permute-done | bytes 147488 | tf_op jit(solution)/shard_map/ppermute | solution.py:589
  506.7 4.9 collective-permute-done.70
  524.0 5.0 collective-permute-done.76
  (423 shorter events, 186.2 us)
Async XLA Ops:
  7.3 487.6 %reduce-scatter.2.cloned.1.call-start = ((), (), s32[]{:S(2)}) async-start(), calls=%async_computation.1 | async-start | bytes 9732096 | tf_op jit(solution)/shard_map/reduce_scatter | solution.py:843
  85.8 31.7 %collective-permute-start.17 = (bf16[8,2,48,768]{3,2,1,0:T(8,128)(2,1)S(1)}, bf16[8,2,48,768]{3,2,1,0:T(8,128)(2,1)}, u32[]{:S(2)}, u32[]{:S(2)}) collective-permute-start(bf16[8,2,48,768]{3,2,1,0:T(8,128)(2,1)S(1)} %pad_maximum_fusion.1.refs_0_), channel_id=1, source_target_pairs={{0,2},{1,3},{2,0},{3,1},{4,6},{5,7},{6,4},{7,5},{8,10},{9,11},{10,... | collective-permute-start | bytes 3538952 | tf_op jit(solution)/shard_map/ppermute | solution.py:589
  87.1 30.4 %collective-permute-start.20 = (bf16[8,2,48,768]{3,2,1,0:T(8,128)(2,1)S(1)}, bf16[8,2,48,768]{3,2,1,0:T(8,128)(2,1)}, u32[]{:S(2)}, u32[]{:S(2)}) collective-permute-start(bf16[8,2,48,768]{3,2,1,0:T(8,128)(2,1)S(1)} %pad_maximum_fusion.1.refs_0_), channel_id=1, source_target_pairs={{0,1},{1,0},{2,3},{3,2},{4,5},{5,4},{6,7},{7,6},{8,9},{9,8},{10,11... | collective-permute-start | bytes 3538952 | tf_op jit(solution)/shard_map/ppermute | solution.py:589
  87.1 30.4 %collective-permute-start.18 = (bf16[8,2,48,768]{3,2,1,0:T(8,128)(2,1)S(1)}, bf16[8,2,48,768]{3,2,1,0:T(8,128)(2,1)}, u32[]{:S(2)}, u32[]{:S(2)}) collective-permute-start(bf16[8,2,48,768]{3,2,1,0:T(8,128)(2,1)S(1)} %pad_maximum_fusion.2.refs_4_), channel_id=1, source_target_pairs={{0,4},{1,5},{2,6},{3,7},{4,0},{5,1},{6,2},{7,3},{8,12},{9,13},{10,... | collective-permute-start | bytes 3538952 | tf_op jit(solution)/shard_map/ppermute | solution.py:589
  88.7 28.9 %collective-permute-start.21 = (bf16[8,2,48,768]{3,2,1,0:T(8,128)(2,1)S(1)}, bf16[8,2,48,768]{3,2,1,0:T(8,128)(2,1)}, u32[]{:S(2)}, u32[]{:S(2)}) collective-permute-start(bf16[8,2,48,768]{3,2,1,0:T(8,128)(2,1)S(1)} %pad_maximum_fusion.2.refs_4_), channel_id=1, source_target_pairs={{0,1},{1,0},{2,3},{3,2},{4,5},{5,4},{6,7},{7,6},{8,9},{9,8},{10,11... | collective-permute-start | bytes 3538952 | tf_op jit(solution)/shard_map/ppermute | solution.py:589
  118.4 30.0 %collective-permute-start.33 = (bf16[8,2,48,768]{3,2,1,0:T(8,128)(2,1)}, bf16[8,2,48,768]{3,2,1,0:T(8,128)(2,1)}, u32[]{:S(2)}, u32[]{:S(2)}) collective-permute-start(bf16[8,2,48,768]{3,2,1,0:T(8,128)(2,1)} %collective-permute-done.17.refs_1_), channel_id=1, source_target_pairs={{0,1},{1,0},{2,3},{3,2},{4,5},{5,4},{6,7},{7,6},{8,9},{9,8},{10,11... | collective-permute-start | bytes 3538952 | tf_op jit(solution)/shard_map/ppermute | solution.py:589
  118.7 29.7 %collective-permute-start.34 = (bf16[8,2,48,768]{3,2,1,0:T(8,128)(2,1)}, bf16[8,2,48,768]{3,2,1,0:T(8,128)(2,1)}, u32[]{:S(2)}, u32[]{:S(2)}) collective-permute-start(bf16[8,2,48,768]{3,2,1,0:T(8,128)(2,1)} %collective-permute-done.18.refs_5_), channel_id=1, source_target_pairs={{0,1},{1,0},{2,3},{3,2},{4,5},{5,4},{6,7},{7,6},{8,9},{9,8},{10,11... | collective-permute-start | bytes 3538952 | tf_op jit(solution)/shard_map/ppermute | solution.py:589
  135.4 35.4 %collective-permute-start.30 = (bf16[8,1,48,768]{3,2,1,0:T(8,128)(2,1)S(1)}, bf16[8,1,48,768]{3,2,1,0:T(8,128)(2,1)}, u32[]{:S(2)}, u32[]{:S(2)}) collective-permute-start(bf16[8,1,48,768]{3,2,1,0:T(8,128)(2,1)S(1)} %pad_maximum_fusion.11.refs_0_), channel_id=1, source_target_pairs={{0,2},{1,3},{2,0},{3,1},{4,6},{5,7},{6,4},{7,5},{8,10},{9,11},{10,... | collective-permute-start | bytes 1769480 | tf_op jit(solution)/shard_map/ppermute | solution.py:589
  136.1 34.7 %collective-permute-start.31 = (bf16[8,1,48,768]{3,2,1,0:T(8,128)(2,1)S(1)}, bf16[8,1,48,768]{3,2,1,0:T(8,128)(2,1)S(1)}, u32[]{:S(2)}, u32[]{:S(2)}) collective-permute-start(bf16[8,1,48,768]{3,2,1,0:T(8,128)(2,1)S(1)} %pad_maximum_fusion.12.refs_4_), channel_id=1, source_target_pairs={{0,4},{1,5},{2,6},{3,7},{4,0},{5,1},{6,2},{7,3},{8,12},{9,13},{10,... | collective-permute-start | bytes 1769480 | tf_op jit(solution)/shard_map/ppermute | solution.py:589
  185.6 31.6 %collective-permute-start.37 = (bf16[8,2,48,768]{3,2,1,0:T(8,128)(2,1)S(1)}, bf16[8,2,48,768]{3,2,1,0:T(8,128)(2,1)}, u32[]{:S(2)}, u32[]{:S(2)}) collective-permute-start(bf16[8,2,48,768]{3,2,1,0:T(8,128)(2,1)S(1)} %pad_maximum_fusion.4.refs_0_), channel_id=1, source_target_pairs={{0,2},{1,3},{2,0},{3,1},{4,6},{5,7},{6,4},{7,5},{8,10},{9,11},{10,... | collective-permute-start | bytes 3538952 | tf_op jit(solution)/shard_map/ppermute | solution.py:589
  187.0 30.3 %collective-permute-start.39 = (bf16[8,2,48,768]{3,2,1,0:T(8,128)(2,1)S(1)}, bf16[8,2,48,768]{3,2,1,0:T(8,128)(2,1)}, u32[]{:S(2)}, u32[]{:S(2)}) collective-permute-start(bf16[8,2,48,768]{3,2,1,0:T(8,128)(2,1)S(1)} %pad_maximum_fusion.4.refs_0_), channel_id=1, source_target_pairs={{0,1},{1,0},{2,3},{3,2},{4,5},{5,4},{6,7},{7,6},{8,9},{9,8},{10,11... | collective-permute-start | bytes 3538952 | tf_op jit(solution)/shard_map/ppermute | solution.py:589
  187.0 30.2 %collective-permute-start.38 = (bf16[8,2,48,768]{3,2,1,0:T(8,128)(2,1)S(1)}, bf16[8,2,48,768]{3,2,1,0:T(8,128)(2,1)S(1)}, u32[]{:S(2)}, u32[]{:S(2)}) collective-permute-start(bf16[8,2,48,768]{3,2,1,0:T(8,128)(2,1)S(1)} %pad_maximum_fusion.5.refs_4_), channel_id=1, source_target_pairs={{0,4},{1,5},{2,6},{3,7},{4,0},{5,1},{6,2},{7,3},{8,12},{9,13},{10,... | collective-permute-start | bytes 3538952 | tf_op jit(solution)/shard_map/ppermute | solution.py:589
  188.6 28.7 %collective-permute-start.40 = (bf16[8,2,48,768]{3,2,1,0:T(8,128)(2,1)S(1)}, bf16[8,2,48,768]{3,2,1,0:T(8,128)(2,1)}, u32[]{:S(2)}, u32[]{:S(2)}) collective-permute-start(bf16[8,2,48,768]{3,2,1,0:T(8,128)(2,1)S(1)} %pad_maximum_fusion.5.refs_4_), channel_id=1, source_target_pairs={{0,1},{1,0},{2,3},{3,2},{4,5},{5,4},{6,7},{7,6},{8,9},{9,8},{10,11... | collective-permute-start | bytes 3538952 | tf_op jit(solution)/shard_map/ppermute | solution.py:589
  341.5 26.1 %collective-permute-start.50 = (bf16[2,16,1,48,768]{4,3,2,1,0:T(8,128)(2,1)}, bf16[2,16,1,48,768]{4,3,2,1,0:T(8,128)(2,1)}, u32[]{:S(2)}, u32[]{:S(2)}) collective-permute-start(bf16[2,16,1,48,768]{4,3,2,1,0:T(8,128)(2,1)} %get-tuple-element.276), channel_id=1, source_target_pairs={{0,1},{1,0},{2,3},{3,2},{4,5},{5,4},{6,7},{7,6},{8,9},{9,8},{10,11... | collective-permute-start | bytes 7077896 | tf_op jit(solution)/shard_map/ppermute | solution.py:589
  343.2 24.4 %collective-permute-start.49 = (bf16[8,1,48,768]{3,2,1,0:T(8,128)(2,1)S(1)}, bf16[8,1,48,768]{3,2,1,0:T(8,128)(2,1)S(1)}, u32[]{:S(2)}, u32[]{:S(2)}) collective-permute-start(bf16[8,1,48,768]{3,2,1,0:T(8,128)(2,1)S(1)} %fusion.1), channel_id=1, source_target_pairs={{0,4},{1,5},{2,6},{3,7},{4,0},{5,1},{6,2},{7,3},{8,12},{9,13},{10,... | collective-permute-start | bytes 1769480 | tf_op jit(solution)/shard_map/ppermute | solution.py:589
  367.6 37.9 %collective-permute-start.55 = (bf16[2,16,1,48,768]{4,3,2,1,0:T(8,128)(2,1)}, bf16[2,16,1,48,768]{4,3,2,1,0:T(8,128)(2,1)}, u32[]{:S(2)}, u32[]{:S(2)}) collective-permute-start(bf16[2,16,1,48,768]{4,3,2,1,0:T(8,128)(2,1)} %get-tuple-element.286), channel_id=1, source_target_pairs={{0,1},{1,0},{2,3},{3,2},{4,5},{5,4},{6,7},{7,6},{8,9},{9,8},{10,11... | collective-permute-start | bytes 7077896 | tf_op jit(solution)/shard_map/ppermute | solution.py:589
  374.3 31.2 %collective-permute-start.53 = (bf16[8,1,48,768]{3,2,0,1:T(8,128)(2,1)}, bf16[8,1,48,768]{3,2,0,1:T(8,128)(2,1)S(1)}, u32[]{:S(2)}, u32[]{:S(2)}) collective-permute-start(bf16[8,1,48,768]{3,2,0,1:T(8,128)(2,1)} %get-tuple-element.433), channel_id=1, source_target_pairs={{0,2},{1,3},{2,0},{3,1},{4,6},{5,7},{6,4},{7,5},{8,10},{9,11},{10,... | collective-permute-start | bytes 1769480 | tf_op jit(solution)/shard_map/ppermute | solution.py:589
  375.4 30.1 %collective-permute-start.54 = (bf16[8,1,48,768]{3,2,0,1:T(8,128)(2,1)}, bf16[8,1,48,768]{3,2,0,1:T(8,128)(2,1)S(1)}, u32[]{:S(2)}, u32[]{:S(2)}) collective-permute-start(bf16[8,1,48,768]{3,2,0,1:T(8,128)(2,1)} %get-tuple-element.432), channel_id=1, source_target_pairs={{0,4},{1,5},{2,6},{3,7},{4,0},{5,1},{6,2},{7,3},{8,12},{9,13},{10,... | collective-permute-start | bytes 1769480 | tf_op jit(solution)/shard_map/ppermute | solution.py:589
  379.0 26.5 %collective-permute-start.52 = (bf16[4,1,48,768]{3,2,1,0:T(8,128)(2,1)}, bf16[4,1,48,768]{3,2,1,0:T(8,128)(2,1)S(1)}, u32[]{:S(2)}, u32[]{:S(2)}) collective-permute-start(bf16[4,1,48,768]{3,2,1,0:T(8,128)(2,1)} %fusion.16), channel_id=1, source_target_pairs={{0,2},{1,3},{2,0},{3,1},{4,6},{5,7},{6,4},{7,5},{8,10},{9,11},{10,... | collective-permute-start | bytes 884744 | tf_op jit(solution)/shard_map/ppermute | solution.py:589
  407.6 34.8 %collective-permute-start.60 = (bf16[8,1,48,768]{3,2,1,0:T(8,128)(2,1)}, bf16[8,1,48,768]{3,2,1,0:T(8,128)(2,1)}, u32[]{:S(2)}, u32[]{:S(2)}) collective-permute-start(bf16[8,1,48,768]{3,2,1,0:T(8,128)(2,1)} %fusion.5), channel_id=1, source_target_pairs={{0,4},{1,5},{2,6},{3,7},{4,0},{5,1},{6,2},{7,3},{8,12},{9,13},{10,... | collective-permute-start | bytes 1769480 | tf_op jit(solution)/shard_map/ppermute | solution.py:589
  412.7 29.7 %collective-permute-start.59 = (bf16[8,1,48,768]{3,2,1,0:T(8,128)(2,1)}, bf16[8,1,48,768]{3,2,1,0:T(8,128)(2,1)}, u32[]{:S(2)}, u32[]{:S(2)}) collective-permute-start(bf16[8,1,48,768]{3,2,1,0:T(8,128)(2,1)} %fusion.4), channel_id=1, source_target_pairs={{0,2},{1,3},{2,0},{3,1},{4,6},{5,7},{6,4},{7,5},{8,10},{9,11},{10,... | collective-permute-start | bytes 1769480 | tf_op jit(solution)/shard_map/ppermute | solution.py:589
  415.0 24.7 %collective-permute-start.57 = (bf16[4,1,48,768]{3,2,0,1:T(8,128)(2,1)}, bf16[4,1,48,768]{3,2,0,1:T(8,128)(2,1)}, u32[]{:S(2)}, u32[]{:S(2)}) collective-permute-start(bf16[4,1,48,768]{3,2,0,1:T(8,128)(2,1)} %get-tuple-element.431), channel_id=1, source_target_pairs={{0,4},{1,5},{2,6},{3,7},{4,0},{5,1},{6,2},{7,3},{8,12},{9,13},{10,... | collective-permute-start | bytes 884744 | tf_op jit(solution)/shard_map/ppermute | solution.py:589
  417.0 25.4 %collective-permute-start.58 = (bf16[4,1,48,768]{3,2,0,1:T(8,128)(2,1)S(1)}, bf16[4,1,48,768]{3,2,0,1:T(8,128)(2,1)}, u32[]{:S(2)}, u32[]{:S(2)}) collective-permute-start(bf16[4,1,48,768]{3,2,0,1:T(8,128)(2,1)S(1)} %get-tuple-element.430), channel_id=1, source_target_pairs={{0,2},{1,3},{2,0},{3,1},{4,6},{5,7},{6,4},{7,5},{8,10},{9,11},{10,... | collective-permute-start | bytes 884744 | tf_op jit(solution)/shard_map/ppermute | solution.py:589
  442.4 25.2 %collective-permute-start.62 = (bf16[2,16,1,48,768]{4,3,2,1,0:T(8,128)(2,1)}, bf16[2,16,1,48,768]{4,3,2,1,0:T(8,128)(2,1)}, u32[]{:S(2)}, u32[]{:S(2)}) collective-permute-start(bf16[2,16,1,48,768]{4,3,2,1,0:T(8,128)(2,1)} %get-tuple-element.306), channel_id=1, source_target_pairs={{0,1},{1,0},{2,3},{3,2},{4,5},{5,4},{6,7},{7,6},{8,9},{9,8},{10,11... | collective-permute-start | bytes 7077896 | tf_op jit(solution)/shard_map/ppermute | solution.py:589
  (118 other events, 1393.7 us)
Sparse Core Ops, SparseCore 0:
  320.1 154.5 reduce-scatter.1

commit v2 on v1

v2 whole, which is shorter than its diff:
```python
import math
from functools import partial

import jax
import jax.numpy as jnp
from jax import lax
from jax.experimental import pallas as pl
from jax.experimental.pallas import tpu as pltpu
from jax.sharding import PartitionSpec as P

HEAD_DIM = 64
EPSILON = 1e-06
AXES = ("wide", "narrow")
F32 = jnp.float32
BF16 = jnp.bfloat16
ANY = pl.BlockSpec(memory_space=pl.ANY)
VMEM = pl.BlockSpec(memory_space=pltpu.VMEM)
SMEM = pl.BlockSpec(memory_space=pltpu.SMEM)
LIMIT = 60 * 2**20
SHARE = 48


def mm(left, right, over=(1, 0)):
    return lax.dot_general(
        left, right, (((over[0],), (over[1],)), ((), ())), preferred_element_type=F32
    )


def nt(left, right):
    return mm(left, right, (1, 1))


def tn(left, right):
    return mm(left, right, (0, 0))


def norm_rows(h):
    centred = h - jnp.mean(h, axis=-1, keepdims=True)
    inv = lax.rsqrt(jnp.mean(centred * centred, axis=-1, keepdims=True) + EPSILON)
    return centred * inv, inv


def norm_rows_back(g, n, inv, gain):
    t = g * gain
    return inv * (
        t
        - jnp.mean(t, axis=-1, keepdims=True)
        - n * jnp.mean(t * n, axis=-1, keepdims=True)
    )


def gelu_pair(f):
    u = jnp.abs(f)
    t = 1.0 / (1.0 + (0.3275911 / math.sqrt(2.0)) * u)
    e = jnp.exp(-0.5 * f * f)
    c = [0.5 * v for v in (0.254829592, -0.284496736, 1.421413741, -1.453152027, 1.061405429)]
    tail = e * (t * (c[0] + t * (c[1] + t * (c[2] + t * (c[3] + t * c[4])))))
    phi = jnp.where(f >= 0, 1.0 - tail, tail)
    return f * phi, phi + f * (e * (1.0 / math.sqrt(2.0 * math.pi)))


def even_lanes():
    return lax.broadcasted_iota(jnp.int32, (1, 2 * HEAD_DIM), 1) < HEAD_DIM


def place_of(idx, block, far, first_is_x):
    k, other = block % 4, block // 4
    z = idx[0] ^ (3 * (k % 2)) ^ (k // 2)
    if first_is_x:
        x, y = idx[1] ^ other, idx[2] ^ far
    else:
        x, y = idx[1] ^ far, idx[2] ^ other
    return z * 4 + x * 2 + y


def relative_of(idx, chip, first_is_x):
    r = (chip // 4) ^ idx[0]
    k = (r // 2) + 2 * ((r ^ (r // 2)) % 2)
    i = (chip // 2 % 2) ^ idx[1]
    j = (chip % 2) ^ idx[2]
    return (i * 8 + j * 4 + k) if first_is_x else (j * 8 + i * 4 + k)


def copy(src, dst, sem):
    return pltpu.make_async_copy(src, dst, sem)


def halves_of(ref):
    length = ref.shape[0] // 2
    return [slice(n * length, (n + 1) * length) for n in range(2)]


def add_small(ref, row, value):
    ref[row : row + 1] += jnp.sum(value.astype(F32), axis=0, keepdims=True)


def load_halves(src, dst, sems, at):
    loads = [copy(src.at[rows], dst.at[rows], sems.at[at + n]) for n, rows in enumerate(halves_of(src))]
    for load in loads:
        load.start()
    return loads


def rows_of(chip):
    return pl.ds(pl.multiple_of(chip * SHARE, SHARE), SHARE)


def fetch_attn(idx, given, w, sem, cores=(None, None)):
    if len(given) == 1:

        def whole(chip, carry):
            for s in range(2):
                for core in (0, 1) if cores[s] is None else (cores[s],):
                    square = 2 * s + core
                    copy(given[0].at[2 * chip + core, 0, s], w.at[square, rows_of(chip)], sem.at[square]).start()
            return carry

        lax.fori_loop(0, 16, whole, 0)
        return

    def go(block, carry):
        for s in range(2):
            if cores[s] == -1:
                continue
            for side in range(2):
                core = idx[3] ^ side

                def start(s=s, side=side, core=core):
                    for far in range(2):
                        rows = rows_of(place_of(idx, block, far, s == 0))
                        copy(given[4 * s + 2 * side + far].at[block, 0], w.at[2 * s + core, rows], sem.at[2 * s + core]).start()

                if cores[s] is None:
                    start()
                else:
                    pl.when(core == cores[s])(start)
        return carry

    lax.fori_loop(0, 8, go, 0)


def wait_square(w, sem, square):
    copy(w.at[square], w.at[square], sem.at[square]).wait()


def fetch_ffn(idx, given, m, w, sem):
    def place(chip, core, s):
        if m == 0:
            return w.at[2 * core + s, rows_of(chip)]
        return w.at[pl.ds(pl.multiple_of((chip * 4 + core * 2 + s) * SHARE, SHARE), SHARE)]

    def whole(chip, carry):
        for s in range(2):
            for core in range(2):
                copy(given[0].at[2 * chip + core, 1 + m, s], place(chip, core, s), sem.at[2 * core + s]).start()
        return carry

    def go(block, carry):
        for s in range(2):
            for side in range(2):
                core = idx[3] ^ side
                for far in range(2):
                    chip = place_of(idx, block, far, s == 0)
                    copy(given[4 * s + 2 * side + far].at[block, m], place(chip, core, s), sem.at[2 * core + s]).start()
        return carry

    if len(given) == 1:
        lax.fori_loop(0, 16, whole, 0)
    else:
        lax.fori_loop(0, 8, go, 0)


def wait_rows(w, sem):
    quarter = w.shape[0] // 4
    for i in range(4):
        copy(w.at[pl.ds(0, quarter)], w.at[pl.ds(0, quarter)], sem.at[i]).wait()


def call(kernel, name, operands, out_shape, scratch, flops, sems, aliases=None):
    return pl.pallas_call(
        kernel,
        in_specs=[SMEM] + [ANY] * (len(operands) - 1),
        out_specs=[ANY] * len(out_shape),
        out_shape=out_shape,
        scratch_shapes=scratch + [pltpu.SemaphoreType.DMA((n,)) for n in sems],
        input_output_aliases=aliases or {},
        compiler_params=pltpu.CompilerParams(vmem_limit_bytes=LIMIT),
        cost_estimate=pl.CostEstimate(flops=flops, bytes_accessed=30 * 2**20, transcendentals=0),
        name=name,
    )(*operands)


def shape(*dims, dtype=F32):
    return jax.ShapeDtypeStruct(dims, dtype)


def attn_forward_kernel(idx, x_ref, vec_ref, *refs):
    given, refs = refs[:-20], refs[-20:]
    y1_ref, r1_ref, qkv_ref, p_ref, att_ref = refs[:5]
    x, vec, w, qkv, p, att, y1, r1, sem_x, sem_vec, sem_w, sem_y, sem_r, sem_q, sem_p = refs[5:]
    loads = load_halves(x_ref, x, sem_x, 0)
    load_vec = copy(vec_ref, vec, sem_vec.at[0])
    load_vec.start()
    fetch_attn(idx, given, w, sem_w)
    load_vec.wait()
    halves = halves_of(x)
    length = halves[0].stop
    for n, rows in enumerate(halves):
        loads[n].wait()
        xr = x[rows].astype(BF16)
        for i in range(3):
            if n == 0:
                wait_square(w, sem_w, i)
            joined = mm(xr, w[i])
            if i != 1:
                joined = joined + vec[i // 2 : i // 2 + 1]
            qkv[i, rows] = joined.astype(BF16)
    save_qkv = copy(qkv, qkv_ref, sem_q.at[0])
    save_qkv.start()
    pairs = x.shape[1] // (2 * HEAD_DIM)
    places = lax.broadcasted_iota(jnp.int32, (1, length), 1)
    even = even_lanes()

    def pair(step, carry):
        n, j = step // pairs, step % pairs
        rows = pl.ds(pl.multiple_of(n * length, length), length)
        lanes = pl.ds(pl.multiple_of(j * 2 * HEAD_DIM, 2 * HEAD_DIM), 2 * HEAD_DIM)
        hidden = jnp.where(places < idx[4 + n], 0.0, -1e30)
        q2 = qkv[0, rows, lanes] * jnp.asarray(HEAD_DIM**-0.5, BF16)
        k2 = qkv[1, rows, lanes]
        v2 = qkv[2, rows, lanes]
        parts = []
        for h in range(2):
            mine = even if h == 0 else jnp.logical_not(even)
            s = nt(jnp.where(mine, q2, jnp.zeros_like(q2)), k2) + hidden
            e = jnp.exp(s - jnp.max(s, axis=-1, keepdims=True))
            soft = (e * (1.0 / jnp.sum(e, axis=-1, keepdims=True))).astype(BF16)
            p[2 * step + h] = soft
            parts.append(mm(soft, v2))
        att[rows, lanes] = jnp.where(even, parts[0], parts[1]).astype(BF16)
        copy(p.at[pl.ds(2 * step, 2)], p_ref.at[pl.ds(2 * step, 2)], sem_p.at[0]).start()
        return carry

    lax.fori_loop(0, 2 * pairs, pair, 0)
    save_att = copy(att, att_ref, sem_q.at[1])
    save_att.start()
    wait_square(w, sem_w, 3)
    saves = [save_qkv, save_att]
    for n, rows in enumerate(halves):
        h = x[rows].astype(F32) + (mm(att[rows], w[3]) + vec[2:3])
        normed, inv = norm_rows(h)
        y1[rows] = normed * vec[3:4] + vec[4:5]
        r1[rows] = inv
        saves += [copy(y1.at[rows], y1_ref.at[rows], sem_y.at[n]), copy(r1.at[rows], r1_ref.at[rows], sem_r.at[n])]
        saves[-2].start()
        saves[-1].start()
    for save in saves:
        save.wait()
    copy(p, p_ref, sem_p.at[0]).wait()


def attn_forward(idx, x, vec, pieces):
    t, d = x.shape
    heads = d // HEAD_DIM
    length = t // 2
    return call(
        attn_forward_kernel,
        "attn_forward",
        (idx, x, vec) + tuple(pieces),
        [shape(t, d), shape(t, 1), shape(3, t, d, dtype=BF16), shape(2 * heads, length, length, dtype=BF16), shape(t, d, dtype=BF16)],
        [
            pltpu.VMEM((t, d), x.dtype),
            pltpu.VMEM(vec.shape, F32),
            pltpu.VMEM((4, d, d), BF16),
            pltpu.VMEM((3, t, d), BF16),
            pltpu.VMEM((2 * heads, length, length), BF16),
            pltpu.VMEM((t, d), BF16),
            pltpu.VMEM((t, d), F32),
            pltpu.VMEM((t, 1), F32),
        ],
        8 * t * d * d + 4 * t * length * d,
        (2, 1, 4, 2, 2, 2, 1),
    )


def ffn_forward_kernel(idx, y1_ref, vec_ref, *refs):
    given, refs = refs[:-22], refs[-22:]
    x_ref, r2_ref, ur_ref, gp_ref = refs[:4]
    y1, vec, we, wc, ur, gp, acc, x, r2, sem_y, sem_vec, sem_e, sem_c, sem_x, sem_r, sem_u, sem_g, sem_z = refs[4:]
    del sem_z
    loads = load_halves(y1_ref, y1, sem_y, 0)
    load_vec = copy(vec_ref, vec, sem_vec.at[0])
    load_vec.start()
    fetch_ffn(idx, given, 0, we, sem_e)
    fetch_ffn(idx, given, 1, wc, sem_c)
    load_vec.wait()
    d = y1.shape[1]
    halves = halves_of(y1)
    for j in range(4):
        cols = slice(j * d, (j + 1) * d)
        wait_square(we, sem_e, j)
        for n, rows in enumerate(halves):
            if j == 0:
                loads[n].wait()
            f = mm(y1[rows].astype(BF16), we[j]) + vec[5 + j : 6 + j]
            u, slope = gelu_pair(f)
            u = u.astype(BF16)
            ur[j, rows] = u
            gp[j, rows] = slope.astype(BF16)
            if j == 0 and n == 0:
                wait_rows(wc, sem_c)
            part = mm(u, wc[cols])
            if j == 0:
                acc[rows] = part
            else:
                acc[rows] += part
        copy(ur.at[j], ur_ref.at[j], sem_u.at[0]).start()
        copy(gp.at[j], gp_ref.at[j], sem_g.at[0]).start()
    saves = []
    for n, rows in enumerate(halves):
        normed, inv = norm_rows(y1[rows] + (acc[rows] + vec[9:10]))
        x[rows] = normed * vec[10:11] + vec[11:12]
        r2[rows] = inv
        saves += [copy(x.at[rows], x_ref.at[rows], sem_x.at[n]), copy(r2.at[rows], r2_ref.at[rows], sem_r.at[n])]
        saves[-2].start()
        saves[-1].start()
    for save in saves:
        save.wait()
    copy(ur, ur_ref, sem_u.at[0]).wait()
    copy(gp, gp_ref, sem_g.at[0]).wait()


def ffn_forward(idx, y1, vec, pieces):
    t, d = y1.shape
    return call(
        ffn_forward_kernel,
        "ffn_forward",
        (idx, y1, vec) + tuple(pieces),
        [shape(t, d), shape(t, 1), shape(4, t, d, dtype=BF16), shape(4, t, d, dtype=BF16)],
        [
            pltpu.VMEM((t, d), F32),
            pltpu.VMEM(vec.shape, F32),
            pltpu.VMEM((4, d, d), BF16),
            pltpu.VMEM((4 * d, d), BF16),
            pltpu.VMEM((4, t, d), BF16),
            pltpu.VMEM((4, t, d), BF16),
            pltpu.VMEM((t, d), F32),
            pltpu.VMEM((t, d), F32),
            pltpu.VMEM((t, 1), F32),
        ],
        16 * t * d * d,
        (2, 1, 4, 4, 2, 2, 1, 1, 1),
    )


def send_rows(idx, block, chip, core, s, m, sums, sem):
    if len(sums) == 1:
        copy(block, sums[0].at[2 * chip + core, s, m], sem).start()
        return
    keep, give = sums
    to = jnp.where(s == 1, relative_of(idx, chip, True), relative_of(idx, chip, False))

    @pl.when(core == idx[3])
    def _():
        copy(block, keep.at[s, to, m], sem).start()

    @pl.when(core != idx[3])
    def _():
        copy(block, give.at[s, to, m], sem).start()


def send_square(idx, stage, core, s, m, sums, sem):
    def go(chip, carry):
        send_rows(idx, stage.at[rows_of(chip)], chip, core, s, m, sums, sem)
        return carry

    lax.fori_loop(0, 16, go, 0)


def sums_shapes(d, whole, m=1):
    if whole:
        return [shape(32, 2, m, SHARE, d, dtype=BF16)]
    return [shape(2, 16, m, SHARE, d, dtype=BF16)] * 2


def ffn_backward_kernel(count, idx, g_ref, x_ref, r2_ref, y1_ref, r1_ref, vec_ref, ur_ref, gp_ref, *refs):
    given, refs = refs[: -(30 + count)], refs[-(30 + count) :]
    attn, given = (given[:1], given[:1]) if len(given) < 16 else (given[8:16], given[:8])
    dh1_ref, small_ref, da_ref = refs[:3]
    sums, refs = refs[3 : 3 + count], refs[3 + count :]
    g, x, r2, y1, r1, vec, we, wc, w, ur, gp, acc, e2, y1r, stage, da, small = refs[:17]
    sem_g, sem_x, sem_y, sem_r, sem_e, sem_c, sem_w, sem_u, sem_d, sem_a = refs[17:]
    d = y1.shape[1]
    halves = halves_of(y1)
    load_vec = copy(vec_ref, vec, sem_r.at[4])
    load_vec.start()
    loads = list(zip(load_halves(g_ref, g, sem_g, 0), load_halves(x_ref, x, sem_x, 0), load_halves(r2_ref, r2, sem_r, 0)))
    load_u = [copy(ur_ref.at[j], ur.at[j], sem_u.at[j]) for j in range(4)]
    load_g = [copy(gp_ref.at[j], gp.at[j], sem_u.at[4 + j]) for j in range(4)]
    load_u[0].start()
    fetch_ffn(idx, given, 1, wc, sem_c)
    load_g[0].start()
    load_y = load_halves(y1_ref, y1, sem_y, 0)
    load_r = load_halves(r1_ref, r1, sem_r, 2)
    fetch_ffn(idx, given, 0, we, sem_e)
    for j in range(1, 4):
        load_u[j].start()
        load_g[j].start()
    fetch_attn(idx, attn, w, sem_w, (-1, 1))
    small[...] = jnp.zeros_like(small)
    load_vec.wait()
    inv_gain = 1.0 / vec[10:11]
    for n, rows in enumerate(halves):
        for load in loads[n]:
            load.wait()
        grad = g[rows].astype(F32)
        normed = (x[rows] - vec[11:12]) * inv_gain
        add_small(small, 8, grad * normed)
        add_small(small, 9, grad)
        back = norm_rows_back(grad, normed, r2[rows], vec[10:11])
        low = back.astype(BF16)
        add_small(small, 7, low)
        acc[rows] = back
        e2[rows] = low
    for j in range(4):
        cols = slice(j * d, (j + 1) * d)
        load_u[j].wait()
        stage[4 + j] = tn(ur[j], e2[...]).astype(BF16)

        def go(b, carry):
            send_rows(idx, stage.at[4 + j, rows_of(b)], 4 * j + b // 4, b // 2 % 2, b % 2, 1, sums, sem_a.at[0])
            return carry

        lax.fori_loop(0, 16, go, 0)
        if j == 0:
            wait_rows(wc, sem_c)
            for n, rows in enumerate(halves):
                load_y[n].wait()
                y1r[rows] = y1[rows].astype(BF16)
        load_g[j].wait()
        for rows in halves:
            ef = (nt(e2[rows], wc[cols]) * gp[j, rows].astype(F32)).astype(BF16)
            gp[j, rows] = ef
            add_small(small, 3 + j, ef)
        stage[j] = tn(y1r[...], gp[j]).astype(BF16)
        send_square(idx, stage.at[j], j // 2, j % 2, 0, sums, sem_a.at[1])
        wait_square(we, sem_e, j)
        for rows in halves:
            acc[rows] += nt(gp[j, rows], we[j])
    wait_square(w, sem_w, 3)
    inv_gain = 1.0 / vec[3:4]
    saves = []
    for n, rows in enumerate(halves):
        load_r[n].wait()
        grad, normed = acc[rows], (y1[rows] - vec[4:5]) * inv_gain
        add_small(small, 1, grad * normed)
        add_small(small, 2, grad)
        back = norm_rows_back(grad, normed, r1[rows], vec[3:4])
        x[rows] = back
        low = back.astype(BF16)
        add_small(small, 0, low)
        da[rows] = nt(low, w[3]).astype(BF16)
        saves += [copy(x.at[rows], dh1_ref.at[rows], sem_d.at[n]), copy(da.at[rows], da_ref.at[rows], sem_d.at[2 + n])]
        saves[-2].start()
        saves[-1].start()
    saves.append(copy(small, small_ref, sem_d.at[4]))
    saves[-1].start()
    for save in saves:
        save.wait()
    copy(stage.at[4:8], stage.at[4:8], sem_a.at[0]).wait()
    copy(stage.at[0:4], stage.at[0:4], sem_a.at[1]).wait()


def ffn_backward(whole, idx, g, x, r2, y1, r1, vec, ur, gp, ffn_pieces, attn_pieces):
    t, d = x.shape
    sums = sums_shapes(d, whole, 2)
    pieces = tuple(ffn_pieces) + tuple(attn_pieces) if len(ffn_pieces) == 8 else tuple(ffn_pieces)
    return call(
        partial(ffn_backward_kernel, len(sums)),
        "ffn_backward",
        (idx, g, x, r2, y1, r1, vec, ur, gp) + pieces,
        [shape(t, d), shape(16, d), shape(t, d, dtype=BF16)] + sums,
        [
            pltpu.VMEM((t, d), g.dtype),
            pltpu.VMEM((t, d), F32),
            pltpu.VMEM((t, 1), F32),
            pltpu.VMEM((t, d), F32),
            pltpu.VMEM((t, 1), F32),
            pltpu.VMEM(vec.shape, F32),
            pltpu.VMEM((4, d, d), BF16),
            pltpu.VMEM((4 * d, d), BF16),
            pltpu.VMEM((4, d, d), BF16),
            pltpu.VMEM((4, t, d), BF16),
            pltpu.VMEM((4, t, d), BF16),
            pltpu.VMEM((t, d), F32),
            pltpu.VMEM((t, d), BF16),
            pltpu.VMEM((t, d), BF16),
            pltpu.VMEM((8, d, d), BF16),
            pltpu.VMEM((t, d), BF16),
            pltpu.VMEM((16, d), F32),
        ],
        32 * t * d * d,
        (2, 2, 2, 5, 4, 4, 4, 8, 5, 2),
    )


def ffn_both_kernel(idx, y1_ref, r1_ref, g_ref, vec_ref, *refs):
    given, refs = refs[:-32], refs[-32:]
    attn, given = (given[:1], given[:1]) if len(given) < 16 else (given[8:16], given[:8])
    x_ref, dh1_ref, small_ref, da_ref, sums = refs[:5]
    y1, r1, g, vec, we, wc, w, ur, gp, acc, x, n2, e2, y1r, stage, da, small = refs[5:22]
    sem_y, sem_r, sem_g, sem_vec, sem_e, sem_c, sem_w, sem_x, sem_d, sem_a = refs[22:]
    d = y1.shape[1]
    halves = halves_of(y1)
    load_y = load_halves(y1_ref, y1, sem_y, 0)
    load_vec = copy(vec_ref, vec, sem_vec.at[0])
    load_vec.start()
    fetch_ffn(idx, given, 0, we, sem_e)
    fetch_ffn(idx, given, 1, wc, sem_c)
    load_g = load_halves(g_ref, g, sem_g, 0)
    load_r = load_halves(r1_ref, r1, sem_r, 0)
    fetch_attn(idx, attn, w, sem_w, (-1, 1))
    small[...] = jnp.zeros_like(small)
    load_vec.wait()
    for n, rows in enumerate(halves):
        load_y[n].wait()
        y1r[rows] = y1[rows].astype(BF16)
    for j in range(4):
        cols = slice(j * d, (j + 1) * d)
        wait_square(we, sem_e, j)
        for n, rows in enumerate(halves):
            u, slope = gelu_pair(mm(y1r[rows], we[j]) + vec[5 + j : 6 + j])
            u = u.astype(BF16)
            ur[j, rows] = u
            gp[j, rows] = slope.astype(BF16)
            if j == 0 and n == 0:
                wait_rows(wc, sem_c)
            part = mm(u, wc[cols])
            if j == 0:
                acc[rows] = part
            else:
                acc[rows] += part
    saves = []
    for n, rows in enumerate(halves):
        normed, inv = norm_rows(y1[rows] + (acc[rows] + vec[9:10]))
        x[rows] = normed * vec[10:11] + vec[11:12]
        saves.append(copy(x.at[rows], x_ref.at[rows], sem_x.at[n]))
        saves[-1].start()
        load_g[n].wait()
        grad = g[rows].astype(F32)
        add_small(small, 8, grad * normed)
        add_small(small, 9, grad)
        back = norm_rows_back(grad, normed, inv, vec[10:11])
        low = back.astype(BF16)
        add_small(small, 7, low)
        acc[rows] = back
        e2[rows] = low
    for j in range(4):
        cols = slice(j * d, (j + 1) * d)
        stage[4 + j] = tn(ur[j], e2[...]).astype(BF16)

        def go(b, carry):
            send_rows(idx, stage.at[4 + j, rows_of(b)], 4 * j + b // 4, b // 2 % 2, b % 2, 1, (sums,), sem_a.at[0])
            return carry

        lax.fori_loop(0, 16, go, 0)
        for rows in halves:
            ef = (nt(e2[rows], wc[cols]) * gp[j, rows].astype(F32)).astype(BF16)
            gp[j, rows] = ef
            add_small(small, 3 + j, ef)
        stage[j] = tn(y1r[...], gp[j]).astype(BF16)
        send_square(idx, stage.at[j], j // 2, j % 2, 0, (sums,), sem_a.at[1])
        for rows in halves:
            acc[rows] += nt(gp[j, rows], we[j])
    wait_square(w, sem_w, 3)
    inv_gain = 1.0 / vec[3:4]
    for n, rows in enumerate(halves):
        load_r[n].wait()
        grad, normed = acc[rows], (y1[rows] - vec[4:5]) * inv_gain
        add_small(small, 1, grad * normed)
        add_small(small, 2, grad)
        back = norm_rows_back(grad, normed, r1[rows], vec[3:4])
        n2[rows] = back
        low = back.astype(BF16)
        add_small(small, 0, low)
        da[rows] = nt(low, w[3]).astype(BF16)
        saves += [copy(n2.at[rows], dh1_ref.at[rows], sem_d.at[n]), copy(da.at[rows], da_ref.at[rows], sem_d.at[2 + n])]
        saves[-2].start()
        saves[-1].start()
    saves.append(copy(small, small_ref, sem_d.at[4]))
    saves[-1].start()
    for save in saves:
        save.wait()
    copy(stage.at[4:8], stage.at[4:8], sem_a.at[0]).wait()
    copy(stage.at[0:4], stage.at[0:4], sem_a.at[1]).wait()


def ffn_both(idx, y1, r1, g, vec, ffn_pieces, attn_pieces):
    t, d = y1.shape
    pieces = tuple(ffn_pieces) + tuple(attn_pieces) if len(ffn_pieces) == 8 else tuple(ffn_pieces)
    return call(
        ffn_both_kernel,
        "ffn_both",
        (idx, y1, r1, g, vec) + pieces,
        [shape(t, d), shape(t, d), shape(16, d), shape(t, d, dtype=BF16)] + sums_shapes(d, True, 2),
        [
            pltpu.VMEM((t, d), F32),
            pltpu.VMEM((t, 1), F32),
            pltpu.VMEM((t, d), g.dtype),
            pltpu.VMEM(vec.shape, F32),
            pltpu.VMEM((4, d, d), BF16),
            pltpu.VMEM((4 * d, d), BF16),
            pltpu.VMEM((4, d, d), BF16),
            pltpu.VMEM((4, t, d), BF16),
            pltpu.VMEM((4, t, d), BF16),
            pltpu.VMEM((t, d), F32),
            pltpu.VMEM((t, d), F32),
            pltpu.VMEM((t, d), F32),
            pltpu.VMEM((t, d), BF16),
            pltpu.VMEM((t, d), BF16),
            pltpu.VMEM((8, d, d), BF16),
            pltpu.VMEM((t, d), BF16),
            pltpu.VMEM((16, d), F32),
        ],
        48 * t * d * d,
        (2, 2, 2, 1, 4, 4, 4, 2, 5, 2),
    )


def heads_backward_kernel(idx, da_ref, qkv_ref, p_ref, back_ref, small_ref, da, qkv, back, small, p, sem_in, sem_p, sem_out):
    t, d = da.shape
    length = t // 2
    pairs = d // (2 * HEAD_DIM)
    factor = HEAD_DIM**-0.5
    even = even_lanes()

    def load(step, slot):
        return copy(p_ref.at[pl.ds(2 * step, 2)], p.at[slot], sem_p.at[slot])

    load(0, 0).start()
    loads = load_halves(da_ref, da, sem_in, 0)
    for n, rows in enumerate(halves_of(da)):
        loads.append(copy(qkv_ref.at[:, rows], qkv.at[:, rows], sem_in.at[2 + n]))
        loads[-1].start()
    for n, rows in enumerate(halves_of(da)):
        loads[n].wait()
        loads[2 + n].wait()

        def pair(j, carry, n=n):
            step = n * pairs + j
            slot = step % 2

            @pl.when(step + 1 < 2 * pairs)
            def _():
                load(step + 1, 1 - slot).start()

            load(step, slot).wait()
            lanes = pl.ds(pl.multiple_of(j * 2 * HEAD_DIM, 2 * HEAD_DIM), 2 * HEAD_DIM)
            q2, k2, v2 = (qkv[i, n * length : (n + 1) * length, lanes] for i in range(3))
            da2 = da[n * length : (n + 1) * length, lanes]
            dqs, dks, dvs = [], [], []
            for h in range(2):
                mine = even if h == 0 else jnp.logical_not(even)
                soft = p[slot, h]
                dp = nt(jnp.where(mine, da2, jnp.zeros_like(da2)), v2)
                dvs.append(tn(soft, da2))
                soft = soft.astype(F32)
                inner = jnp.sum(soft * dp, axis=-1, keepdims=True)
                ds = (soft * (dp - inner)).astype(BF16)
                dqs.append(mm(ds, k2))
                dks.append(tn(ds, q2))
            dq, dk, dv = (jnp.where(even, m[0], m[1]) for m in (dqs, dks, dvs))
            back[0, n * length : (n + 1) * length, lanes] = (dq * factor).astype(BF16)
            back[1, n * length : (n + 1) * length, lanes] = (dk * factor).astype(BF16)
            back[2, n * length : (n + 1) * length, lanes] = dv.astype(BF16)
            return carry

        lax.fori_loop(0, pairs, pair, 0)
        copy(back.at[:, rows], back_ref.at[:, rows], sem_out.at[n]).start()
    small[0:1] = jnp.sum(back[0].astype(F32), axis=0, keepdims=True)
    small[1:2] = jnp.sum(back[2].astype(F32), axis=0, keepdims=True)
    save = copy(small, small_ref, sem_out.at[2])
    save.start()
    for n, rows in enumerate(halves_of(da)):
        copy(back.at[:, rows], back_ref.at[:, rows], sem_out.at[n]).wait()
    save.wait()


def heads_backward(idx, da, qkv, p):
    t, d = da.shape
    length = t // 2
    return call(
        heads_backward_kernel,
        "heads_backward",
        (idx, da, qkv, p),
        [shape(3, t, d, dtype=BF16), shape(8, d)],
        [
            pltpu.VMEM((t, d), BF16),
            pltpu.VMEM((3, t, d), BF16),
            pltpu.VMEM((3, t, d), BF16),
            pltpu.VMEM((8, d), F32),
            pltpu.VMEM((2, 2, length, length), BF16),
        ],
        30 * t * length * d,
        (4, 2, 3),
    )


def inward_backward_kernel(count, idx, dh1_ref, x_ref, att_ref, back_ref, *refs):
    given, refs = refs[: -(16 + count)], refs[-(16 + count) :]
    dx_ref = refs[0]
    sums, refs = refs[1 : 1 + count], refs[1 + count :]
    dh1, x, att, back, w, stage, dx, sem_d, sem_x, sem_a, sem_b, sem_w, sem_out, sem_s, _ = refs[:15]
    halves = halves_of(x)
    load_x = load_halves(x_ref, x, sem_x, 0)
    load_b = [copy(back_ref.at[i], back.at[i], sem_b.at[i]) for i in range(3)]
    for load in load_b:
        load.start()
    fetch_attn(idx, given, w, sem_w, (None, 0))
    load_d = load_halves(dh1_ref, dh1, sem_d, 0)
    load_a = copy(att_ref, att, sem_a.at[0])
    load_a.start()
    for load in load_x:
        load.wait()
    xr = x[...].astype(BF16)
    for i, (core, s) in enumerate(((0, 0), (1, 0), (0, 1))):
        load_b[i].wait()
        stage[i] = tn(xr, back[i]).astype(BF16)
        send_square(idx, stage.at[i], core, s, 0, sums, sem_s.at[0])
    for load in load_d:
        load.wait()
    load_a.wait()
    stage[3] = tn(att[...], dh1[...].astype(BF16)).astype(BF16)
    send_square(idx, stage.at[3], 1, 1, 0, sums, sem_s.at[0])
    for i in range(3):
        wait_square(w, sem_w, i)
    saves = []
    for n, rows in enumerate(halves):
        dx[rows] = dh1[rows] + (nt(back[0, rows], w[0]) + nt(back[1, rows], w[1]) + nt(back[2, rows], w[2]))
        saves.append(copy(dx.at[rows], dx_ref.at[rows], sem_out.at[n]))
        saves[-1].start()
    for save in saves:
        save.wait()
    copy(stage, stage, sem_s.at[0]).wait()


def inward_backward(whole, idx, dh1, x, att, back, pieces):
    t, d = dh1.shape
    sums = sums_shapes(d, whole)
    return call(
        partial(inward_backward_kernel, len(sums)),
        "inward_backward",
        (idx, dh1, x, att, back) + tuple(pieces),
        [shape(t, d)] + sums,
        [
            pltpu.VMEM((t, d), F32),
            pltpu.VMEM((t, d), x.dtype),
            pltpu.VMEM((t, d), BF16),
            pltpu.VMEM((3, t, d), BF16),
            pltpu.VMEM((4, d, d), BF16),
            pltpu.VMEM((4, d, d), BF16),
            pltpu.VMEM((t, d), F32),
        ],
        14 * t * d * d,
        (2, 2, 1, 3, 4, 2, 1, 1),
    )


BITS = {"c": 1, "y": 2, "x": 4, "z1": 8, "z2": 16, "z3": 24}


def swap(array, by):
    return lax.ppermute(array, AXES, [(i, i ^ BITS[by]) for i in range(32)])


def tie(values, *others):
    return lax.optimization_barrier((values, others))[0]


def pair_up(share):
    return jnp.stack([share, swap(share, "z3")])


def column_up(pair):
    return jnp.concatenate([pair, swap(pair, "z1")])


def near_up(cols):
    return tuple(jnp.concatenate([col, swap(col, by)]) for col, by in zip(cols, "xy"))


def far_up(near):
    return tuple(swap(piece, by) for piece, by in zip(near, "yx"))


def other_core(pieces):
    return tuple(swap(piece, "c") for piece in pieces)


def in_order(near, far, near_c, far_c):
    return sum(((near[s], far[s], near_c[s], far_c[s]) for s in range(2)), ())


def place_small(qb, vb, ob, ag, ash, eb, cb, fg, fs, width, device):
    layers, rows = qb.shape
    lanes = lax.broadcasted_iota(jnp.int32, (1, 1, width), 2)
    thin = jnp.stack([qb, vb, ob, ag, ash, cb, fg, fs], axis=1).astype(F32)
    thin = jnp.where(lanes // rows == device, jnp.tile(thin, (1, 1, width // rows)), 0.0)
    lines = lax.broadcasted_iota(jnp.int32, (1, 4, width), 1)
    wide = jnp.tile(eb.astype(F32)[:, None], (1, 4, width // eb.shape[1]))
    wide = jnp.where(lines * (width // eb.shape[1]) + lanes // eb.shape[1] == device, wide, 0.0)
    return jnp.concatenate([thin[:, 0:5], wide, thin[:, 5:8], jnp.zeros((layers, 4, width), F32)], axis=1)


def own_small(total, rows, device):
    layers, _, width = total.shape
    thin = lax.dynamic_slice_in_dim(total, device * rows, rows, 2)
    count = width // (4 * rows)
    wide = lax.dynamic_slice(total, (0, 5 + device // count, device % count * 4 * rows), (layers, 1, 4 * rows))
    return [thin[:, i] for i in range(5)] + [wide[:, 0]] + [thin[:, i] for i in range(9, 12)]


def add_swap(array, by):
    return array + swap(array, by)


class Sums:
    def __init__(self, keep, give):
        self.both = [keep]
        self.parts = [[], []]
        self.give = give

    def total(self, s, lo, hi):
        whole = None
        for a in [b[s] for b in self.both] + self.parts[s]:
            a = a[lo:hi].astype(F32)
            whole = a if whole is None else whole + a
        return whole

    def latest(self):
        return self.parts if self.parts[0] else self.both

    def hold(self, *others):
        if self.parts[0]:
            self.parts = tie(self.parts, *others)
        else:
            self.both = tie(self.both, *others)

    def core(self):
        self.both = self.both + [swap(self.give, "c")]

    def plane(self, lo, bys):
        arrived = [swap(self.total(s, lo, 2 * lo).astype(BF16), bys[s]) for s in range(2)]
        for s in range(2):
            self.parts[s] = self.parts[s] + [arrived[s]]

    def first(self):
        self.plane(8, "yx")

    def second(self):
        self.plane(4, "xy")

    def line(self, lo, by):
        arrived = swap(jnp.stack([self.total(s, lo, 2 * lo) for s in range(2)]).astype(BF16), by)
        for s in range(2):
            self.parts[s] = self.parts[s] + [arrived[s]]

    def third(self):
        self.line(2, "z1")

    def fourth(self):
        self.line(1, "z3")

    def result(self):
        return jnp.stack([self.total(s, 0, 1)[0] for s in range(2)])


def front(first, last, rows, width, c, attention):
    layers = first.shape[0]
    first = first.reshape(layers, rows, -1)
    cut = lambda i: first[:, :, i * width : (i + 1) * width]
    if attention:
        zero, one = (cut(0), cut(2)), (cut(1), last.reshape(layers, rows, width))
    else:
        zero, one = (cut(0), cut(1)), (cut(2), cut(3))
    zero, one = jnp.stack(zero, 1), jnp.stack(one, 1)
    return jnp.where(c == 0, zero, one), jnp.where(c == 0, one, zero)


def both_cores(mine, got, c):
    return jnp.where(c == 0, jnp.concatenate([mine, got], 2), jnp.concatenate([got, mine], 2))


def gather_any(w_inward, w_outward, w_expand, w_contract, width):
    whole = lambda m, n: lax.all_gather(m, AXES, axis=0, tiled=True).reshape(-1, n)
    inward, outward = whole(w_inward, 3 * width), whole(w_outward, width)
    expand, contract = whole(w_expand, 4 * width), whole(w_contract, width)
    cut = lambda m, i: m[:, i * width : (i + 1) * width].reshape(16, SHARE, width)
    squares = [cut(inward, i) for i in range(3)] + [cut(outward, 0)] + [cut(expand, i) for i in range(4)]
    down = contract.reshape(16, 2, 2, SHARE, width)
    sides = []
    for core in range(2):
        pick = (core, 2 + core, 4 + 2 * core, 5 + 2 * core)
        pairs = [squares[i] for i in pick] + [down[:, core, s] for s in range(2)]
        sides.append(jnp.stack(pairs, 1).reshape(16, 3, 2, SHARE, width))
    return jnp.stack(sides, 1).reshape(32, 3, 2, SHARE, width)


def collect_any(attn, ffn, width):
    attn = attn.reshape(16, 2, 2, SHARE, width)
    ffn = ffn.reshape(16, 2, 2, 2, SHARE, width)
    expand, contract = ffn[:, :, :, 0], ffn[:, :, :, 1]
    inward = jnp.concatenate([attn[:, 0, 0], attn[:, 1, 0], attn[:, 0, 1]], axis=-1)
    expand = jnp.concatenate([expand[:, core, s] for core in range(2) for s in range(2)], axis=-1)
    return tuple(
        lax.psum_scatter(m.reshape(-1).astype(F32), AXES, scatter_dimension=0, tiled=True)
        for m in (inward, attn[:, 1, 1], expand, contract)
    )


def local(blocked, tokens, lengths, w_inward, qb, vb, w_outward, ob, ag, ash, w_expand, eb, w_contract, cb, fg, fs, cotangent):
    layers = w_inward.shape[0]
    width = tokens.shape[-1]
    rows = qb.shape[1]
    device = lax.axis_index("wide") * lax.axis_size("narrow") + lax.axis_index("narrow")
    me = device if blocked else jnp.int32(0)
    c = me & 1
    place = jnp.stack([me >> 3, (me >> 2) & 1, (me >> 1) & 1, c]).astype(jnp.int32)
    idx = jnp.concatenate([place, lengths.reshape(-1), jnp.zeros((2,), jnp.int32)])
    small = place_small(qb, vb, ob, ag, ash, eb, cb, fg, fs, width, device)
    x = tokens.reshape(-1, width)
    kept = []

    def keep_layer(x, y1, attn, ffn, attn_pieces, ffn_pieces):
        kept.append((x, y1) + tuple(attn[1:]) + tuple(ffn) + (attn_pieces, ffn_pieces))
        return ffn[0]

    if blocked:
        mine, got = front(w_inward, w_outward, rows, width, c, True)
        halves = lambda col: (col[:, 0, None], col[:, 1, None])
        halves2 = lambda col: (col[:, :, 0], col[:, :, 1])
        share_a = both_cores(mine, swap(got, "c"), c)
        small = add_swap(small, "c")
        mine, got = front(w_expand, None, rows, width, c, False)
        share_e = both_cores(mine, swap(got, "c"), c)
        contract = w_contract.reshape(layers, 2, SHARE, width)
        share_f = [jnp.stack([share_e[l], contract[l]]) for l in range(layers)]
        a_pair = pair_up(share_a[0])
        share, a_pair, small = tie((share_f[0], a_pair, small))
        f_pair = pair_up(share)
        a_col = column_up(a_pair)
        small = add_swap(small, "z1")
        f_pair, a_col, small = tie((f_pair, a_col, small))
        f_col = column_up(f_pair)
        a_near = near_up(halves(a_col))
        small = add_swap(small, "z2")
        a_near, small = tie((a_near, small))
        a_far = far_up(a_near)
        a_core = other_core(a_near)
        f_col, a_far, small = tie((f_col, a_far, small))
        f_near = near_up(halves2(f_col))
        small = add_swap(small, "x")
        a1_pair = pair_up(tie((share_a[1], a_far))[0])
        a_core += other_core(a_far)
        x, f_near, a1_pair, small = tie((x, f_near, a1_pair, small))
        f_far = far_up(f_near)
        small = add_swap(small, "y")
        a1_col = column_up(a1_pair)
        f_core = other_core(f_near)
        vecs = [small[l] for l in range(layers)]
        a_pieces = in_order(a_near, a_far, a_core[:2], a_core[2:])
        attn = attn_forward(idx, x, vecs[0], a_pieces)
        f_far, a1_col, f_core, y1, share = tie((f_far, a1_col, f_core, attn[0], share_f[1]))
        f_core += other_core(f_far)
        a1_near = near_up(halves(a1_col))
        f1_pair = pair_up(share)
        y1, a1_near, f1_pair = tie((y1, a1_near, f1_pair))
        a1_far = far_up(a1_near)
        f1_col = column_up(f1_pair)
        f_pieces = in_order(f_near, f_far, f_core[:2], f_core[2:])
        ffn = ffn_forward(idx, y1, vecs[0], f_pieces)
        x1 = keep_layer(x, y1, attn, ffn, a_pieces, f_pieces)
        a1_far, f1_col, x1 = tie((a1_far, f1_col, x1))
        a1_core = other_core(a1_near + a1_far)
        f1_near = near_up(halves2(f1_col))
        x1, f1_near = tie((x1, f1_near))
        f1_far = far_up(f1_near)
        f1_core = other_core(f1_near)
        a1_pieces = in_order(a1_near, a1_far, a1_core[:2], a1_core[2:])
        attn = attn_forward(idx, x1, vecs[1], a1_pieces)
        f1_far, f1_core, y1 = tie((f1_far, f1_core, attn[0]))
        f1_core += other_core(f1_far)
        f1_pieces = in_order(f1_near, f1_far, f1_core[:2], f1_core[2:])
        output, dh1, small, da, whole = ffn_both(idx, y1, attn[1], cotangent.reshape(-1, width), vecs[1], f1_pieces, a1_pieces)
        keep_layer(x1, y1, attn, (output, None, None, None), a1_pieces, f1_pieces)
    else:
        small = lax.psum(small, AXES)
        vecs = [small[l] for l in range(layers)]
        for l in range(layers):
            pieces = (gather_any(w_inward[l], w_outward[l], w_expand[l], w_contract[l], width),)
            attn = attn_forward(idx, x, vecs[l], pieces)
            if l + 1 < layers:
                x = keep_layer(x, attn[0], attn, ffn_forward(idx, attn[0], vecs[l], pieces), pieces, pieces)
        output, dh1, small, da, whole = ffn_both(idx, attn[0], attn[1], cotangent.reshape(-1, width), vecs[l], pieces, pieces)
        keep_layer(x, attn[0], attn, (output, None, None, None), pieces, pieces)
    w_sums, smalls = [None] * layers, [None] * layers

    def ffn_back(l, g):
        x, y1, r1, qkv, p, att, out, r2, ur, gp, attn_pieces, ffn_pieces = kept[l]
        return ffn_backward(not blocked, idx, g, out, r2, y1, r1, vecs[l], ur, gp, ffn_pieces, attn_pieces)

    def heads_back(l, da):
        x, y1, r1, qkv, p, att, out, r2, ur, gp, attn_pieces, ffn_pieces = kept[l]
        return heads_backward(idx, da, qkv, p)

    def inward_back(l, dh1, back):
        x, y1, r1, qkv, p, att, out, r2, ur, gp, attn_pieces, ffn_pieces = kept[l]
        return inward_backward(not blocked, idx, dh1, x, att, back, attn_pieces)

    if blocked:
        f1 = lax.psum_scatter(whole, AXES, scatter_dimension=0, tiled=True)
        back, small_h = heads_back(1, da)
        smalls[1] = jnp.concatenate([small_h[0:2], small[0:10]])
        g, *sums = inward_back(1, dh1, back)
        a1 = Sums(*sums)
        a1.core()
        dh1, small, da, *sums = ffn_back(0, g)
        f0 = Sums(*sums)
        da, f0.give, a1.both = tie((da, f0.give, a1.both))
        f0.core()
        a1.first()
        back, small_h = heads_back(0, da)
        smalls[0] = jnp.concatenate([small_h[0:2], small[0:10]])
        back, a1.parts, f0.both = tie((back, a1.parts, f0.both))
        f0.first()
        a1.second()
        g, *sums = inward_back(0, dh1, back)
        a0 = Sums(*sums)
        a0.give, a1.parts, f0.parts = tie((a0.give, a1.parts, f0.parts))
        a0.core()
        f0.second()
        a1.third()
        a0.both, a1.parts = tie((a0.both, a1.parts))
        a0.first()
        a1.fourth()
        small, f0.parts = tie((jnp.stack(smalls), f0.parts))
        f0.third()
        small = add_swap(small, "z2")
        small, a0.parts, f1 = tie((small, a0.parts, f1))
        a0.second()
        small = add_swap(small, "x")
        small, a0.parts, f0.parts = tie((small, a0.parts, f0.parts))
        a0.third()
        f0.fourth()
        small = add_swap(small, "y")
        small, a0.parts, f0.parts = tie((small, a0.parts, f0.parts))
        a0.fourth()
        small = add_swap(small, "z1")
        small, a0.parts = tie((small, a0.parts))
        small = add_swap(small, "c")
        f1 = f1[0].astype(F32)
        f0 = f0.result()
        a0, a1 = (m.result()[:, 0] for m in (a0, a1))
        w_sums = [(a0, f0[:, 0], f0[:, 1]), (a1, f1[:, 0], f1[:, 1])]
    else:
        for l in reversed(range(layers)):
            if l + 1 < layers:
                dh1, small, da, whole = ffn_back(l, g)
            back, small_h = heads_back(l, da)
            g, sums_a = inward_back(l, dh1, back)
            smalls[l] = jnp.concatenate([small_h[0:2], small[0:10]])
            w_sums[l] = collect_any(sums_a, whole, width)
        small = lax.psum(jnp.stack(smalls), AXES)
    names = ("qb", "vb", "ob", "ag", "as", "eb", "cb", "fg", "fs")
    outs = dict(zip(names, own_small(small, rows, device)))
    flat = {"in": [], "out": [], "ex": [], "co": []}
    for l in range(layers):
        if not blocked:
            for name, share in zip(("in", "out", "ex", "co"), w_sums[l]):
                flat[name].append(share)
            continue
        attn, expand, contract = w_sums[l]
        squares = jnp.stack([attn[0], attn[1], expand[0], expand[1]])
        low, high = squares[:, :rows], squares[:, rows:]
        mine = jnp.where(c == 0, low, high)
        got = swap(jnp.where(c == 0, high, low), "c")
        zero, one = jnp.where(c == 0, mine, got), jnp.where(c == 0, got, mine)
        flat["in"].append(jnp.concatenate([zero[0], one[0], zero[1]], axis=1).reshape(-1))
        flat["out"].append(one[1].reshape(-1))
        flat["ex"].append(jnp.concatenate([zero[2], zero[3], one[2], one[3]], axis=1).reshape(-1))
        flat["co"].append(contract.reshape(-1))
    flat = {k: jnp.stack(v) for k, v in flat.items()}
    shape = tokens.shape
    return (
        output.reshape(shape), g.reshape(shape), flat["in"], outs["qb"], outs["vb"], flat["out"], outs["ob"],
        outs["ag"], outs["as"], flat["ex"], outs["eb"], flat["co"], outs["cb"], outs["fg"], outs["fs"],
    )


def solution(mesh):
    flat = P(None, AXES)
    deep = P(None, AXES, None, None)
    blocked = mesh.shape["wide"] == 8 and mesh.shape["narrow"] == 4
    return jax.shard_map(
        partial(local, blocked),
        mesh=mesh,
        in_specs=(deep,) + (flat,) * 14 + (deep,),
        out_specs=(deep, deep) + (flat,) * 13,
        check_vma=False,
    )
```

time: 554 us -> 515 us (0.930)
  Pallas kernels: 246 us -> 210 us
  waiting for transfers between devices: 129 us -> 147 us
  starting transfers between devices: 78.3 us -> 70.5 us
  other arithmetic: 52.9 us -> 46 us
    pallas_call x12 -> x9, Pallas kernels: 246 us -> 210 us  [call(): pl.pallas_call(kernel, in_specs=[SMEM] + [ANY] * (len(operands) - 1), out...]
    ppermute x82 -> x75, waiting for transfers between devices: 129 us -> 147 us  [swap(): return lax.ppermute(array, AXES, [(i, i ^ BITS[by]) for i in range(32)])]
    ppermute x82 -> x75, starting transfers between devices: 78.2 us -> 70.5 us  [swap(): return lax.ppermute(array, AXES, [(i, i ^ BITS[by]) for i in range(32)])]
    another operation x20 -> x14, other arithmetic: 15.6 us -> 11.3 us  [line(): jnp.stack([self.total(s, lo, 2 * lo) for s in range(2)]).astype(BF16)]
    convert_element_type x12 -> x8, other arithmetic: 21.8 us -> 18.4 us  [plane(): self.total(s, lo, 2 * lo).astype(BF16)]
  transfers between devices with their start and end apart: 83 -> 76, of which waited for: 27 -> 30; matrix products, arithmetic and copies ran while one was open for 11% -> 9% of each run, Pallas kernels for 27% -> 33%
where the time goes in v2:
time: 515 us; the launch traced here: 509 us
  Pallas kernels  210 us (41%)
  waiting for transfers between devices  147 us (29%)
  starting transfers between devices  70.5 us (14%)
  other arithmetic  46 us (9%)
  local copies, waits for them, and re-layouts  19.3 us (4%)
  between operations  15.8 us (3%)
    pallas_call x9, Pallas kernels, call(): pl.pallas_call(kernel, in_specs=[SMEM] + [ANY] * (len(operands) - 1), out...  210 us
    ppermute x75, waiting for transfers between devices, swap(): return lax.ppermute(array, AXES, [(i, i ^ BITS[by]) for i in range(32)])  147 us
    ppermute x75, starting transfers between devices, swap(): return lax.ppermute(array, AXES, [(i, i ^ BITS[by]) for i in range(32)])  70.5 us
    convert_element_type x8, other arithmetic, plane(): self.total(s, lo, 2 * lo).astype(BF16)  18.4 us
    another operation x14, other arithmetic, line(): jnp.stack([self.total(s, lo, 2 * lo) for s in range(2)]).astype(BF16)  11.3 us
  transfers between devices with their start and end apart: 76, of which 30 were waited for; matrix products, arithmetic and copies ran while one was open for 9% of the time, Pallas kernels for 33%

profile of v2, /device:TPU:0, one launch (start us, length us, event | category | flops | bytes accessed | tf_op | source)
XLA Modules:
  0.0 508.7 jit_solution(17622811073694637072)
XLA Ops:
  13.2 4.7 collective-permute-start.2
  18.1 4.5 collective-permute-done.2
  28.2 13.5 %collective-permute-done.6 = f32[2,16,768]{2,1,0:T(8,128)S(1)} collective-permute-done((f32[2,16,768]{2,1,0:T(8,128)S(1)}, f32[2,16,768]{2,1,0:T(8,128)S(1)}, u32[]{:S(2)}, u32[]{:S(2)}) %collective-permute-start.6) | collective-permute-done | bytes 98336 | tf_op jit(solution)/shard_map/ppermute | solution.py:773
  54.1 7.5 %collective-permute-done.7 = bf16[2,2,2,48,768]{4,3,2,1,0:T(8,128)(2,1)S(1)} collective-permute-done((bf16[2,2,2,48,768]{4,3,2,1,0:T(8,128)(2,1)S(1)}, bf16[2,2,2,48,768]{4,3,2,1,0:T(8,128)(2,1)S(1)}, u32[]{:S(2)}, u32[]{:S(2)}) %collective-permute-start.7) | collective-permute-done | bytes 589856 | tf_op jit(solution)/shard_map/ppermute | solution.py:773
  61.8 4.5 collective-permute-done.11.refs_1_.refs_9_
  70.7 12.2 %collective-permute-done.16 = f32[2,16,768]{2,1,0:T(8,128)S(1)} collective-permute-done((f32[2,16,768]{2,1,0:T(8,128)S(1)}, f32[2,16,768]{2,1,0:T(8,128)S(1)}, u32[]{:S(2)}, u32[]{:S(2)}) %collective-permute-start.16) | collective-permute-done | bytes 98336 | tf_op jit(solution)/shard_map/ppermute | solution.py:773
  92.8 23.1 %attn_forward.2 = (f32[768,768]{1,0:T(8,128)}, f32[768,1]{1,0:T(8,128)}, bf16[3,768,768]{2,1,0:T(8,128)(2,1)}, bf16[24,384,384]{2,1,0:T(8,128)(2,1)}, bf16[768,768]{1,0:T(8,128)(2,1)}) custom-call(s32[8]{0:T(128)} %concatenate.121.idx, bf16[768,768]{1,0:T(8,128)(2,1)} %bitcast.478, f32[16,768]{1,0:T(8,128)} %get-tuple-element.437.vec_ref, ...), custom_call_target="tpu_custom_call" | custom-call | flops 4529848320 | bytes 31457280 | tf_op jit(solution)/shard_map/attn_forward/pallas_call | solution.py:180
  119.1 8.4 %collective-permute-done.29 = bf16[2,2,48,768]{3,2,1,0:T(8,128)(2,1)S(1)} collective-permute-done((bf16[2,2,48,768]{3,2,1,0:T(8,128)(2,1)S(1)}, bf16[2,2,48,768]{3,2,1,0:T(8,128)(2,1)S(1)}, u32[]{:S(2)}, u32[]{:S(2)}) %collective-permute-start.29) | collective-permute-done | bytes 294944 | tf_op jit(solution)/shard_map/ppermute | solution.py:773
  127.7 6.2 %collective-permute-start.32 = (bf16[2,2,2,48,768]{4,3,2,1,0:T(8,128)(2,1)S(1)}, bf16[2,2,2,48,768]{4,3,2,1,0:T(8,128)(2,1)S(1)}, u32[]{:S(2)}, u32[]{:S(2)}) collective-permute-start(bf16[2,2,2,48,768]{4,3,2,1,0:T(8,128)(2,1)S(1)} %pad_maximum_fusion.13), channel_id=1, source_target_pairs={{0,8},{1,9},{2,10},{3,11},{4,12},{5,13},{6,14},{7,15},{8,0},{9,1},... | collective-permute-start | bytes 1769480 | tf_op jit(solution)/shard_map/ppermute | solution.py:773
  136.2 10.6 %collective-permute-done.32 = bf16[2,2,2,48,768]{4,3,2,1,0:T(8,128)(2,1)S(1)} collective-permute-done((bf16[2,2,2,48,768]{4,3,2,1,0:T(8,128)(2,1)S(1)}, bf16[2,2,2,48,768]{4,3,2,1,0:T(8,128)(2,1)S(1)}, u32[]{:S(2)}, u32[]{:S(2)}) %collective-permute-start.32) | collective-permute-done | bytes 589856 | tf_op jit(solution)/shard_map/ppermute | solution.py:773
  147.0 20.5 %ffn_forward.1 = (f32[768,768]{1,0:T(8,128)}, f32[768,1]{1,0:T(8,128)}, bf16[4,768,768]{2,1,0:T(8,128)(2,1)}, bf16[4,768,768]{2,1,0:T(8,128)(2,1)}) custom-call(s32[8]{0:T(128)} %concatenate.121.idx, f32[768,768]{1,0:T(8,128)} %get-tuple-element.185.y1_ref, f32[16,768]{1,0:T(8,128)} %get-tuple-element.437.vec_ref, bf16[8,2,48,768]{3,2,1,0:T(8,128)(2,1)} %copy-done.4, ...), custom_call_target="tpu_custom_call" | custom-call | flops 7247757312 | bytes 31457280 | tf_op jit(solution)/shard_map/ffn_forward/pallas_call | solution.py:180
  171.3 11.3 %collective-permute-done.36 = bf16[4,2,48,768]{3,2,1,0:T(8,128)(2,1)S(1)} collective-permute-done((bf16[4,2,48,768]{3,2,1,0:T(8,128)(2,1)S(1)}, bf16[4,2,48,768]{3,2,1,0:T(8,128)(2,1)S(1)}, u32[]{:S(2)}, u32[]{:S(2)}) %collective-permute-start.36) | collective-permute-done | bytes 589856 | tf_op jit(solution)/shard_map/ppermute | solution.py:773
  190.8 23.2 %attn_forward.3 = (f32[768,768]{1,0:T(8,128)}, f32[768,1]{1,0:T(8,128)}, bf16[3,768,768]{2,1,0:T(8,128)(2,1)}, bf16[24,384,384]{2,1,0:T(8,128)(2,1)}, bf16[768,768]{1,0:T(8,128)(2,1)}) custom-call(s32[8]{0:T(128)} %concatenate.121.idx, f32[768,768]{1,0:T(8,128)} %get-tuple-element.195.x_ref, f32[16,768]{1,0:T(8,128)} %get-tuple-element.436.vec_ref, ...), custom_call_target="tpu_custom_call" | custom-call | flops 4529848320 | bytes 31457280 | tf_op jit(solution)/shard_map/attn_forward/pallas_call | solution.py:180
  219.7 43.0 %ffn_both.1 = (f32[768,768]{1,0:T(8,128)}, f32[768,768]{1,0:T(8,128)}, f32[16,768]{1,0:T(8,128)}, bf16[768,768]{1,0:T(8,128)(2,1)}, bf16[32,2,2,48,768]{4,3,2,1,0:T(8,128)(2,1)}) custom-call(s32[8]{0:T(128)} %concatenate.121.idx, f32[768,768]{1,0:T(8,128)} %get-tuple-element.199.y1_ref, f32[768,1]{1,0:T(8,128)} %get-tuple-element.200.r1_ref, ...), custom_call_target="tpu_custom_call" | custom-call | flops 21743271936 | bytes 31457280 | tf_op jit(solution)/shard_map/ffn_both/pallas_call | solution.py:180
  262.7 17.6 %heads_backward.2 = (bf16[3,768,768]{2,1,0:T(8,128)(2,1)}, f32[8,768]{1,0:T(8,128)}) custom-call(s32[8]{0:T(128)} %concatenate.121.idx, bf16[768,768]{1,0:T(8,128)(2,1)} %get-tuple-element.208.da_ref, bf16[3,768,768]{2,1,0:T(8,128)(2,1)} %get-tuple-element.209.qkv_ref, bf16[24,384,384]{2,1,0:T(8,128)(2,1)} %get-tuple-element.210.p_ref), custom_call_target="tpu_custom_call" | custom-call | flops 6794772480 | bytes 31457280 | tf_op jit(solution)/shard_map/heads_backward/pallas_call | solution.py:180
  280.3 16.3 %inward_backward.2 = (f32[768,768]{1,0:T(8,128)}, bf16[2,16,1,48,768]{4,3,2,1,0:T(8,128)(2,1)}, bf16[2,16,1,48,768]{4,3,2,1,0:T(8,128)(2,1)}) custom-call(s32[8]{0:T(128)} %concatenate.121.idx, f32[768,768]{1,0:T(8,128)} %get-tuple-element.206.dh1_ref, f32[768,768]{1,0:T(8,128)} %get-tuple-element.195.x_ref, bf16[768,768]{1,0:T(8,128)(2,1)} %get-tuple-element.207.att_ref, ...), custom_call_target="tpu_custom_call" | custom-call | flops 6341787648 | bytes 31457280 | tf_op jit(solution)/shard_map/inward_backward/pallas_call | solution.py:180
  296.9 33.1 %ffn_backward.1 = (f32[768,768]{1,0:T(8,128)}, f32[16,768]{1,0:T(8,128)}, bf16[768,768]{1,0:T(8,128)(2,1)}, bf16[2,16,2,48,768]{4,3,2,1,0:T(8,128)(2,1)}, bf16[2,16,2,48,768]{4,3,2,1,0:T(8,128)(2,1)}) custom-call(s32[8]{0:T(128)} %concatenate.121.idx, f32[768,768]{1,0:T(8,128)} %get-tuple-element.212.g_ref, f32[768,768]{1,0:T(8,128)} %get-tuple-element.195.x_ref, ...), custom_call_target="tpu_custom_call" | custom-call | flops 14495514624 | bytes 31457280 | tf_op jit(solution)/shard_map/ffn_backward/pallas_call | solution.py:180
  334.4 17.8 %heads_backward.3 = (bf16[3,768,768]{2,1,0:T(8,128)(2,1)}, f32[8,768]{1,0:T(8,128)}) custom-call(s32[8]{0:T(128)} %concatenate.121.idx, bf16[768,768]{1,0:T(8,128)(2,1)} %get-tuple-element.223.da_ref, bf16[3,768,768]{2,1,0:T(8,128)(2,1)} %get-tuple-element.224.qkv_ref, bf16[24,384,384]{2,1,0:T(8,128)(2,1)} %get-tuple-element.225.p_ref), custom_call_target="tpu_custom_call" | custom-call | flops 6794772480 | bytes 31457280 | tf_op jit(solution)/shard_map/heads_backward/pallas_call | solution.py:180
  357.0 4.5 fusion.1
  369.3 15.5 %inward_backward.3 = (f32[768,768]{1,0:T(8,128)}, bf16[2,16,1,48,768]{4,3,2,1,0:T(8,128)(2,1)}, bf16[2,16,1,48,768]{4,3,2,1,0:T(8,128)(2,1)}) custom-call(s32[8]{0:T(128)} %concatenate.121.idx, f32[768,768]{1,0:T(8,128)} %get-tuple-element.217.dh1_ref, bf16[768,768]{1,0:T(8,128)(2,1)} %bitcast.479, bf16[768,768]{1,0:T(8,128)(2,1)} %get-tuple-element.218.att_ref, ...), custom_call_target="tpu_custom_call" | custom-call | flops 6341787648 | bytes 31457280 | tf_op jit(solution)/shard_map/inward_backward/pallas_call | solution.py:180
  384.8 17.3 %collective-permute-done.52 = bf16[4,1,48,768]{3,2,1,0:T(8,128)(2,1)S(1)} collective-permute-done((bf16[4,1,48,768]{3,2,1,0:T(8,128)(2,1)}, bf16[4,1,48,768]{3,2,1,0:T(8,128)(2,1)S(1)}, u32[]{:S(2)}, u32[]{:S(2)}) %collective-permute-start.52) | collective-permute-done | bytes 294944 | tf_op jit(solution)/shard_map/ppermute | solution.py:773
  415.0 5.4 %collective-permute-done.56 = bf16[2,2,1,48,768]{4,3,1,2,0:T(8,128)(2,1)S(1)} collective-permute-done((bf16[2,2,1,48,768]{4,3,1,2,0:T(8,128)(2,1)S(1)}, bf16[2,2,1,48,768]{4,3,1,2,0:T(8,128)(2,1)S(1)}, u32[]{:S(2)}, u32[]{:S(2)}) %collective-permute-start.56) | collective-permute-done | bytes 294944 | tf_op jit(solution)/shard_map/ppermute | solution.py:773
  438.0 4.2 collective-permute-done.65
  486.2 4.5 collective-permute-done.69
  (381 shorter events, 163.6 us)
Async XLA Ops:
  7.2 441.1 %reduce-scatter.2.cloned.1.call-start = ((), (), s32[]{:S(2)}) async-start(), calls=%async_computation.1 | async-start | bytes 9732096 | tf_op jit(solution)/shard_map/reduce_scatter | solution.py:1021
  84.8 31.1 %collective-permute-start.17 = (bf16[8,2,48,768]{3,2,1,0:T(8,128)(2,1)S(1)}, bf16[8,2,48,768]{3,2,1,0:T(8,128)(2,1)}, u32[]{:S(2)}, u32[]{:S(2)}) collective-permute-start(bf16[8,2,48,768]{3,2,1,0:T(8,128)(2,1)S(1)} %pad_maximum_fusion.1.refs_0_), channel_id=1, source_target_pairs={{0,2},{1,3},{2,0},{3,1},{4,6},{5,7},{6,4},{7,5},{8,10},{9,11},{10,... | collective-permute-start | bytes 3538952 | tf_op jit(solution)/shard_map/ppermute | solution.py:773
  86.1 29.9 %collective-permute-start.20 = (bf16[8,2,48,768]{3,2,1,0:T(8,128)(2,1)S(1)}, bf16[8,2,48,768]{3,2,1,0:T(8,128)(2,1)}, u32[]{:S(2)}, u32[]{:S(2)}) collective-permute-start(bf16[8,2,48,768]{3,2,1,0:T(8,128)(2,1)S(1)} %pad_maximum_fusion.1.refs_0_), channel_id=1, source_target_pairs={{0,1},{1,0},{2,3},{3,2},{4,5},{5,4},{6,7},{7,6},{8,9},{9,8},{10,11... | collective-permute-start | bytes 3538952 | tf_op jit(solution)/shard_map/ppermute | solution.py:773
  86.2 29.8 %collective-permute-start.18 = (bf16[8,2,48,768]{3,2,1,0:T(8,128)(2,1)S(1)}, bf16[8,2,48,768]{3,2,1,0:T(8,128)(2,1)}, u32[]{:S(2)}, u32[]{:S(2)}) collective-permute-start(bf16[8,2,48,768]{3,2,1,0:T(8,128)(2,1)S(1)} %pad_maximum_fusion.2.refs_4_), channel_id=1, source_target_pairs={{0,4},{1,5},{2,6},{3,7},{4,0},{5,1},{6,2},{7,3},{8,12},{9,13},{10,... | collective-permute-start | bytes 3538952 | tf_op jit(solution)/shard_map/ppermute | solution.py:773
  87.7 28.3 %collective-permute-start.21 = (bf16[8,2,48,768]{3,2,1,0:T(8,128)(2,1)S(1)}, bf16[8,2,48,768]{3,2,1,0:T(8,128)(2,1)}, u32[]{:S(2)}, u32[]{:S(2)}) collective-permute-start(bf16[8,2,48,768]{3,2,1,0:T(8,128)(2,1)S(1)} %pad_maximum_fusion.2.refs_4_), channel_id=1, source_target_pairs={{0,1},{1,0},{2,3},{3,2},{4,5},{5,4},{6,7},{7,6},{8,9},{9,8},{10,11... | collective-permute-start | bytes 3538952 | tf_op jit(solution)/shard_map/ppermute | solution.py:773
  92.8 23.1 %collective-permute-start.19 = (bf16[2,2,48,768]{3,2,1,0:T(8,128)(2,1)S(1)}, bf16[2,2,48,768]{3,2,1,0:T(8,128)(2,1)S(1)}, u32[]{:S(2)}, u32[]{:S(2)}) collective-permute-start(bf16[2,2,48,768]{3,2,1,0:T(8,128)(2,1)S(1)} %pad_maximum_fusion.23), channel_id=1, source_target_pairs={{0,8},{1,9},{2,10},{3,11},{4,12},{5,13},{6,14},{7,15},{8,0},{9,1},... | collective-permute-start | bytes 884744 | tf_op jit(solution)/shard_map/ppermute | solution.py:773
  116.9 30.0 %collective-permute-start.33 = (bf16[8,2,48,768]{3,2,1,0:T(8,128)(2,1)}, bf16[8,2,48,768]{3,2,1,0:T(8,128)(2,1)}, u32[]{:S(2)}, u32[]{:S(2)}) collective-permute-start(bf16[8,2,48,768]{3,2,1,0:T(8,128)(2,1)} %collective-permute-done.17.refs_1_), channel_id=1, source_target_pairs={{0,1},{1,0},{2,3},{3,2},{4,5},{5,4},{6,7},{7,6},{8,9},{9,8},{10,11... | collective-permute-start | bytes 3538952 | tf_op jit(solution)/shard_map/ppermute | solution.py:773
  117.2 29.8 %collective-permute-start.34 = (bf16[8,2,48,768]{3,2,1,0:T(8,128)(2,1)}, bf16[8,2,48,768]{3,2,1,0:T(8,128)(2,1)}, u32[]{:S(2)}, u32[]{:S(2)}) collective-permute-start(bf16[8,2,48,768]{3,2,1,0:T(8,128)(2,1)} %collective-permute-done.18.refs_5_), channel_id=1, source_target_pairs={{0,1},{1,0},{2,3},{3,2},{4,5},{5,4},{6,7},{7,6},{8,9},{9,8},{10,11... | collective-permute-start | bytes 3538952 | tf_op jit(solution)/shard_map/ppermute | solution.py:773
  127.7 19.2 %collective-permute-start.32 = (bf16[2,2,2,48,768]{4,3,2,1,0:T(8,128)(2,1)S(1)}, bf16[2,2,2,48,768]{4,3,2,1,0:T(8,128)(2,1)S(1)}, u32[]{:S(2)}, u32[]{:S(2)}) collective-permute-start(bf16[2,2,2,48,768]{4,3,2,1,0:T(8,128)(2,1)S(1)} %pad_maximum_fusion.13), channel_id=1, source_target_pairs={{0,8},{1,9},{2,10},{3,11},{4,12},{5,13},{6,14},{7,15},{8,0},{9,1},... | collective-permute-start | bytes 1769480 | tf_op jit(solution)/shard_map/ppermute | solution.py:773
  133.9 33.6 %collective-permute-start.30 = (bf16[8,1,48,768]{3,2,1,0:T(8,128)(2,1)S(1)}, bf16[8,1,48,768]{3,2,1,0:T(8,128)(2,1)}, u32[]{:S(2)}, u32[]{:S(2)}) collective-permute-start(bf16[8,1,48,768]{3,2,1,0:T(8,128)(2,1)S(1)} %pad_maximum_fusion.11.refs_0_.refs_8_), channel_id=1, source_target_pairs={{0,2},{1,3},{2,0},{3,1},{4,6},{5,7},{6,4},{7,5},{8,10},{9,11},{10,... | collective-permute-start | bytes 1769480 | tf_op jit(solution)/shard_map/ppermute | solution.py:773
  134.6 32.9 %collective-permute-start.31 = (bf16[8,1,48,768]{3,2,1,0:T(8,128)(2,1)S(1)}, bf16[8,1,48,768]{3,2,1,0:T(8,128)(2,1)S(1)}, u32[]{:S(2)}, u32[]{:S(2)}) collective-permute-start(bf16[8,1,48,768]{3,2,1,0:T(8,128)(2,1)S(1)} %pad_maximum_fusion.12.refs_4_.refs_12_), channel_id=1, source_target_pairs={{0,4},{1,5},{2,6},{3,7},{4,0},{5,1},{6,2},{7,3},{8,12},{9,13},{10,... | collective-permute-start | bytes 1769480 | tf_op jit(solution)/shard_map/ppermute | solution.py:773
  183.1 30.9 %collective-permute-start.37 = (bf16[8,2,48,768]{3,2,1,0:T(8,128)(2,1)S(1)}, bf16[8,2,48,768]{3,2,1,0:T(8,128)(2,1)}, u32[]{:S(2)}, u32[]{:S(2)}) collective-permute-start(bf16[8,2,48,768]{3,2,1,0:T(8,128)(2,1)S(1)} %pad_maximum_fusion.4.refs_0_), channel_id=1, source_target_pairs={{0,2},{1,3},{2,0},{3,1},{4,6},{5,7},{6,4},{7,5},{8,10},{9,11},{10,... | collective-permute-start | bytes 3538952 | tf_op jit(solution)/shard_map/ppermute | solution.py:773
  184.5 29.6 %collective-permute-start.39 = (bf16[8,2,48,768]{3,2,1,0:T(8,128)(2,1)S(1)}, bf16[8,2,48,768]{3,2,1,0:T(8,128)(2,1)}, u32[]{:S(2)}, u32[]{:S(2)}) collective-permute-start(bf16[8,2,48,768]{3,2,1,0:T(8,128)(2,1)S(1)} %pad_maximum_fusion.4.refs_0_), channel_id=1, source_target_pairs={{0,1},{1,0},{2,3},{3,2},{4,5},{5,4},{6,7},{7,6},{8,9},{9,8},{10,11... | collective-permute-start | bytes 3538952 | tf_op jit(solution)/shard_map/ppermute | solution.py:773
  184.5 29.5 %collective-permute-start.38 = (bf16[8,2,48,768]{3,2,1,0:T(8,128)(2,1)S(1)}, bf16[8,2,48,768]{3,2,1,0:T(8,128)(2,1)S(1)}, u32[]{:S(2)}, u32[]{:S(2)}) collective-permute-start(bf16[8,2,48,768]{3,2,1,0:T(8,128)(2,1)S(1)} %pad_maximum_fusion.5.refs_4_), channel_id=1, source_target_pairs={{0,4},{1,5},{2,6},{3,7},{4,0},{5,1},{6,2},{7,3},{8,12},{9,13},{10,... | collective-permute-start | bytes 3538952 | tf_op jit(solution)/shard_map/ppermute | solution.py:773
  186.0 28.1 %collective-permute-start.40 = (bf16[8,2,48,768]{3,2,1,0:T(8,128)(2,1)S(1)}, bf16[8,2,48,768]{3,2,1,0:T(8,128)(2,1)}, u32[]{:S(2)}, u32[]{:S(2)}) collective-permute-start(bf16[8,2,48,768]{3,2,1,0:T(8,128)(2,1)S(1)} %pad_maximum_fusion.5.refs_4_), channel_id=1, source_target_pairs={{0,1},{1,0},{2,3},{3,2},{4,5},{5,4},{6,7},{7,6},{8,9},{9,8},{10,11... | collective-permute-start | bytes 3538952 | tf_op jit(solution)/shard_map/ppermute | solution.py:773
  296.6 33.3 %collective-permute-start.47 = (bf16[2,16,1,48,768]{4,3,2,1,0:T(8,128)(2,1)}, bf16[2,16,1,48,768]{4,3,2,1,0:T(8,128)(2,1)}, u32[]{:S(2)}, u32[]{:S(2)}) collective-permute-start(bf16[2,16,1,48,768]{4,3,2,1,0:T(8,128)(2,1)} %get-tuple-element.222), channel_id=1, source_target_pairs={{0,1},{1,0},{2,3},{3,2},{4,5},{5,4},{6,7},{7,6},{8,9},{9,8},{10,11... | collective-permute-start | bytes 7077896 | tf_op jit(solution)/shard_map/ppermute | solution.py:773
  329.9 27.1 %collective-permute-start.50 = (bf16[2,16,2,48,768]{4,3,2,1,0:T(8,128)(2,1)}, bf16[2,16,2,48,768]{4,3,2,1,0:T(8,128)(2,1)}, u32[]{:S(2)}, u32[]{:S(2)}) collective-permute-start(bf16[2,16,2,48,768]{4,3,2,1,0:T(8,128)(2,1)} %get-tuple-element.230), channel_id=1, source_target_pairs={{0,1},{1,0},{2,3},{3,2},{4,5},{5,4},{6,7},{7,6},{8,9},{9,8},{10,11... | collective-permute-start | bytes 14155784 | tf_op jit(solution)/shard_map/ppermute | solution.py:773
  331.5 23.2 %collective-permute-start.49 = (bf16[8,1,48,768]{3,2,1,0:T(8,128)(2,1)S(1)}, bf16[8,1,48,768]{3,2,1,0:T(8,128)(2,1)S(1)}, u32[]{:S(2)}, u32[]{:S(2)}) collective-permute-start(bf16[8,1,48,768]{3,2,1,0:T(8,128)(2,1)S(1)} %fusion.5), channel_id=1, source_target_pairs={{0,4},{1,5},{2,6},{3,7},{4,0},{5,1},{6,2},{7,3},{8,12},{9,13},{10,... | collective-permute-start | bytes 1769480 | tf_op jit(solution)/shard_map/ppermute | solution.py:773
  333.4 23.6 %collective-permute-start.48 = (bf16[8,1,48,768]{3,2,1,0:T(8,128)(2,1)S(1)}, bf16[8,1,48,768]{3,2,1,0:T(8,128)(2,1)}, u32[]{:S(2)}, u32[]{:S(2)}) collective-permute-start(bf16[8,1,48,768]{3,2,1,0:T(8,128)(2,1)S(1)} %fusion.4), channel_id=1, source_target_pairs={{0,2},{1,3},{2,0},{3,1},{4,6},{5,7},{6,4},{7,5},{8,10},{9,11},{10,... | collective-permute-start | bytes 1769480 | tf_op jit(solution)/shard_map/ppermute | solution.py:773
  361.6 40.6 %collective-permute-start.53 = (bf16[8,2,48,768]{3,2,1,0:T(8,128)(2,1)}, bf16[8,2,48,768]{3,2,1,0:T(8,128)(2,1)S(1)}, u32[]{:S(2)}, u32[]{:S(2)}) collective-permute-start(bf16[8,2,48,768]{3,2,1,0:T(8,128)(2,1)} %get-tuple-element.359), channel_id=1, source_target_pairs={{0,2},{1,3},{2,0},{3,1},{4,6},{5,7},{6,4},{7,5},{8,10},{9,11},{10,... | collective-permute-start | bytes 3538952 | tf_op jit(solution)/shard_map/ppermute | solution.py:773
  362.7 39.5 %collective-permute-start.54 = (bf16[8,2,48,768]{3,2,1,0:T(8,128)(2,1)}, bf16[8,2,48,768]{3,2,1,0:T(8,128)(2,1)}, u32[]{:S(2)}, u32[]{:S(2)}) collective-permute-start(bf16[8,2,48,768]{3,2,1,0:T(8,128)(2,1)} %get-tuple-element.358), channel_id=1, source_target_pairs={{0,4},{1,5},{2,6},{3,7},{4,0},{5,1},{6,2},{7,3},{8,12},{9,13},{10,... | collective-permute-start | bytes 3538952 | tf_op jit(solution)/shard_map/ppermute | solution.py:773
  365.9 36.2 %collective-permute-start.52 = (bf16[4,1,48,768]{3,2,1,0:T(8,128)(2,1)}, bf16[4,1,48,768]{3,2,1,0:T(8,128)(2,1)S(1)}, u32[]{:S(2)}, u32[]{:S(2)}) collective-permute-start(bf16[4,1,48,768]{3,2,1,0:T(8,128)(2,1)} %fusion.16), channel_id=1, source_target_pairs={{0,2},{1,3},{2,0},{3,1},{4,6},{5,7},{6,4},{7,5},{8,10},{9,11},{10,... | collective-permute-start | bytes 884744 | tf_op jit(solution)/shard_map/ppermute | solution.py:773
  369.0 33.1 %collective-permute-start.51 = (bf16[4,1,48,768]{3,2,1,0:T(8,128)(2,1)}, bf16[4,1,48,768]{3,2,1,0:T(8,128)(2,1)}, u32[]{:S(2)}, u32[]{:S(2)}) collective-permute-start(bf16[4,1,48,768]{3,2,1,0:T(8,128)(2,1)} %fusion.15), channel_id=1, source_target_pairs={{0,4},{1,5},{2,6},{3,7},{4,0},{5,1},{6,2},{7,3},{8,12},{9,13},{10,... | collective-permute-start | bytes 884744 | tf_op jit(solution)/shard_map/ppermute | solution.py:773
  402.2 28.0 %collective-permute-start.55 = (bf16[2,16,1,48,768]{4,3,2,1,0:T(8,128)(2,1)}, bf16[2,16,1,48,768]{4,3,2,1,0:T(8,128)(2,1)}, u32[]{:S(2)}, u32[]{:S(2)}) collective-permute-start(bf16[2,16,1,48,768]{4,3,2,1,0:T(8,128)(2,1)} %get-tuple-element.239), channel_id=1, source_target_pairs={{0,1},{1,0},{2,3},{3,2},{4,5},{5,4},{6,7},{7,6},{8,9},{9,8},{10,11... | collective-permute-start | bytes 7077896 | tf_op jit(solution)/shard_map/ppermute | solution.py:773
  (104 other events, 956.4 us)
Sparse Core Ops, SparseCore 0:
  262.8 152.6 reduce-scatter.1

commit v3 on v2

--- a/solution.py
+++ b/solution.py
@@ -218,7 +218,7 @@
     save_qkv = copy(qkv, qkv_ref, sem_q.at[0])
     save_qkv.start()
     pairs = x.shape[1] // (2 * HEAD_DIM)
-    places = lax.broadcasted_iota(jnp.int32, (1, length), 1)
+    places = lax.broadcasted_iota(jnp.int32, (length, 1), 0)
     even = even_lanes()
 
     def pair(step, carry):
@@ -228,20 +228,20 @@
         hidden = jnp.where(places < idx[4 + n], 0.0, -1e30)
         q2 = qkv[0, rows, lanes] * jnp.asarray(HEAD_DIM**-0.5, BF16)
         k2 = qkv[1, rows, lanes]
-        v2 = qkv[2, rows, lanes]
+        v2 = qkv[2, rows, lanes].T
+        masks = (even, jnp.logical_not(even))
+        scores = [nt(k2, jnp.where(mine, q2, jnp.zeros_like(q2))) + hidden for mine in masks]
         parts = []
-        for h in range(2):
-            mine = even if h == 0 else jnp.logical_not(even)
-            s = nt(jnp.where(mine, q2, jnp.zeros_like(q2)), k2) + hidden
-            e = jnp.exp(s - jnp.max(s, axis=-1, keepdims=True))
-            soft = (e * (1.0 / jnp.sum(e, axis=-1, keepdims=True))).astype(BF16)
+        for h, s in enumerate(scores):
+            e = jnp.exp(s - jnp.max(s, axis=0, keepdims=True))
+            soft = (e * (1.0 / jnp.sum(e, axis=0, keepdims=True))).astype(BF16)
             p[2 * step + h] = soft
-            parts.append(mm(soft, v2))
-        att[rows, lanes] = jnp.where(even, parts[0], parts[1]).astype(BF16)
+            parts.append(mm(v2[h * HEAD_DIM : (h + 1) * HEAD_DIM], soft))
+        att[rows, lanes] = jnp.concatenate(parts, axis=0).T.astype(BF16)
         copy(p.at[pl.ds(2 * step, 2)], p_ref.at[pl.ds(2 * step, 2)], sem_p.at[0]).start()
         return carry
 
-    lax.fori_loop(0, 2 * pairs, pair, 0)
+    lax.fori_loop(0, 2 * pairs, pair, 0, unroll=3)
     save_att = copy(att, att_ref, sem_q.at[1])
     save_att.start()
     wait_square(w, sem_w, 3)
@@ -658,18 +658,18 @@
             lanes = pl.ds(pl.multiple_of(j * 2 * HEAD_DIM, 2 * HEAD_DIM), 2 * HEAD_DIM)
             q2, k2, v2 = (qkv[i, n * length : (n + 1) * length, lanes] for i in range(3))
             da2 = da[n * length : (n + 1) * length, lanes]
-            dqs, dks, dvs = [], [], []
-            for h in range(2):
-                mine = even if h == 0 else jnp.logical_not(even)
-                soft = p[slot, h]
-                dp = nt(jnp.where(mine, da2, jnp.zeros_like(da2)), v2)
-                dvs.append(tn(soft, da2))
+            masks = (even, jnp.logical_not(even))
+            k2t = k2.T
+            dps = [nt(v2, jnp.where(mine, da2, jnp.zeros_like(da2))) for mine in masks]
+            softs = [p[slot, h] for h in range(2)]
+            dss = []
+            for soft, dp in zip(softs, dps):
                 soft = soft.astype(F32)
-                inner = jnp.sum(soft * dp, axis=-1, keepdims=True)
-                ds = (soft * (dp - inner)).astype(BF16)
-                dqs.append(mm(ds, k2))
-                dks.append(tn(ds, q2))
-            dq, dk, dv = (jnp.where(even, m[0], m[1]) for m in (dqs, dks, dvs))
+                inner = jnp.sum(soft * dp, axis=0, keepdims=True)
+                dss.append((soft * (dp - inner)).astype(BF16))
+            dv = jnp.where(even, mm(softs[0], da2), mm(softs[1], da2))
+            dk = jnp.where(even, mm(dss[0], q2), mm(dss[1], q2))
+            dq = jnp.concatenate([mm(k2t[h * HEAD_DIM : (h + 1) * HEAD_DIM], dss[h]) for h in range(2)], axis=0).T
             back[0, n * length : (n + 1) * length, lanes] = (dq * factor).astype(BF16)
             back[1, n * length : (n + 1) * length, lanes] = (dk * factor).astype(BF16)
             back[2, n * length : (n + 1) * length, lanes] = dv.astype(BF16)

time: 515 us -> 507 us (0.984)
  Pallas kernels: 210 us -> 198 us
    pallas_call x9, Pallas kernels: 210 us -> 198 us  [call(): pl.pallas_call(kernel, in_specs=[SMEM] + [ANY] * (len(operands) - 1), out...]
  transfers between devices with their start and end apart: 76 -> 76, of which waited for: 30 -> 33; matrix products, arithmetic and copies ran while one was open for 9% -> 9% of each run, Pallas kernels for 33% -> 31%
where the time goes in v3:
time: 507 us; the launch traced here: 500 us
  Pallas kernels  198 us (39%)
  waiting for transfers between devices  151 us (30%)
  starting transfers between devices  69.4 us (14%)
  other arithmetic  45.9 us (9%)
  local copies, waits for them, and re-layouts  19.3 us (4%)
  between operations  15.7 us (3%)
    pallas_call x9, Pallas kernels, call(): pl.pallas_call(kernel, in_specs=[SMEM] + [ANY] * (len(operands) - 1), out...  198 us
    ppermute x75, waiting for transfers between devices, swap(): return lax.ppermute(array, AXES, [(i, i ^ BITS[by]) for i in range(32)])  151 us
    ppermute x75, starting transfers between devices, swap(): return lax.ppermute(array, AXES, [(i, i ^ BITS[by]) for i in range(32)])  69.4 us
    convert_element_type x8, other arithmetic, plane(): self.total(s, lo, 2 * lo).astype(BF16)  18.2 us
    another operation x14, other arithmetic, line(): jnp.stack([self.total(s, lo, 2 * lo) for s in range(2)]).astype(BF16)  11.3 us
  transfers between devices with their start and end apart: 76, of which 33 were waited for; matrix products, arithmetic and copies ran while one was open for 9% of the time, Pallas kernels for 31%

profile of v3, /device:TPU:0, one launch (start us, length us, event | category | flops | bytes accessed | tf_op | source)
XLA Modules:
  0.0 499.7 jit_solution(5719381576489118086)
XLA Ops:
  13.2 4.7 collective-permute-start.2
  18.1 4.5 collective-permute-done.2
  28.2 13.5 %collective-permute-done.6 = f32[2,16,768]{2,1,0:T(8,128)S(1)} collective-permute-done((f32[2,16,768]{2,1,0:T(8,128)S(1)}, f32[2,16,768]{2,1,0:T(8,128)S(1)}, u32[]{:S(2)}, u32[]{:S(2)}) %collective-permute-start.6) | collective-permute-done | bytes 98336 | tf_op jit(solution)/shard_map/ppermute | solution.py:773
  47.2 4.0 collective-permute-done.10
  54.1 7.5 %collective-permute-done.7 = bf16[2,2,2,48,768]{4,3,2,1,0:T(8,128)(2,1)S(1)} collective-permute-done((bf16[2,2,2,48,768]{4,3,2,1,0:T(8,128)(2,1)S(1)}, bf16[2,2,2,48,768]{4,3,2,1,0:T(8,128)(2,1)S(1)}, u32[]{:S(2)}, u32[]{:S(2)}) %collective-permute-start.7) | collective-permute-done | bytes 589856 | tf_op jit(solution)/shard_map/ppermute | solution.py:773
  61.8 4.5 collective-permute-done.11.refs_1_.refs_9_
  70.7 12.2 %collective-permute-done.16 = f32[2,16,768]{2,1,0:T(8,128)S(1)} collective-permute-done((f32[2,16,768]{2,1,0:T(8,128)S(1)}, f32[2,16,768]{2,1,0:T(8,128)S(1)}, u32[]{:S(2)}, u32[]{:S(2)}) %collective-permute-start.16) | collective-permute-done | bytes 98336 | tf_op jit(solution)/shard_map/ppermute | solution.py:773
  92.8 18.3 %attn_forward.2 = (f32[768,768]{1,0:T(8,128)}, f32[768,1]{1,0:T(8,128)}, bf16[3,768,768]{2,1,0:T(8,128)(2,1)}, bf16[24,384,384]{2,1,0:T(8,128)(2,1)}, bf16[768,768]{1,0:T(8,128)(2,1)}) custom-call(s32[8]{0:T(128)} %concatenate.121.idx, bf16[768,768]{1,0:T(8,128)(2,1)} %bitcast.478, f32[16,768]{1,0:T(8,128)} %get-tuple-element.437.vec_ref, ...), custom_call_target="tpu_custom_call" | custom-call | flops 4529848320 | bytes 31457280 | tf_op jit(solution)/shard_map/attn_forward/pallas_call | solution.py:180
  117.6 7.5 %collective-permute-done.29 = bf16[2,2,48,768]{3,2,1,0:T(8,128)(2,1)S(1)} collective-permute-done((bf16[2,2,48,768]{3,2,1,0:T(8,128)(2,1)S(1)}, bf16[2,2,48,768]{3,2,1,0:T(8,128)(2,1)S(1)}, u32[]{:S(2)}, u32[]{:S(2)}) %collective-permute-start.29) | collective-permute-done | bytes 294944 | tf_op jit(solution)/shard_map/ppermute | solution.py:773
  131.4 10.6 %collective-permute-done.32 = bf16[2,2,2,48,768]{4,3,2,1,0:T(8,128)(2,1)S(1)} collective-permute-done((bf16[2,2,2,48,768]{4,3,2,1,0:T(8,128)(2,1)S(1)}, bf16[2,2,2,48,768]{4,3,2,1,0:T(8,128)(2,1)S(1)}, u32[]{:S(2)}, u32[]{:S(2)}) %collective-permute-start.32) | collective-permute-done | bytes 589856 | tf_op jit(solution)/shard_map/ppermute | solution.py:773
  142.2 20.5 %ffn_forward.1 = (f32[768,768]{1,0:T(8,128)}, f32[768,1]{1,0:T(8,128)}, bf16[4,768,768]{2,1,0:T(8,128)(2,1)}, bf16[4,768,768]{2,1,0:T(8,128)(2,1)}) custom-call(s32[8]{0:T(128)} %concatenate.121.idx, f32[768,768]{1,0:T(8,128)} %get-tuple-element.185.y1_ref, f32[16,768]{1,0:T(8,128)} %get-tuple-element.437.vec_ref, bf16[8,2,48,768]{3,2,1,0:T(8,128)(2,1)} %copy-done.4, ...), custom_call_target="tpu_custom_call" | custom-call | flops 7247757312 | bytes 31457280 | tf_op jit(solution)/shard_map/ffn_forward/pallas_call | solution.py:180
  166.5 11.3 %collective-permute-done.36 = bf16[4,2,48,768]{3,2,1,0:T(8,128)(2,1)S(1)} collective-permute-done((bf16[4,2,48,768]{3,2,1,0:T(8,128)(2,1)S(1)}, bf16[4,2,48,768]{3,2,1,0:T(8,128)(2,1)S(1)}, u32[]{:S(2)}, u32[]{:S(2)}) %collective-permute-start.36) | collective-permute-done | bytes 589856 | tf_op jit(solution)/shard_map/ppermute | solution.py:773
  186.0 18.5 %attn_forward.3 = (f32[768,768]{1,0:T(8,128)}, f32[768,1]{1,0:T(8,128)}, bf16[3,768,768]{2,1,0:T(8,128)(2,1)}, bf16[24,384,384]{2,1,0:T(8,128)(2,1)}, bf16[768,768]{1,0:T(8,128)(2,1)}) custom-call(s32[8]{0:T(128)} %concatenate.121.idx, f32[768,768]{1,0:T(8,128)} %get-tuple-element.195.x_ref, f32[16,768]{1,0:T(8,128)} %get-tuple-element.436.vec_ref, ...), custom_call_target="tpu_custom_call" | custom-call | flops 4529848320 | bytes 31457280 | tf_op jit(solution)/shard_map/attn_forward/pallas_call | solution.py:180
  213.7 42.9 %ffn_both.1 = (f32[768,768]{1,0:T(8,128)}, f32[768,768]{1,0:T(8,128)}, f32[16,768]{1,0:T(8,128)}, bf16[768,768]{1,0:T(8,128)(2,1)}, bf16[32,2,2,48,768]{4,3,2,1,0:T(8,128)(2,1)}) custom-call(s32[8]{0:T(128)} %concatenate.121.idx, f32[768,768]{1,0:T(8,128)} %get-tuple-element.199.y1_ref, f32[768,1]{1,0:T(8,128)} %get-tuple-element.200.r1_ref, ...), custom_call_target="tpu_custom_call" | custom-call | flops 21743271936 | bytes 31457280 | tf_op jit(solution)/shard_map/ffn_both/pallas_call | solution.py:180
  256.7 16.7 %heads_backward.2 = (bf16[3,768,768]{2,1,0:T(8,128)(2,1)}, f32[8,768]{1,0:T(8,128)}) custom-call(s32[8]{0:T(128)} %concatenate.121.idx, bf16[768,768]{1,0:T(8,128)(2,1)} %get-tuple-element.208.da_ref, bf16[3,768,768]{2,1,0:T(8,128)(2,1)} %get-tuple-element.209.qkv_ref, bf16[24,384,384]{2,1,0:T(8,128)(2,1)} %get-tuple-element.210.p_ref), custom_call_target="tpu_custom_call" | custom-call | flops 6794772480 | bytes 31457280 | tf_op jit(solution)/shard_map/heads_backward/pallas_call | solution.py:180
  273.4 16.2 %inward_backward.2 = (f32[768,768]{1,0:T(8,128)}, bf16[2,16,1,48,768]{4,3,2,1,0:T(8,128)(2,1)}, bf16[2,16,1,48,768]{4,3,2,1,0:T(8,128)(2,1)}) custom-call(s32[8]{0:T(128)} %concatenate.121.idx, f32[768,768]{1,0:T(8,128)} %get-tuple-element.206.dh1_ref, f32[768,768]{1,0:T(8,128)} %get-tuple-element.195.x_ref, bf16[768,768]{1,0:T(8,128)(2,1)} %get-tuple-element.207.att_ref, ...), custom_call_target="tpu_custom_call" | custom-call | flops 6341787648 | bytes 31457280 | tf_op jit(solution)/shard_map/inward_backward/pallas_call | solution.py:180
  289.9 33.2 %ffn_backward.1 = (f32[768,768]{1,0:T(8,128)}, f32[16,768]{1,0:T(8,128)}, bf16[768,768]{1,0:T(8,128)(2,1)}, bf16[2,16,2,48,768]{4,3,2,1,0:T(8,128)(2,1)}, bf16[2,16,2,48,768]{4,3,2,1,0:T(8,128)(2,1)}) custom-call(s32[8]{0:T(128)} %concatenate.121.idx, f32[768,768]{1,0:T(8,128)} %get-tuple-element.212.g_ref, f32[768,768]{1,0:T(8,128)} %get-tuple-element.195.x_ref, ...), custom_call_target="tpu_custom_call" | custom-call | flops 14495514624 | bytes 31457280 | tf_op jit(solution)/shard_map/ffn_backward/pallas_call | solution.py:180
  328.3 16.6 %heads_backward.3 = (bf16[3,768,768]{2,1,0:T(8,128)(2,1)}, f32[8,768]{1,0:T(8,128)}) custom-call(s32[8]{0:T(128)} %concatenate.121.idx, bf16[768,768]{1,0:T(8,128)(2,1)} %get-tuple-element.223.da_ref, bf16[3,768,768]{2,1,0:T(8,128)(2,1)} %get-tuple-element.224.qkv_ref, bf16[24,384,384]{2,1,0:T(8,128)(2,1)} %get-tuple-element.225.p_ref), custom_call_target="tpu_custom_call" | custom-call | flops 6794772480 | bytes 31457280 | tf_op jit(solution)/shard_map/heads_backward/pallas_call | solution.py:180
  346.3 4.7 collective-permute-done.48
  350.9 4.5 fusion.1
  363.2 15.5 %inward_backward.3 = (f32[768,768]{1,0:T(8,128)}, bf16[2,16,1,48,768]{4,3,2,1,0:T(8,128)(2,1)}, bf16[2,16,1,48,768]{4,3,2,1,0:T(8,128)(2,1)}) custom-call(s32[8]{0:T(128)} %concatenate.121.idx, f32[768,768]{1,0:T(8,128)} %get-tuple-element.217.dh1_ref, bf16[768,768]{1,0:T(8,128)(2,1)} %bitcast.479, bf16[768,768]{1,0:T(8,128)(2,1)} %get-tuple-element.218.att_ref, ...), custom_call_target="tpu_custom_call" | custom-call | flops 6341787648 | bytes 31457280 | tf_op jit(solution)/shard_map/inward_backward/pallas_call | solution.py:180
  378.7 16.8 %collective-permute-done.52 = bf16[4,1,48,768]{3,2,1,0:T(8,128)(2,1)S(1)} collective-permute-done((bf16[4,1,48,768]{3,2,1,0:T(8,128)(2,1)}, bf16[4,1,48,768]{3,2,1,0:T(8,128)(2,1)S(1)}, u32[]{:S(2)}, u32[]{:S(2)}) %collective-permute-start.52) | collective-permute-done | bytes 294944 | tf_op jit(solution)/shard_map/ppermute | solution.py:773
  406.7 6.4 %collective-permute-done.56 = bf16[2,2,1,48,768]{4,3,1,2,0:T(8,128)(2,1)S(1)} collective-permute-done((bf16[2,2,1,48,768]{4,3,1,2,0:T(8,128)(2,1)S(1)}, bf16[2,2,1,48,768]{4,3,1,2,0:T(8,128)(2,1)S(1)}, u32[]{:S(2)}, u32[]{:S(2)}) %collective-permute-start.56) | collective-permute-done | bytes 294944 | tf_op jit(solution)/shard_map/ppermute | solution.py:773
  429.9 4.4 collective-permute-done.65
  (381 shorter events, 168.5 us)
Async XLA Ops:
  7.2 432.4 %reduce-scatter.2.cloned.1.call-start = ((), (), s32[]{:S(2)}) async-start(), calls=%async_computation.1 | async-start | bytes 9732096 | tf_op jit(solution)/shard_map/reduce_scatter | solution.py:1021
  22.6 19.2 %collective-permute-start.4 = (bf16[2,2,48,768]{3,2,1,0:T(8,128)(2,1)S(1)}, bf16[2,2,48,768]{3,2,1,0:T(8,128)(2,1)S(1)}, u32[]{:S(2)}, u32[]{:S(2)}) collective-permute-start(bf16[2,2,48,768]{3,2,1,0:T(8,128)(2,1)S(1)} %pad_maximum_fusion.21), channel_id=1, source_target_pairs={{0,24},{1,25},{2,26},{3,27},{4,28},{5,29},{6,30},{7,31},{8,16},{9,... | collective-permute-start | bytes 884744 | tf_op jit(solution)/shard_map/ppermute | solution.py:773
  84.8 29.4 %collective-permute-start.17 = (bf16[8,2,48,768]{3,2,1,0:T(8,128)(2,1)S(1)}, bf16[8,2,48,768]{3,2,1,0:T(8,128)(2,1)}, u32[]{:S(2)}, u32[]{:S(2)}) collective-permute-start(bf16[8,2,48,768]{3,2,1,0:T(8,128)(2,1)S(1)} %pad_maximum_fusion.1.refs_0_), channel_id=1, source_target_pairs={{0,2},{1,3},{2,0},{3,1},{4,6},{5,7},{6,4},{7,5},{8,10},{9,11},{10,... | collective-permute-start | bytes 3538952 | tf_op jit(solution)/shard_map/ppermute | solution.py:773
  86.1 28.5 %collective-permute-start.20 = (bf16[8,2,48,768]{3,2,1,0:T(8,128)(2,1)S(1)}, bf16[8,2,48,768]{3,2,1,0:T(8,128)(2,1)}, u32[]{:S(2)}, u32[]{:S(2)}) collective-permute-start(bf16[8,2,48,768]{3,2,1,0:T(8,128)(2,1)S(1)} %pad_maximum_fusion.1.refs_0_), channel_id=1, source_target_pairs={{0,1},{1,0},{2,3},{3,2},{4,5},{5,4},{6,7},{7,6},{8,9},{9,8},{10,11... | collective-permute-start | bytes 3538952 | tf_op jit(solution)/shard_map/ppermute | solution.py:773
  86.2 28.5 %collective-permute-start.18 = (bf16[8,2,48,768]{3,2,1,0:T(8,128)(2,1)S(1)}, bf16[8,2,48,768]{3,2,1,0:T(8,128)(2,1)}, u32[]{:S(2)}, u32[]{:S(2)}) collective-permute-start(bf16[8,2,48,768]{3,2,1,0:T(8,128)(2,1)S(1)} %pad_maximum_fusion.2.refs_4_), channel_id=1, source_target_pairs={{0,4},{1,5},{2,6},{3,7},{4,0},{5,1},{6,2},{7,3},{8,12},{9,13},{10,... | collective-permute-start | bytes 3538952 | tf_op jit(solution)/shard_map/ppermute | solution.py:773
  87.7 26.9 %collective-permute-start.21 = (bf16[8,2,48,768]{3,2,1,0:T(8,128)(2,1)S(1)}, bf16[8,2,48,768]{3,2,1,0:T(8,128)(2,1)}, u32[]{:S(2)}, u32[]{:S(2)}) collective-permute-start(bf16[8,2,48,768]{3,2,1,0:T(8,128)(2,1)S(1)} %pad_maximum_fusion.2.refs_4_), channel_id=1, source_target_pairs={{0,1},{1,0},{2,3},{3,2},{4,5},{5,4},{6,7},{7,6},{8,9},{9,8},{10,11... | collective-permute-start | bytes 3538952 | tf_op jit(solution)/shard_map/ppermute | solution.py:773
  92.8 18.3 %collective-permute-start.19 = (bf16[2,2,48,768]{3,2,1,0:T(8,128)(2,1)S(1)}, bf16[2,2,48,768]{3,2,1,0:T(8,128)(2,1)S(1)}, u32[]{:S(2)}, u32[]{:S(2)}) collective-permute-start(bf16[2,2,48,768]{3,2,1,0:T(8,128)(2,1)S(1)} %pad_maximum_fusion.23), channel_id=1, source_target_pairs={{0,8},{1,9},{2,10},{3,11},{4,12},{5,13},{6,14},{7,15},{8,0},{9,1},... | collective-permute-start | bytes 884744 | tf_op jit(solution)/shard_map/ppermute | solution.py:773
  115.5 26.7 %collective-permute-start.33 = (bf16[8,2,48,768]{3,2,1,0:T(8,128)(2,1)}, bf16[8,2,48,768]{3,2,1,0:T(8,128)(2,1)}, u32[]{:S(2)}, u32[]{:S(2)}) collective-permute-start(bf16[8,2,48,768]{3,2,1,0:T(8,128)(2,1)} %collective-permute-done.17.refs_1_), channel_id=1, source_target_pairs={{0,1},{1,0},{2,3},{3,2},{4,5},{5,4},{6,7},{7,6},{8,9},{9,8},{10,11... | collective-permute-start | bytes 3538952 | tf_op jit(solution)/shard_map/ppermute | solution.py:773
  115.5 26.7 %collective-permute-start.34 = (bf16[8,2,48,768]{3,2,1,0:T(8,128)(2,1)}, bf16[8,2,48,768]{3,2,1,0:T(8,128)(2,1)}, u32[]{:S(2)}, u32[]{:S(2)}) collective-permute-start(bf16[8,2,48,768]{3,2,1,0:T(8,128)(2,1)} %collective-permute-done.18.refs_5_), channel_id=1, source_target_pairs={{0,1},{1,0},{2,3},{3,2},{4,5},{5,4},{6,7},{7,6},{8,9},{9,8},{10,11... | collective-permute-start | bytes 3538952 | tf_op jit(solution)/shard_map/ppermute | solution.py:773
  129.1 33.6 %collective-permute-start.30 = (bf16[8,1,48,768]{3,2,1,0:T(8,128)(2,1)S(1)}, bf16[8,1,48,768]{3,2,1,0:T(8,128)(2,1)}, u32[]{:S(2)}, u32[]{:S(2)}) collective-permute-start(bf16[8,1,48,768]{3,2,1,0:T(8,128)(2,1)S(1)} %pad_maximum_fusion.11.refs_0_.refs_8_), channel_id=1, source_target_pairs={{0,2},{1,3},{2,0},{3,1},{4,6},{5,7},{6,4},{7,5},{8,10},{9,11},{10,... | collective-permute-start | bytes 1769480 | tf_op jit(solution)/shard_map/ppermute | solution.py:773
  129.8 32.9 %collective-permute-start.31 = (bf16[8,1,48,768]{3,2,1,0:T(8,128)(2,1)S(1)}, bf16[8,1,48,768]{3,2,1,0:T(8,128)(2,1)S(1)}, u32[]{:S(2)}, u32[]{:S(2)}) collective-permute-start(bf16[8,1,48,768]{3,2,1,0:T(8,128)(2,1)S(1)} %pad_maximum_fusion.12.refs_4_.refs_12_), channel_id=1, source_target_pairs={{0,4},{1,5},{2,6},{3,7},{4,0},{5,1},{6,2},{7,3},{8,12},{9,13},{10,... | collective-permute-start | bytes 1769480 | tf_op jit(solution)/shard_map/ppermute | solution.py:773
  178.3 26.1 %collective-permute-start.37 = (bf16[8,2,48,768]{3,2,1,0:T(8,128)(2,1)S(1)}, bf16[8,2,48,768]{3,2,1,0:T(8,128)(2,1)}, u32[]{:S(2)}, u32[]{:S(2)}) collective-permute-start(bf16[8,2,48,768]{3,2,1,0:T(8,128)(2,1)S(1)} %pad_maximum_fusion.4.refs_0_), channel_id=1, source_target_pairs={{0,2},{1,3},{2,0},{3,1},{4,6},{5,7},{6,4},{7,5},{8,10},{9,11},{10,... | collective-permute-start | bytes 3538952 | tf_op jit(solution)/shard_map/ppermute | solution.py:773
  179.7 28.4 %collective-permute-start.39 = (bf16[8,2,48,768]{3,2,1,0:T(8,128)(2,1)S(1)}, bf16[8,2,48,768]{3,2,1,0:T(8,128)(2,1)}, u32[]{:S(2)}, u32[]{:S(2)}) collective-permute-start(bf16[8,2,48,768]{3,2,1,0:T(8,128)(2,1)S(1)} %pad_maximum_fusion.4.refs_0_), channel_id=1, source_target_pairs={{0,1},{1,0},{2,3},{3,2},{4,5},{5,4},{6,7},{7,6},{8,9},{9,8},{10,11... | collective-permute-start | bytes 3538952 | tf_op jit(solution)/shard_map/ppermute | solution.py:773
  179.7 28.4 %collective-permute-start.38 = (bf16[8,2,48,768]{3,2,1,0:T(8,128)(2,1)S(1)}, bf16[8,2,48,768]{3,2,1,0:T(8,128)(2,1)S(1)}, u32[]{:S(2)}, u32[]{:S(2)}) collective-permute-start(bf16[8,2,48,768]{3,2,1,0:T(8,128)(2,1)S(1)} %pad_maximum_fusion.5.refs_4_), channel_id=1, source_target_pairs={{0,4},{1,5},{2,6},{3,7},{4,0},{5,1},{6,2},{7,3},{8,12},{9,13},{10,... | collective-permute-start | bytes 3538952 | tf_op jit(solution)/shard_map/ppermute | solution.py:773
  181.2 26.9 %collective-permute-start.40 = (bf16[8,2,48,768]{3,2,1,0:T(8,128)(2,1)S(1)}, bf16[8,2,48,768]{3,2,1,0:T(8,128)(2,1)}, u32[]{:S(2)}, u32[]{:S(2)}) collective-permute-start(bf16[8,2,48,768]{3,2,1,0:T(8,128)(2,1)S(1)} %pad_maximum_fusion.5.refs_4_), channel_id=1, source_target_pairs={{0,1},{1,0},{2,3},{3,2},{4,5},{5,4},{6,7},{7,6},{8,9},{9,8},{10,11... | collective-permute-start | bytes 3538952 | tf_op jit(solution)/shard_map/ppermute | solution.py:773
  289.7 33.4 %collective-permute-start.47 = (bf16[2,16,1,48,768]{4,3,2,1,0:T(8,128)(2,1)}, bf16[2,16,1,48,768]{4,3,2,1,0:T(8,128)(2,1)}, u32[]{:S(2)}, u32[]{:S(2)}) collective-permute-start(bf16[2,16,1,48,768]{4,3,2,1,0:T(8,128)(2,1)} %get-tuple-element.222), channel_id=1, source_target_pairs={{0,1},{1,0},{2,3},{3,2},{4,5},{5,4},{6,7},{7,6},{8,9},{9,8},{10,11... | collective-permute-start | bytes 7077896 | tf_op jit(solution)/shard_map/ppermute | solution.py:773
  323.1 27.8 %collective-permute-start.50 = (bf16[2,16,2,48,768]{4,3,2,1,0:T(8,128)(2,1)}, bf16[2,16,2,48,768]{4,3,2,1,0:T(8,128)(2,1)}, u32[]{:S(2)}, u32[]{:S(2)}) collective-permute-start(bf16[2,16,2,48,768]{4,3,2,1,0:T(8,128)(2,1)} %get-tuple-element.230), channel_id=1, source_target_pairs={{0,1},{1,0},{2,3},{3,2},{4,5},{5,4},{6,7},{7,6},{8,9},{9,8},{10,11... | collective-permute-start | bytes 14155784 | tf_op jit(solution)/shard_map/ppermute | solution.py:773
  324.8 21.4 %collective-permute-start.49 = (bf16[8,1,48,768]{3,2,1,0:T(8,128)(2,1)S(1)}, bf16[8,1,48,768]{3,2,1,0:T(8,128)(2,1)S(1)}, u32[]{:S(2)}, u32[]{:S(2)}) collective-permute-start(bf16[8,1,48,768]{3,2,1,0:T(8,128)(2,1)S(1)} %fusion.5), channel_id=1, source_target_pairs={{0,4},{1,5},{2,6},{3,7},{4,0},{5,1},{6,2},{7,3},{8,12},{9,13},{10,... | collective-permute-start | bytes 1769480 | tf_op jit(solution)/shard_map/ppermute | solution.py:773
  327.4 23.5 %collective-permute-start.48 = (bf16[8,1,48,768]{3,2,1,0:T(8,128)(2,1)S(1)}, bf16[8,1,48,768]{3,2,1,0:T(8,128)(2,1)}, u32[]{:S(2)}, u32[]{:S(2)}) collective-permute-start(bf16[8,1,48,768]{3,2,1,0:T(8,128)(2,1)S(1)} %fusion.4), channel_id=1, source_target_pairs={{0,2},{1,3},{2,0},{3,1},{4,6},{5,7},{6,4},{7,5},{8,10},{9,11},{10,... | collective-permute-start | bytes 1769480 | tf_op jit(solution)/shard_map/ppermute | solution.py:773
  355.4 40.1 %collective-permute-start.53 = (bf16[8,2,48,768]{3,2,1,0:T(8,128)(2,1)}, bf16[8,2,48,768]{3,2,1,0:T(8,128)(2,1)S(1)}, u32[]{:S(2)}, u32[]{:S(2)}) collective-permute-start(bf16[8,2,48,768]{3,2,1,0:T(8,128)(2,1)} %get-tuple-element.359), channel_id=1, source_target_pairs={{0,2},{1,3},{2,0},{3,1},{4,6},{5,7},{6,4},{7,5},{8,10},{9,11},{10,... | collective-permute-start | bytes 3538952 | tf_op jit(solution)/shard_map/ppermute | solution.py:773
  356.5 39.0 %collective-permute-start.54 = (bf16[8,2,48,768]{3,2,1,0:T(8,128)(2,1)}, bf16[8,2,48,768]{3,2,1,0:T(8,128)(2,1)}, u32[]{:S(2)}, u32[]{:S(2)}) collective-permute-start(bf16[8,2,48,768]{3,2,1,0:T(8,128)(2,1)} %get-tuple-element.358), channel_id=1, source_target_pairs={{0,4},{1,5},{2,6},{3,7},{4,0},{5,1},{6,2},{7,3},{8,12},{9,13},{10,... | collective-permute-start | bytes 3538952 | tf_op jit(solution)/shard_map/ppermute | solution.py:773
  358.4 37.1 %collective-permute-start.52 = (bf16[4,1,48,768]{3,2,1,0:T(8,128)(2,1)}, bf16[4,1,48,768]{3,2,1,0:T(8,128)(2,1)S(1)}, u32[]{:S(2)}, u32[]{:S(2)}) collective-permute-start(bf16[4,1,48,768]{3,2,1,0:T(8,128)(2,1)} %fusion.16), channel_id=1, source_target_pairs={{0,2},{1,3},{2,0},{3,1},{4,6},{5,7},{6,4},{7,5},{8,10},{9,11},{10,... | collective-permute-start | bytes 884744 | tf_op jit(solution)/shard_map/ppermute | solution.py:773
  361.4 34.1 %collective-permute-start.51 = (bf16[4,1,48,768]{3,2,1,0:T(8,128)(2,1)}, bf16[4,1,48,768]{3,2,1,0:T(8,128)(2,1)}, u32[]{:S(2)}, u32[]{:S(2)}) collective-permute-start(bf16[4,1,48,768]{3,2,1,0:T(8,128)(2,1)} %fusion.15), channel_id=1, source_target_pairs={{0,4},{1,5},{2,6},{3,7},{4,0},{5,1},{6,2},{7,3},{8,12},{9,13},{10,... | collective-permute-start | bytes 884744 | tf_op jit(solution)/shard_map/ppermute | solution.py:773
  395.5 26.9 %collective-permute-start.55 = (bf16[2,16,1,48,768]{4,3,2,1,0:T(8,128)(2,1)}, bf16[2,16,1,48,768]{4,3,2,1,0:T(8,128)(2,1)}, u32[]{:S(2)}, u32[]{:S(2)}) collective-permute-start(bf16[2,16,1,48,768]{4,3,2,1,0:T(8,128)(2,1)} %get-tuple-element.239), channel_id=1, source_target_pairs={{0,1},{1,0},{2,3},{3,2},{4,5},{5,4},{6,7},{7,6},{8,9},{9,8},{10,11... | collective-permute-start | bytes 7077896 | tf_op jit(solution)/shard_map/ppermute | solution.py:773
  (104 other events, 931.3 us)
Sparse Core Ops, SparseCore 0:
  256.8 152.0 reduce-scatter.1

commit v4 on v3

--- a/solution.py
+++ b/solution.py
@@ -974,16 +974,16 @@
         f_core += other_core(f_far)
         a1_near = near_up(halves(a1_col))
         f1_pair = pair_up(share)
-        y1, a1_near, f1_pair = tie((y1, a1_near, f1_pair))
+        y1, a1_near, f1_pair, f_core = tie((y1, a1_near, f1_pair, f_core))
         a1_far = far_up(a1_near)
         f1_col = column_up(f1_pair)
+        y1, f1_col = tie((y1, f1_col))
+        f1_near = near_up(halves2(f1_col))
         f_pieces = in_order(f_near, f_far, f_core[:2], f_core[2:])
         ffn = ffn_forward(idx, y1, vecs[0], f_pieces)
         x1 = keep_layer(x, y1, attn, ffn, a_pieces, f_pieces)
-        a1_far, f1_col, x1 = tie((a1_far, f1_col, x1))
+        a1_far, f1_near, x1 = tie((a1_far, f1_near, x1))
         a1_core = other_core(a1_near + a1_far)
-        f1_near = near_up(halves2(f1_col))
-        x1, f1_near = tie((x1, f1_near))
         f1_far = far_up(f1_near)
         f1_core = other_core(f1_near)
         a1_pieces = in_order(a1_near, a1_far, a1_core[:2], a1_core[2:])

time: 507 us -> 498 us (0.982)
  waiting for transfers between devices: 151 us -> 142 us
    ppermute x75, waiting for transfers between devices: 151 us -> 142 us  [swap(): return lax.ppermute(array, AXES, [(i, i ^ BITS[by]) for i in range(32)])]
  transfers between devices with their start and end apart: 76 -> 76, of which waited for: 33 -> 32; matrix products, arithmetic and copies ran while one was open for 9% -> 10% of each run, Pallas kernels for 31% -> 32%
where the time goes in v4:
time: 498 us; the launch traced here: 491 us
  Pallas kernels  199 us (40%)
  waiting for transfers between devices  142 us (29%)
  starting transfers between devices  67.2 us (13%)
  other arithmetic  47.4 us (10%)
  local copies, waits for them, and re-layouts  20 us (4%)
  between operations  15.7 us (3%)
    pallas_call x9, Pallas kernels, call(): pl.pallas_call(kernel, in_specs=[SMEM] + [ANY] * (len(operands) - 1), out...  199 us
    ppermute x75, waiting for transfers between devices, swap(): return lax.ppermute(array, AXES, [(i, i ^ BITS[by]) for i in range(32)])  142 us
    ppermute x75, starting transfers between devices, swap(): return lax.ppermute(array, AXES, [(i, i ^ BITS[by]) for i in range(32)])  67.1 us
    convert_element_type x8, other arithmetic, plane(): self.total(s, lo, 2 * lo).astype(BF16)  18.3 us
    another operation x14, other arithmetic, line(): jnp.stack([self.total(s, lo, 2 * lo) for s in range(2)]).astype(BF16)  11.3 us
  transfers between devices with their start and end apart: 76, of which 32 were waited for; matrix products, arithmetic and copies ran while one was open for 10% of the time, Pallas kernels for 32%

profile of v4, /device:TPU:0, one launch (start us, length us, event | category | flops | bytes accessed | tf_op | source)
XLA Modules:
  0.0 491.0 jit_solution(4054292967714057354)
XLA Ops:
  13.2 4.7 collective-permute-start.2
  18.1 4.5 collective-permute-done.2
  28.2 13.5 %collective-permute-done.6 = f32[2,16,768]{2,1,0:T(8,128)S(1)} collective-permute-done((f32[2,16,768]{2,1,0:T(8,128)S(1)}, f32[2,16,768]{2,1,0:T(8,128)S(1)}, u32[]{:S(2)}, u32[]{:S(2)}) %collective-permute-start.6) | collective-permute-done | bytes 98336 | tf_op jit(solution)/shard_map/ppermute | solution.py:773
  47.2 4.0 collective-permute-done.10
  54.1 7.5 %collective-permute-done.7 = bf16[2,2,2,48,768]{4,3,2,1,0:T(8,128)(2,1)S(1)} collective-permute-done((bf16[2,2,2,48,768]{4,3,2,1,0:T(8,128)(2,1)S(1)}, bf16[2,2,2,48,768]{4,3,2,1,0:T(8,128)(2,1)S(1)}, u32[]{:S(2)}, u32[]{:S(2)}) %collective-permute-start.7) | collective-permute-done | bytes 589856 | tf_op jit(solution)/shard_map/ppermute | solution.py:773
  61.8 4.5 collective-permute-done.11.refs_1_.refs_9_
  70.7 12.2 %collective-permute-done.16 = f32[2,16,768]{2,1,0:T(8,128)S(1)} collective-permute-done((f32[2,16,768]{2,1,0:T(8,128)S(1)}, f32[2,16,768]{2,1,0:T(8,128)S(1)}, u32[]{:S(2)}, u32[]{:S(2)}) %collective-permute-start.16) | collective-permute-done | bytes 98336 | tf_op jit(solution)/shard_map/ppermute | solution.py:773
  92.8 18.2 %attn_forward.2 = (f32[768,768]{1,0:T(8,128)}, f32[768,1]{1,0:T(8,128)}, bf16[3,768,768]{2,1,0:T(8,128)(2,1)}, bf16[24,384,384]{2,1,0:T(8,128)(2,1)}, bf16[768,768]{1,0:T(8,128)(2,1)}) custom-call(s32[8]{0:T(128)} %concatenate.121.idx, bf16[768,768]{1,0:T(8,128)(2,1)} %bitcast.478, f32[16,768]{1,0:T(8,128)} %get-tuple-element.445.vec_ref, ...), custom_call_target="tpu_custom_call" | custom-call | flops 4529848320 | bytes 31457280 | tf_op jit(solution)/shard_map/attn_forward/pallas_call | solution.py:180
  117.6 8.4 %collective-permute-done.29 = bf16[2,2,48,768]{3,2,1,0:T(8,128)(2,1)S(1)} collective-permute-done((bf16[2,2,48,768]{3,2,1,0:T(8,128)(2,1)S(1)}, bf16[2,2,48,768]{3,2,1,0:T(8,128)(2,1)S(1)}, u32[]{:S(2)}, u32[]{:S(2)}) %collective-permute-start.29) | collective-permute-done | bytes 294944 | tf_op jit(solution)/shard_map/ppermute | solution.py:773
  132.0 10.6 %collective-permute-done.34 = bf16[2,2,2,48,768]{4,3,2,1,0:T(8,128)(2,1)S(1)} collective-permute-done((bf16[2,2,2,48,768]{4,3,2,1,0:T(8,128)(2,1)S(1)}, bf16[2,2,2,48,768]{4,3,2,1,0:T(8,128)(2,1)S(1)}, u32[]{:S(2)}, u32[]{:S(2)}) %collective-permute-start.34) | collective-permute-done | bytes 589856 | tf_op jit(solution)/shard_map/ppermute | solution.py:773
  145.2 20.5 %ffn_forward.1 = (f32[768,768]{1,0:T(8,128)}, f32[768,1]{1,0:T(8,128)}, bf16[4,768,768]{2,1,0:T(8,128)(2,1)}, bf16[4,768,768]{2,1,0:T(8,128)(2,1)}) custom-call(s32[8]{0:T(128)} %concatenate.121.idx, f32[768,768]{1,0:T(8,128)} %get-tuple-element.195.y1_ref, f32[16,768]{1,0:T(8,128)} %get-tuple-element.445.vec_ref, bf16[8,2,48,768]{3,2,1,0:T(8,128)(2,1)} %copy-done.4, ...), custom_call_target="tpu_custom_call" | custom-call | flops 7247757312 | bytes 31457280 | tf_op jit(solution)/shard_map/ffn_forward/pallas_call | solution.py:180
  175.8 18.5 %attn_forward.3 = (f32[768,768]{1,0:T(8,128)}, f32[768,1]{1,0:T(8,128)}, bf16[3,768,768]{2,1,0:T(8,128)(2,1)}, bf16[24,384,384]{2,1,0:T(8,128)(2,1)}, bf16[768,768]{1,0:T(8,128)(2,1)}) custom-call(s32[8]{0:T(128)} %concatenate.121.idx, f32[768,768]{1,0:T(8,128)} %get-tuple-element.203.x_ref, f32[16,768]{1,0:T(8,128)} %get-tuple-element.444.vec_ref, ...), custom_call_target="tpu_custom_call" | custom-call | flops 4529848320 | bytes 31457280 | tf_op jit(solution)/shard_map/attn_forward/pallas_call | solution.py:180
  203.7 43.0 %ffn_both.1 = (f32[768,768]{1,0:T(8,128)}, f32[768,768]{1,0:T(8,128)}, f32[16,768]{1,0:T(8,128)}, bf16[768,768]{1,0:T(8,128)(2,1)}, bf16[32,2,2,48,768]{4,3,2,1,0:T(8,128)(2,1)}) custom-call(s32[8]{0:T(128)} %concatenate.121.idx, f32[768,768]{1,0:T(8,128)} %get-tuple-element.207.y1_ref, f32[768,1]{1,0:T(8,128)} %get-tuple-element.208.r1_ref, ...), custom_call_target="tpu_custom_call" | custom-call | flops 21743271936 | bytes 31457280 | tf_op jit(solution)/shard_map/ffn_both/pallas_call | solution.py:180
  246.7 16.8 %heads_backward.2 = (bf16[3,768,768]{2,1,0:T(8,128)(2,1)}, f32[8,768]{1,0:T(8,128)}) custom-call(s32[8]{0:T(128)} %concatenate.121.idx, bf16[768,768]{1,0:T(8,128)(2,1)} %get-tuple-element.216.da_ref, bf16[3,768,768]{2,1,0:T(8,128)(2,1)} %get-tuple-element.217.qkv_ref, bf16[24,384,384]{2,1,0:T(8,128)(2,1)} %get-tuple-element.218.p_ref), custom_call_target="tpu_custom_call" | custom-call | flops 6794772480 | bytes 31457280 | tf_op jit(solution)/shard_map/heads_backward/pallas_call | solution.py:180
  263.5 16.3 %inward_backward.2 = (f32[768,768]{1,0:T(8,128)}, bf16[2,16,1,48,768]{4,3,2,1,0:T(8,128)(2,1)}, bf16[2,16,1,48,768]{4,3,2,1,0:T(8,128)(2,1)}) custom-call(s32[8]{0:T(128)} %concatenate.121.idx, f32[768,768]{1,0:T(8,128)} %get-tuple-element.214.dh1_ref, f32[768,768]{1,0:T(8,128)} %get-tuple-element.203.x_ref, bf16[768,768]{1,0:T(8,128)(2,1)} %get-tuple-element.215.att_ref, ...), custom_call_target="tpu_custom_call" | custom-call | flops 6341787648 | bytes 31457280 | tf_op jit(solution)/shard_map/inward_backward/pallas_call | solution.py:180
  279.9 33.2 %ffn_backward.1 = (f32[768,768]{1,0:T(8,128)}, f32[16,768]{1,0:T(8,128)}, bf16[768,768]{1,0:T(8,128)(2,1)}, bf16[2,16,2,48,768]{4,3,2,1,0:T(8,128)(2,1)}, bf16[2,16,2,48,768]{4,3,2,1,0:T(8,128)(2,1)}) custom-call(s32[8]{0:T(128)} %concatenate.121.idx, f32[768,768]{1,0:T(8,128)} %get-tuple-element.220.g_ref, f32[768,768]{1,0:T(8,128)} %get-tuple-element.203.x_ref, ...), custom_call_target="tpu_custom_call" | custom-call | flops 14495514624 | bytes 31457280 | tf_op jit(solution)/shard_map/ffn_backward/pallas_call | solution.py:180
  317.4 16.6 %heads_backward.3 = (bf16[3,768,768]{2,1,0:T(8,128)(2,1)}, f32[8,768]{1,0:T(8,128)}) custom-call(s32[8]{0:T(128)} %concatenate.121.idx, bf16[768,768]{1,0:T(8,128)(2,1)} %get-tuple-element.231.da_ref, bf16[3,768,768]{2,1,0:T(8,128)(2,1)} %get-tuple-element.232.qkv_ref, bf16[24,384,384]{2,1,0:T(8,128)(2,1)} %get-tuple-element.233.p_ref), custom_call_target="tpu_custom_call" | custom-call | flops 6794772480 | bytes 31457280 | tf_op jit(solution)/shard_map/heads_backward/pallas_call | solution.py:180
  340.1 4.5 fusion.1
  352.4 15.5 %inward_backward.3 = (f32[768,768]{1,0:T(8,128)}, bf16[2,16,1,48,768]{4,3,2,1,0:T(8,128)(2,1)}, bf16[2,16,1,48,768]{4,3,2,1,0:T(8,128)(2,1)}) custom-call(s32[8]{0:T(128)} %concatenate.121.idx, f32[768,768]{1,0:T(8,128)} %get-tuple-element.225.dh1_ref, bf16[768,768]{1,0:T(8,128)(2,1)} %bitcast.479, bf16[768,768]{1,0:T(8,128)(2,1)} %get-tuple-element.226.att_ref, ...), custom_call_target="tpu_custom_call" | custom-call | flops 6341787648 | bytes 31457280 | tf_op jit(solution)/shard_map/inward_backward/pallas_call | solution.py:180
  367.9 17.0 %collective-permute-done.52 = bf16[4,1,48,768]{3,2,1,0:T(8,128)(2,1)S(1)} collective-permute-done((bf16[4,1,48,768]{3,2,1,0:T(8,128)(2,1)}, bf16[4,1,48,768]{3,2,1,0:T(8,128)(2,1)S(1)}, u32[]{:S(2)}, u32[]{:S(2)}) %collective-permute-start.52) | collective-permute-done | bytes 294944 | tf_op jit(solution)/shard_map/ppermute | solution.py:773
  397.9 5.7 %collective-permute-done.56 = bf16[2,2,1,48,768]{4,3,1,2,0:T(8,128)(2,1)S(1)} collective-permute-done((bf16[2,2,1,48,768]{4,3,1,2,0:T(8,128)(2,1)S(1)}, bf16[2,2,1,48,768]{4,3,1,2,0:T(8,128)(2,1)S(1)}, u32[]{:S(2)}, u32[]{:S(2)}) %collective-permute-start.56) | collective-permute-done | bytes 294944 | tf_op jit(solution)/shard_map/ppermute | solution.py:773
  423.9 5.4 %collective-permute-done.72 = bf16[2,1,1,48,768]{4,3,2,1,0:T(8,128)(2,1)S(1)} collective-permute-done((bf16[2,1,1,48,768]{4,3,2,1,0:T(8,128)(2,1)S(1)}, bf16[2,1,1,48,768]{4,3,2,1,0:T(8,128)(2,1)S(1)}, u32[]{:S(2)}, u32[]{:S(2)}) %collective-permute-start.72) | collective-permute-done | bytes 147488 | tf_op jit(solution)/shard_map/ppermute | solution.py:773
  440.1 3.9 collective-permute-done.62
  453.6 4.9 collective-permute-done.68
  (379 shorter events, 165.4 us)
Async XLA Ops:
  7.2 424.0 %reduce-scatter.2.cloned.1.call-start = ((), (), s32[]{:S(2)}) async-start(), calls=%async_computation.1 | async-start | bytes 9732096 | tf_op jit(solution)/shard_map/reduce_scatter | solution.py:1021
  22.6 19.2 %collective-permute-start.4 = (bf16[2,2,48,768]{3,2,1,0:T(8,128)(2,1)S(1)}, bf16[2,2,48,768]{3,2,1,0:T(8,128)(2,1)S(1)}, u32[]{:S(2)}, u32[]{:S(2)}) collective-permute-start(bf16[2,2,48,768]{3,2,1,0:T(8,128)(2,1)S(1)} %pad_maximum_fusion.21), channel_id=1, source_target_pairs={{0,24},{1,25},{2,26},{3,27},{4,28},{5,29},{6,30},{7,31},{8,16},{9,... | collective-permute-start | bytes 884744 | tf_op jit(solution)/shard_map/ppermute | solution.py:773
  84.8 29.4 %collective-permute-start.17 = (bf16[8,2,48,768]{3,2,1,0:T(8,128)(2,1)S(1)}, bf16[8,2,48,768]{3,2,1,0:T(8,128)(2,1)}, u32[]{:S(2)}, u32[]{:S(2)}) collective-permute-start(bf16[8,2,48,768]{3,2,1,0:T(8,128)(2,1)S(1)} %pad_maximum_fusion.1.refs_0_), channel_id=1, source_target_pairs={{0,2},{1,3},{2,0},{3,1},{4,6},{5,7},{6,4},{7,5},{8,10},{9,11},{10,... | collective-permute-start | bytes 3538952 | tf_op jit(solution)/shard_map/ppermute | solution.py:773
  86.1 28.5 %collective-permute-start.20 = (bf16[8,2,48,768]{3,2,1,0:T(8,128)(2,1)S(1)}, bf16[8,2,48,768]{3,2,1,0:T(8,128)(2,1)}, u32[]{:S(2)}, u32[]{:S(2)}) collective-permute-start(bf16[8,2,48,768]{3,2,1,0:T(8,128)(2,1)S(1)} %pad_maximum_fusion.1.refs_0_), channel_id=1, source_target_pairs={{0,1},{1,0},{2,3},{3,2},{4,5},{5,4},{6,7},{7,6},{8,9},{9,8},{10,11... | collective-permute-start | bytes 3538952 | tf_op jit(solution)/shard_map/ppermute | solution.py:773
  86.2 28.5 %collective-permute-start.18 = (bf16[8,2,48,768]{3,2,1,0:T(8,128)(2,1)S(1)}, bf16[8,2,48,768]{3,2,1,0:T(8,128)(2,1)}, u32[]{:S(2)}, u32[]{:S(2)}) collective-permute-start(bf16[8,2,48,768]{3,2,1,0:T(8,128)(2,1)S(1)} %pad_maximum_fusion.2.refs_4_), channel_id=1, source_target_pairs={{0,4},{1,5},{2,6},{3,7},{4,0},{5,1},{6,2},{7,3},{8,12},{9,13},{10,... | collective-permute-start | bytes 3538952 | tf_op jit(solution)/shard_map/ppermute | solution.py:773
  87.7 26.9 %collective-permute-start.21 = (bf16[8,2,48,768]{3,2,1,0:T(8,128)(2,1)S(1)}, bf16[8,2,48,768]{3,2,1,0:T(8,128)(2,1)}, u32[]{:S(2)}, u32[]{:S(2)}) collective-permute-start(bf16[8,2,48,768]{3,2,1,0:T(8,128)(2,1)S(1)} %pad_maximum_fusion.2.refs_4_), channel_id=1, source_target_pairs={{0,1},{1,0},{2,3},{3,2},{4,5},{5,4},{6,7},{7,6},{8,9},{9,8},{10,11... | collective-permute-start | bytes 3538952 | tf_op jit(solution)/shard_map/ppermute | solution.py:773
  129.6 38.0 %collective-permute-start.32 = (bf16[8,1,48,768]{3,2,1,0:T(8,128)(2,1)S(1)}, bf16[8,1,48,768]{3,2,1,0:T(8,128)(2,1)}, u32[]{:S(2)}, u32[]{:S(2)}) collective-permute-start(bf16[8,1,48,768]{3,2,1,0:T(8,128)(2,1)S(1)} %pad_maximum_fusion.11.refs_0_.refs_8_), channel_id=1, source_target_pairs={{0,2},{1,3},{2,0},{3,1},{4,6},{5,7},{6,4},{7,5},{8,10},{9,11},{10,... | collective-permute-start | bytes 1769480 | tf_op jit(solution)/shard_map/ppermute | solution.py:773
  130.4 39.0 %collective-permute-start.41 = (bf16[8,1,48,768]{3,2,1,0:T(8,128)(2,1)S(1)}, bf16[8,1,48,768]{3,2,1,0:T(8,128)(2,1)}, u32[]{:S(2)}, u32[]{:S(2)}) collective-permute-start(bf16[8,1,48,768]{3,2,1,0:T(8,128)(2,1)S(1)} %pad_maximum_fusion.11.refs_0_.refs_8_), channel_id=1, source_target_pairs={{0,1},{1,0},{2,3},{3,2},{4,5},{5,4},{6,7},{7,6},{8,9},{9,8},{10,11... | collective-permute-start | bytes 1769480 | tf_op jit(solution)/shard_map/ppermute | solution.py:773
  130.4 37.2 %collective-permute-start.33 = (bf16[8,1,48,768]{3,2,1,0:T(8,128)(2,1)S(1)}, bf16[8,1,48,768]{3,2,1,0:T(8,128)(2,1)}, u32[]{:S(2)}, u32[]{:S(2)}) collective-permute-start(bf16[8,1,48,768]{3,2,1,0:T(8,128)(2,1)S(1)} %pad_maximum_fusion.12.refs_4_.refs_12_), channel_id=1, source_target_pairs={{0,4},{1,5},{2,6},{3,7},{4,0},{5,1},{6,2},{7,3},{8,12},{9,13},{10,... | collective-permute-start | bytes 1769480 | tf_op jit(solution)/shard_map/ppermute | solution.py:773
  142.8 22.9 %collective-permute-start.36 = (bf16[4,2,48,768]{3,2,1,0:T(8,128)(2,1)S(1)}, bf16[4,2,48,768]{3,2,1,0:T(8,128)(2,1)S(1)}, u32[]{:S(2)}, u32[]{:S(2)}) collective-permute-start(bf16[4,2,48,768]{3,2,1,0:T(8,128)(2,1)S(1)} %get-tuple-element.380), channel_id=1, source_target_pairs={{0,2},{1,3},{2,0},{3,1},{4,6},{5,7},{6,4},{7,5},{8,10},{9,11},{10,... | collective-permute-start | bytes 1769480 | tf_op jit(solution)/shard_map/ppermute | solution.py:773
  143.6 22.4 %collective-permute-start.35 = (bf16[4,2,48,768]{3,2,1,0:T(8,128)(2,1)S(1)}, bf16[4,2,48,768]{3,2,1,0:T(8,128)(2,1)}, u32[]{:S(2)}, u32[]{:S(2)}) collective-permute-start(bf16[4,2,48,768]{3,2,1,0:T(8,128)(2,1)S(1)} %get-tuple-element.381), channel_id=1, source_target_pairs={{0,4},{1,5},{2,6},{3,7},{4,0},{5,1},{6,2},{7,3},{8,12},{9,13},{10,... | collective-permute-start | bytes 1769480 | tf_op jit(solution)/shard_map/ppermute | solution.py:773
  168.2 28.1 %collective-permute-start.37 = (bf16[8,2,48,768]{3,2,1,0:T(8,128)(2,1)S(1)}, bf16[8,2,48,768]{3,2,1,0:T(8,128)(2,1)}, u32[]{:S(2)}, u32[]{:S(2)}) collective-permute-start(bf16[8,2,48,768]{3,2,1,0:T(8,128)(2,1)S(1)} %pad_maximum_fusion.4.refs_0_), channel_id=1, source_target_pairs={{0,2},{1,3},{2,0},{3,1},{4,6},{5,7},{6,4},{7,5},{8,10},{9,11},{10,... | collective-permute-start | bytes 3538952 | tf_op jit(solution)/shard_map/ppermute | solution.py:773
  169.3 28.5 %collective-permute-start.39 = (bf16[8,2,48,768]{3,2,1,0:T(8,128)(2,1)S(1)}, bf16[8,2,48,768]{3,2,1,0:T(8,128)(2,1)}, u32[]{:S(2)}, u32[]{:S(2)}) collective-permute-start(bf16[8,2,48,768]{3,2,1,0:T(8,128)(2,1)S(1)} %pad_maximum_fusion.4.refs_0_), channel_id=1, source_target_pairs={{0,1},{1,0},{2,3},{3,2},{4,5},{5,4},{6,7},{7,6},{8,9},{9,8},{10,11... | collective-permute-start | bytes 3538952 | tf_op jit(solution)/shard_map/ppermute | solution.py:773
  169.3 28.5 %collective-permute-start.38 = (bf16[8,2,48,768]{3,2,1,0:T(8,128)(2,1)S(1)}, bf16[8,2,48,768]{3,2,1,0:T(8,128)(2,1)}, u32[]{:S(2)}, u32[]{:S(2)}) collective-permute-start(bf16[8,2,48,768]{3,2,1,0:T(8,128)(2,1)S(1)} %pad_maximum_fusion.5.refs_4_), channel_id=1, source_target_pairs={{0,4},{1,5},{2,6},{3,7},{4,0},{5,1},{6,2},{7,3},{8,12},{9,13},{10,... | collective-permute-start | bytes 3538952 | tf_op jit(solution)/shard_map/ppermute | solution.py:773
  169.9 27.9 %collective-permute-start.40 = (bf16[8,2,48,768]{3,2,1,0:T(8,128)(2,1)S(1)}, bf16[8,2,48,768]{3,2,1,0:T(8,128)(2,1)S(1)}, u32[]{:S(2)}, u32[]{:S(2)}) collective-permute-start(bf16[8,2,48,768]{3,2,1,0:T(8,128)(2,1)S(1)} %pad_maximum_fusion.5.refs_4_), channel_id=1, source_target_pairs={{0,1},{1,0},{2,3},{3,2},{4,5},{5,4},{6,7},{7,6},{8,9},{9,8},{10,11... | collective-permute-start | bytes 3538952 | tf_op jit(solution)/shard_map/ppermute | solution.py:773
  279.8 33.3 %collective-permute-start.47 = (bf16[2,16,1,48,768]{4,3,2,1,0:T(8,128)(2,1)}, bf16[2,16,1,48,768]{4,3,2,1,0:T(8,128)(2,1)}, u32[]{:S(2)}, u32[]{:S(2)}) collective-permute-start(bf16[2,16,1,48,768]{4,3,2,1,0:T(8,128)(2,1)} %get-tuple-element.230), channel_id=1, source_target_pairs={{0,1},{1,0},{2,3},{3,2},{4,5},{5,4},{6,7},{7,6},{8,9},{9,8},{10,11... | collective-permute-start | bytes 7077896 | tf_op jit(solution)/shard_map/ppermute | solution.py:773
  313.1 27.0 %collective-permute-start.50 = (bf16[2,16,2,48,768]{4,3,2,1,0:T(8,128)(2,1)}, bf16[2,16,2,48,768]{4,3,2,1,0:T(8,128)(2,1)}, u32[]{:S(2)}, u32[]{:S(2)}) collective-permute-start(bf16[2,16,2,48,768]{4,3,2,1,0:T(8,128)(2,1)} %get-tuple-element.238), channel_id=1, source_target_pairs={{0,1},{1,0},{2,3},{3,2},{4,5},{5,4},{6,7},{7,6},{8,9},{9,8},{10,11... | collective-permute-start | bytes 14155784 | tf_op jit(solution)/shard_map/ppermute | solution.py:773
  314.9 22.4 %collective-permute-start.49 = (bf16[8,1,48,768]{3,2,1,0:T(8,128)(2,1)S(1)}, bf16[8,1,48,768]{3,2,1,0:T(8,128)(2,1)S(1)}, u32[]{:S(2)}, u32[]{:S(2)}) collective-permute-start(bf16[8,1,48,768]{3,2,1,0:T(8,128)(2,1)S(1)} %fusion.5), channel_id=1, source_target_pairs={{0,4},{1,5},{2,6},{3,7},{4,0},{5,1},{6,2},{7,3},{8,12},{9,13},{10,... | collective-permute-start | bytes 1769480 | tf_op jit(solution)/shard_map/ppermute | solution.py:773
  316.5 23.6 %collective-permute-start.48 = (bf16[8,1,48,768]{3,2,1,0:T(8,128)(2,1)S(1)}, bf16[8,1,48,768]{3,2,1,0:T(8,128)(2,1)}, u32[]{:S(2)}, u32[]{:S(2)}) collective-permute-start(bf16[8,1,48,768]{3,2,1,0:T(8,128)(2,1)S(1)} %fusion.4), channel_id=1, source_target_pairs={{0,2},{1,3},{2,0},{3,1},{4,6},{5,7},{6,4},{7,5},{8,10},{9,11},{10,... | collective-permute-start | bytes 1769480 | tf_op jit(solution)/shard_map/ppermute | solution.py:773
  344.6 40.3 %collective-permute-start.53 = (bf16[8,2,48,768]{3,2,1,0:T(8,128)(2,1)}, bf16[8,2,48,768]{3,2,1,0:T(8,128)(2,1)S(1)}, u32[]{:S(2)}, u32[]{:S(2)}) collective-permute-start(bf16[8,2,48,768]{3,2,1,0:T(8,128)(2,1)} %get-tuple-element.367), channel_id=1, source_target_pairs={{0,2},{1,3},{2,0},{3,1},{4,6},{5,7},{6,4},{7,5},{8,10},{9,11},{10,... | collective-permute-start | bytes 3538952 | tf_op jit(solution)/shard_map/ppermute | solution.py:773
  345.5 39.4 %collective-permute-start.54 = (bf16[8,2,48,768]{3,2,1,0:T(8,128)(2,1)}, bf16[8,2,48,768]{3,2,1,0:T(8,128)(2,1)}, u32[]{:S(2)}, u32[]{:S(2)}) collective-permute-start(bf16[8,2,48,768]{3,2,1,0:T(8,128)(2,1)} %get-tuple-element.366), channel_id=1, source_target_pairs={{0,4},{1,5},{2,6},{3,7},{4,0},{5,1},{6,2},{7,3},{8,12},{9,13},{10,... | collective-permute-start | bytes 3538952 | tf_op jit(solution)/shard_map/ppermute | solution.py:773
  349.0 35.8 %collective-permute-start.52 = (bf16[4,1,48,768]{3,2,1,0:T(8,128)(2,1)}, bf16[4,1,48,768]{3,2,1,0:T(8,128)(2,1)S(1)}, u32[]{:S(2)}, u32[]{:S(2)}) collective-permute-start(bf16[4,1,48,768]{3,2,1,0:T(8,128)(2,1)} %fusion.16), channel_id=1, source_target_pairs={{0,2},{1,3},{2,0},{3,1},{4,6},{5,7},{6,4},{7,5},{8,10},{9,11},{10,... | collective-permute-start | bytes 884744 | tf_op jit(solution)/shard_map/ppermute | solution.py:773
  352.0 32.9 %collective-permute-start.51 = (bf16[4,1,48,768]{3,2,1,0:T(8,128)(2,1)}, bf16[4,1,48,768]{3,2,1,0:T(8,128)(2,1)}, u32[]{:S(2)}, u32[]{:S(2)}) collective-permute-start(bf16[4,1,48,768]{3,2,1,0:T(8,128)(2,1)} %fusion.15), channel_id=1, source_target_pairs={{0,4},{1,5},{2,6},{3,7},{4,0},{5,1},{6,2},{7,3},{8,12},{9,13},{10,... | collective-permute-start | bytes 884744 | tf_op jit(solution)/shard_map/ppermute | solution.py:773
  384.9 27.5 %collective-permute-start.55 = (bf16[2,16,1,48,768]{4,3,2,1,0:T(8,128)(2,1)}, bf16[2,16,1,48,768]{4,3,2,1,0:T(8,128)(2,1)}, u32[]{:S(2)}, u32[]{:S(2)}) collective-permute-start(bf16[2,16,1,48,768]{4,3,2,1,0:T(8,128)(2,1)} %get-tuple-element.247), channel_id=1, source_target_pairs={{0,1},{1,0},{2,3},{3,2},{4,5},{5,4},{6,7},{7,6},{8,9},{9,8},{10,11... | collective-permute-start | bytes 7077896 | tf_op jit(solution)/shard_map/ppermute | solution.py:773
  (103 other events, 910.0 us)
Sparse Core Ops, SparseCore 0:
  246.8 152.1 reduce-scatter.1
